TPU v7x, 32 devices: a whole 2x2x4 slice. The times are simulated.
32 devices in a mesh: ctx: 16 (over z, y, core), head: 2 (over x).
Axes of the slice: x: 2, y: 2, z: 4, core: 2. Of those that a mesh axis runs over, the one named last changes fastest.
Arguments:
- queries: bfloat16 [8192, 512], P('ctx', 'head'), may hold values from -256 to 256
- rotated_key_rows: bfloat16 [8192, 256], P('ctx', 'head'), may hold values from -8 to 8
- value_head_rows: bfloat16 [8192, 256], P('ctx', 'head'), may hold values from -24 to 24
- stride_offset: int32 [4], P('head'), may hold values from 0 to 7
- w_out: bfloat16 [512, 4096], P('head'), may hold values from -0.25 to 0.25
- grad_out: bfloat16 [8192, 4096], P('ctx', 'head'), may hold values from -6 to 6
Outputs:
- layer_out: bfloat16 [8192, 4096], P('ctx', 'head')
- grad_queries: bfloat16 [8192, 512], P('ctx', 'head')
- key_gradient: bfloat16 [8192, 256], P('ctx', 'head')
- value_gradient: bfloat16 [8192, 256], P('ctx', 'head')
- grad_w_out: bfloat16 [512, 4096], P('head', 'ctx')
All inputs are finite; a program needn't handle non-finite values.
Results may differ from a plain program's by a relative error of at most 0.033.
Values may be sent and summed in bfloat16 or wider, within the bound.
No kernel may reach another device: no remote copies, remote signals or barrier semaphores. Data moves between devices by JAX's collectives and lax.ppermute only.
A program may use at most 128 MiB of HBM per device.

v0:
```python
import math

import jax
import jax.numpy as jnp
from jax import lax
from jax.sharding import PartitionSpec as P

HEAD_SIZE = 128
BLOCK_TOKENS = 64
LOCAL = 16
STRIDE = 8


def shifted(block, axis, distance):
    devices = range(lax.axis_size(axis))
    route = [(i - distance, i) for i in devices if i - distance in devices]
    return lax.ppermute(block, axis, route)


def contract_rows(form, left, right):
    return jnp.einsum(form, left, right, preferred_element_type=jnp.float32)


def exact_map(form, left, right):
    return jnp.einsum(form, left, right, precision=lax.Precision.HIGHEST)


def band_allowed(shard_id, tok_rows, phase_list):
    tokens_q = shard_id * tok_rows + jnp.arange(tok_rows, dtype=jnp.int32)
    tokens_k = (shard_id - 2) * tok_rows + jnp.arange(3 * tok_rows, dtype=jnp.int32)
    block_q = tokens_q // BLOCK_TOKENS
    block_k = tokens_k // BLOCK_TOKENS
    causal = (tokens_k[None, :] >= 0) & (tokens_k[None, :] <= tokens_q[:, None])
    nearby = block_q[:, None] - block_k[None, :] < LOCAL
    on_stride = (block_k[None, None, :] + phase_list[:, :, None]) % STRIDE == STRIDE - 1
    return causal[None, None] & (nearby[None, None] | on_stride[:, :, None, :])


def keep_state(running):
    return running


def body(queries, rotated_key_rows, value_head_rows, stride_offset, w_out, grad_out):
    tok_rows = queries.shape[0]
    groups = rotated_key_rows.shape[1] // HEAD_SIZE
    per_group = queries.shape[1] // (groups * HEAD_SIZE)
    shards = lax.axis_size("ctx")
    shard_id = lax.axis_index("ctx")
    scaling = HEAD_SIZE ** (-0.5)
    picked_rows = tok_rows // STRIDE
    picked_count = picked_rows * shards
    tile_rows = BLOCK_TOKENS * math.gcd(picked_count // BLOCK_TOKENS, max(1, 512 // BLOCK_TOKENS))
    tile_count = picked_count // tile_rows
    bound_rows = (shard_id - 2) * picked_rows
    q_heads = queries.reshape(tok_rows, groups, per_group, HEAD_SIZE)
    phase_list = stride_offset.reshape(groups, per_group)
    offsets = jnp.arange(STRIDE, dtype=jnp.int32)
    select_mask = offsets[None, None, :] == (STRIDE - 1 - phase_list)[:, :, None]
    head_ids = jnp.arange(per_group, dtype=jnp.int32)
    same_phase = phase_list[:, :, None] == phase_list[:, None, :]
    earlier = jnp.any(same_phase & (head_ids[None, None, :] < head_ids[None, :, None]), axis=2)
    leading = jnp.logical_not(earlier)

    def pick_rows(source):
        grouped = source.reshape(-1, STRIDE, BLOCK_TOKENS, groups, HEAD_SIZE)
        chosen = contract_rows("grs,nsbgd->grnbd", select_mask.astype(jnp.bfloat16), grouped)
        return chosen.astype(jnp.bfloat16)

    behind = []
    for distance in (2, 1):
        behind.append(shifted((rotated_key_rows, value_head_rows), "ctx", distance))
    near_k = jnp.concatenate([behind[0][0], behind[1][0], rotated_key_rows], axis=0)
    near_v = jnp.concatenate([behind[0][1], behind[1][1], value_head_rows], axis=0)
    picked_k, picked_v = (
        lax.all_gather(pick_rows(rotated_key_rows), "ctx", axis=2, tiled=True),
        lax.all_gather(pick_rows(value_head_rows), "ctx", axis=2, tiled=True),
    )
    near_k = near_k.reshape(3 * tok_rows, groups, HEAD_SIZE)
    near_v = near_v.reshape(3 * tok_rows, groups, HEAD_SIZE)
    picked_k = picked_k.reshape(groups, per_group, picked_count, HEAD_SIZE)
    picked_v = picked_v.reshape(groups, per_group, picked_count, HEAD_SIZE)
    allowed = band_allowed(shard_id, tok_rows, phase_list)
    scores = jnp.where(
        allowed, contract_rows("tgrd,ugd->grtu", q_heads, near_k) * scaling, -jnp.inf
    )
    row_max = jnp.max(scores, axis=-1)
    weights = jnp.where(allowed, jnp.exp(scores - row_max[..., None]), 0.0)
    row_sum = jnp.sum(weights, axis=-1)
    weighted = contract_rows("grtu,ugd->grtd", weights.astype(jnp.bfloat16), near_v)

    def forward_tile(tile_index, running):
        tile_start = tile_index * tile_rows

        def forward_update(running):
            row_max, row_sum, weighted = running
            tile_k = lax.dynamic_slice_in_dim(picked_k, tile_start, tile_rows, 2)
            tile_v = lax.dynamic_slice_in_dim(picked_v, tile_start, tile_rows, 2)
            usable = tile_start + jnp.arange(tile_rows, dtype=jnp.int32) < bound_rows
            scores = jnp.where(
                usable, contract_rows("tgrd,grkd->grtk", q_heads, tile_k) * scaling, -jnp.inf
            )
            new_max = jnp.maximum(row_max, jnp.max(scores, axis=-1))
            weights = jnp.where(usable, jnp.exp(scores - new_max[..., None]), 0.0)
            factor = jnp.exp(row_max - new_max)
            row_sum = row_sum * factor + jnp.sum(weights, axis=-1)
            weighted = weighted * factor[..., None] + contract_rows(
                "grtk,grkd->grtd", weights.astype(jnp.bfloat16), tile_v
            )
            return (new_max, row_sum, weighted)

        return lax.cond(tile_start < bound_rows, forward_update, keep_state, running)

    row_max, row_sum, weighted = lax.fori_loop(
        0, tile_count, forward_tile, (row_max, row_sum, weighted)
    )
    attended_rows = jnp.transpose(weighted / row_sum[..., None], (2, 0, 1, 3)).astype(jnp.bfloat16)
    log_total = row_max + jnp.log(row_sum)
    flat_out = attended_rows.reshape(tok_rows, -1)
    head_part = jnp.dot(flat_out, w_out, preferred_element_type=jnp.float32)
    layer_out = lax.psum_scatter(
        head_part.astype(jnp.bfloat16), "head", scatter_dimension=1, tiled=True
    )
    full_grad = lax.all_gather(grad_out, "head", axis=1, tiled=True)
    grad_flat = contract_rows("te,he->th", full_grad, w_out).astype(jnp.bfloat16)
    weight_term = contract_rows("th,te->he", flat_out, full_grad)
    grad_w_out = lax.psum_scatter(
        weight_term.astype(jnp.bfloat16), "ctx", scatter_dimension=1, tiled=True
    )
    do_heads = grad_flat.reshape(tok_rows, groups, per_group, HEAD_SIZE)
    row_dot = jnp.transpose(
        jnp.sum(do_heads.astype(jnp.float32) * attended_rows.astype(jnp.float32), axis=-1),
        (1, 2, 0),
    )
    scores = contract_rows("tgrd,ugd->grtu", q_heads, near_k) * scaling
    weights = jnp.where(allowed, jnp.exp(scores - log_total[..., None]), 0.0)
    grad_near_v = contract_rows("grtu,tgrd->ugd", weights.astype(jnp.bfloat16), do_heads)
    grad_weights = contract_rows("tgrd,ugd->grtu", do_heads, near_v)
    grad_scores = (weights * (grad_weights - row_dot[..., None])).astype(jnp.bfloat16)
    grad_q = contract_rows("grtu,ugd->tgrd", grad_scores, near_k) * scaling
    grad_near_k = contract_rows("grtu,tgrd->ugd", grad_scores, q_heads) * scaling

    def backward_tile(tile_index, inner):
        tile_start = tile_index * tile_rows

        def backward_update(inner):
            grad_q, grad_pk, grad_pv = inner
            tile_k = lax.dynamic_slice_in_dim(picked_k, tile_start, tile_rows, 2)
            tile_v = lax.dynamic_slice_in_dim(picked_v, tile_start, tile_rows, 2)
            usable = tile_start + jnp.arange(tile_rows, dtype=jnp.int32) < bound_rows
            scores = contract_rows("tgrd,grkd->grtk", q_heads, tile_k) * scaling
            weights = jnp.where(usable, jnp.exp(scores - log_total[..., None]), 0.0)
            tile_gv = contract_rows("grtk,tgrd->grkd", weights.astype(jnp.bfloat16), do_heads)
            grad_weights = contract_rows("tgrd,grkd->grtk", do_heads, tile_v)
            grad_scores = (weights * (grad_weights - row_dot[..., None])).astype(jnp.bfloat16)
            grad_q = grad_q + contract_rows("grtk,grkd->tgrd", grad_scores, tile_k) * scaling
            tile_gk = contract_rows("grtk,tgrd->grkd", grad_scores, q_heads) * scaling
            grad_pk = lax.dynamic_update_slice_in_dim(grad_pk, tile_gk, tile_start, 2)
            grad_pv = lax.dynamic_update_slice_in_dim(grad_pv, tile_gv, tile_start, 2)
            return (grad_q, grad_pk, grad_pv)

        return lax.cond(tile_start < bound_rows, backward_update, keep_state, inner)

    empty_state = jnp.zeros((groups, per_group, picked_count, HEAD_SIZE), jnp.float32)
    grad_q, grad_pk, grad_pv = lax.fori_loop(
        0, tile_count, backward_tile, (grad_q, empty_state, empty_state)
    )
    grad_queries = grad_q.astype(jnp.bfloat16).reshape(tok_rows, -1)
    phase_match = same_phase.astype(jnp.float32)
    merged_k = exact_map("grq,gqnd->grnd", phase_match, grad_pk)
    merged_v = exact_map("grq,gqnd->grnd", phase_match, grad_pv)
    stride_k, stride_v = (
        lax.psum_scatter(
            merged_k.astype(jnp.bfloat16), "ctx", scatter_dimension=2, tiled=True
        ).astype(jnp.float32),
        lax.psum_scatter(
            merged_v.astype(jnp.bfloat16), "ctx", scatter_dimension=2, tiled=True
        ).astype(jnp.float32),
    )
    owner_map = (select_mask & leading[:, :, None]).astype(jnp.float32)
    own_k = exact_map(
        "xij,xiucz->ujcxz",
        owner_map,
        stride_k.reshape(groups, per_group, -1, BLOCK_TOKENS, HEAD_SIZE),
    ).reshape(tok_rows, groups, HEAD_SIZE)
    own_v = exact_map(
        "xij,xiucz->ujcxz",
        owner_map,
        stride_v.reshape(groups, per_group, -1, BLOCK_TOKENS, HEAD_SIZE),
    ).reshape(tok_rows, groups, HEAD_SIZE)
    own_k = own_k + lax.optimization_barrier(
        grad_near_k[2 * tok_rows :].astype(jnp.bfloat16)
    ).astype(jnp.float32)
    own_v = own_v + lax.optimization_barrier(
        grad_near_v[2 * tok_rows :].astype(jnp.bfloat16)
    ).astype(jnp.float32)
    for distance in (1, 2):
        row_start = (2 - distance) * tok_rows
        part_k = grad_near_k[row_start : row_start + tok_rows].astype(jnp.bfloat16)
        part_v = grad_near_v[row_start : row_start + tok_rows].astype(jnp.bfloat16)
        got_k, got_v = shifted((part_k, part_v), "ctx", -distance)
        own_k = own_k + got_k.astype(jnp.float32)
        own_v = own_v + got_v.astype(jnp.float32)
    key_gradient = own_k.astype(jnp.bfloat16).reshape(tok_rows, groups * HEAD_SIZE)
    value_gradient = own_v.astype(jnp.bfloat16).reshape(tok_rows, groups * HEAD_SIZE)
    return (layer_out, grad_queries, key_gradient, value_gradient, grad_w_out)


def solution(mesh):
    placed = (
        P("ctx", "head"),
        P("ctx", "head"),
        P("ctx", "head"),
        P("head"),
        P("head", None),
        P("ctx", "head"),
    )
    return jax.shard_map(
        body,
        mesh=mesh,
        in_specs=placed,
        out_specs=(
            P("ctx", "head"),
            P("ctx", "head"),
            P("ctx", "head"),
            P("ctx", "head"),
            P("head", "ctx"),
        ),
        check_vma=False,
    )
```

profile of v0, /device:TPU:0, one launch (start us, length us, event | category | flops | bytes accessed | tf_op | source)
XLA Modules:
  0.0 361.4 jit_solution(14844034912126552506)
XLA Ops:
  7.2 0.0 all-gather.4.cloned.1.call-start
  7.3 5.7 %collective-permute-start = (bf16[512,128]{1,0:T(8,128)(2,1)}, bf16[512,128]{1,0:T(8,128)(2,1)}, u32[]{:S(2)}, u32[]{:S(2)}) collective-permute-start(bf16[512,128]{1,0:T(8,128)(2,1)} %param.15), channel_id=1, source_target_pairs={{0,4},{2,6},{4,8},{6,10},{8,12},{10,14},{12,16},{14,18},{16,20},{1... | collective-permute-start | bytes 393224 | tf_op jit(solution)/shard_map/ppermute | solution.py:17
  12.9 2.1 collective-permute-start.1
  15.0 3.2 collective-permute-start.2
  18.3 3.9 %collective-permute-start.3 = (bf16[512,128]{1,0:T(8,128)(2,1)}, bf16[512,128]{1,0:T(8,128)(2,1)}, u32[]{:S(2)}, u32[]{:S(2)}) collective-permute-start(bf16[512,128]{1,0:T(8,128)(2,1)} %param.16), channel_id=1, source_target_pairs={{0,2},{2,4},{4,6},{6,8},{8,10},{10,12},{12,14},{14,16},{16,18},{18... | collective-permute-start | bytes 393224 | tf_op jit(solution)/shard_map/ppermute | solution.py:17
  22.2 0.0 all-gather.4.cloned.1.call-update
  22.2 0.0 reduce-scatter.17.cloned.1.call-start
  22.3 0.2 convolution_convert_fusion.6
  22.6 18.8 %all-gather = bf16[2,1024,128]{2,0,1:T(2,128)(2,1)S(1)} all-gather(bf16[2,64,128]{2,0,1:T(2,128)(2,1)S(1)} %convolution_convert_fusion.6), channel_id=2, replica_groups=mesh['ctx'=16,'head'=2] {'ctx'}, dimensions={1}, use_global_device_ids=true | all-gather | bytes 557056 | tf_op jit(solution)/shard_map/all_gather | solution.py:75
  41.4 0.1 copy.93
  41.4 0.2 convolution_convert_fusion.5
  41.7 0.1 fusion.91
  41.8 1.5 subtract_compare_fusion
  43.2 1.8 compare_and_fusion
  45.1 20.4 %all-gather.1 = bf16[2,1024,128]{2,0,1:T(2,128)(2,1)S(1)} all-gather(bf16[2,64,128]{2,0,1:T(2,128)(2,1)S(1)} %convolution_convert_fusion.5), channel_id=3, replica_groups=mesh['ctx'=16,'head'=2] {'ctx'}, dimensions={1}, use_global_device_ids=true | all-gather | bytes 557056 | tf_op jit(solution)/shard_map/all_gather | solution.py:76
  65.5 0.1 copy.95
  65.6 0.8 copy.91
  66.4 1.1 copy.94
  67.6 3.8 %fusion.46 = (f32[2,512]{1,0:T(2,128)S(1)}, f32[1536,512,2]{1,0,2:T(8,128)S(1)}) fusion(pred[2,1536]{1,0:T(4,128)(4,1)S(1)} %fusion.91, pred[512,1536]{0,1:T(8,128)(4,1)} %subtract_compare_fusion, pred[512,1536]{0,1:T(8,128)(4,1)} %compare_and_fusion, bf16[512,128]{1,0:T(8,128)(2,1)S(1)} %copy-done.19, bf16[512,128]{1,0:T(8,128)(2,1)} %collective-permute-done.1, ...), kind=kOutput, calls=%fused_computation.66 | convolution fusion | flops 411696128 | bytes 8526848 | tf_op jit(solution)/shard_map/tgrd,ugd->grtu/dot_general | solution.py:21
  71.4 2.7 fusion.58
  74.2 4.7 %fusion.72 = f32[1,2,512,128]{3,2,1,0:T(8,128)} fusion(f32[2,512]{1,0:T(2,128)S(1)} %get-tuple-element.571, f32[1536,512,2]{1,0,2:T(8,128)S(1)} %get-tuple-element.572, pred[2,1536]{1,0:T(4,128)(4,1)S(1)} %fusion.91, pred[512,1536]{0,1:T(8,128)(4,1)S(1)} %copy-done.6, pred[512,1536]{0,1:T(8,128)(4,1)S(1)} %copy-done.7, bf16[512,128]{1,0:T(8,128)(2,1)S(1)} %copy-done.26, ...), kind=kOutput, calls=%fused_computation.91 | convolution fusion | flops 414842880 | bytes 8788992 | tf_op jit(solution)/shard_map/grtu,ugd->grtd/dot_general | solution.py:21
  78.9 2.4 copy.96
  81.3 0.6 log_add_fusion
  81.9 4.2 %convolution_convert_fusion.4 = bf16[512,256]{0,1:T(8,128)(2,1)} fusion(bf16[512,4096]{1,0:T(8,128)(2,1)} %all-gather.4.cloned.1.call-done, bf16[256,4096]{1,0:T(8,128)(2,1)S(1)} %copy-done), kind=kOutput, calls=%fused_computation.92 | convolution fusion | flops 1073872896 | bytes 6553600 | tf_op jit(solution)/shard_map/te,he->th/dot_general | solution.py:21
  86.1 1.1 copy.103
  87.2 1.2 multiply_reduce_fusion
  88.4 5.4 %fusion.48 = bf16[2,512,1536]{1,2,0:T(8,128)(2,1)S(1)} fusion(bf16[512,2,128]{0,2,1:T(8,128)(2,1)} %bitcast.316, f32[1536,512,2]{1,0,2:T(8,128)} %copy-done.5, f32[2,512]{1,0:T(2,128)S(1)} %bitcast.323, f32[2,512]{1,0:T(2,128)} %bitcast.328, pred[2,1536]{1,0:T(4,128)(4,1)S(1)} %fusion.91, pred[512,1536]{0,1:T(8,128)(4,1)} %subtract_compare_fusion, ...), kind=kOutput, calls=%fused_computation.68 | convolution fusion | flops 416415744 | bytes 11676672 | tf_op jit(solution)/shard_map/tgrd,ugd->grtu/dot_general | solution.py:21
  93.9 1.9 fusion.71
  95.8 1.0 broadcast_in_dim.55
  96.9 1.0 broadcast_in_dim.55.clone
  97.9 0.6 copy-done.24
  98.6 3.8 %convolution_convert_fusion.2 = bf16[2,1024,128]{2,0,1:T(2,128)(2,1)S(1)} fusion(f32[2,1024,128]{2,1,0:T(8,128)} %bitcast.309, s32[2]{0:T(128)S(1)} %copy-done.24), kind=kOutput, calls=%fused_computation.87 | convolution fusion | flops 6553604 | bytes 1572872 | tf_op jit(solution)/shard_map/grq,gqnd->grnd/dot_general | solution.py:25
  102.4 0.9 copy.149
  103.3 0.0 reduce-scatter.15.cloned.1.call-start
  103.3 3.8 %convolution_convert_fusion.3 = bf16[2,1024,128]{2,0,1:T(2,128)(2,1)S(1)} fusion(f32[2,1024,128]{2,1,0:T(8,128)} %bitcast.308, s32[2]{0:T(128)S(1)} %copy-done.24), kind=kOutput, calls=%fused_computation.88 | convolution fusion | flops 6553604 | bytes 1572872 | tf_op jit(solution)/shard_map/grq,gqnd->grnd/dot_general | solution.py:25
  107.2 0.9 copy.150
  108.1 0.0 reduce-scatter.13.cloned.1.call-start
  108.2 4.8 %convolution_convert_fusion.1 = bf16[256,4096]{1,0:T(8,128)(2,1)} fusion(bf16[512,256]{0,1:T(8,128)(2,1)S(1)} %bitcast.310, bf16[512,4096]{1,0:T(8,128)(2,1)} %all-gather.4.cloned.1.call-done), kind=kOutput, calls=%fused_computation.65 | convolution fusion | flops 1074790400 | bytes 6553600 | tf_op jit(solution)/shard_map/th,te->he/dot_general | solution.py:21
  113.0 0.0 reduce-scatter.11.cloned.1.call-start
  113.0 3.4 convolution_convert_fusion
  116.4 0.2 and_reduce_fusion
  116.6 0.7 copy-done.14
  117.3 4.7 %fusion.68 = bf16[1536,1,128]{0,2,1:T(8,128)(2,1)S(1)} fusion(bf16[512,2,128]{0,2,1:T(8,128)(2,1)S(1)} %bitcast.317, f32[1536,512,2]{1,0,2:T(8,128)} %copy-done.5, f32[2,512]{1,0:T(2,128)S(1)} %bitcast.330, pred[2,1536]{1,0:T(4,128)(4,1)S(1)} %fusion.91, pred[512,1536]{0,1:T(8,128)(4,1)} %subtract_compare_fusion, pred[512,1536]{0,1:T(8,128)(4,1)} %compare_and_fusion), kind=kOutput, calls=%fused_computation.86 | convolution fusion | flops 412286976 | bytes 8526848 | tf_op jit(solution)/shard_map/grtu,tgrd->ugd/dot_general | solution.py:21
  122.0 0.7 fusion.126
  122.8 1.3 collective-permute-start.6
  124.1 1.3 collective-permute-start.7
  125.4 1.0 fusion.67
  126.4 1.3 collective-permute-start.4
  127.7 1.3 collective-permute-start.5
  129.1 0.8 copy.121
  129.9 45.1 %reduce-scatter.17.cloned.1.call-done = bf16[64,256]{1,0:T(8,128)(2,1)} async-done(((bf16[1024,256]{1,0:T(8,128)(2,1)}), bf16[64,256]{1,0:T(8,128)(2,1)}) %reduce-scatter.17.cloned.1.call-update) | async-done | bytes 32784
  175.0 0.8 reshape.728
  175.8 0.3 convolution_bitcast_fusion.3
  176.1 0.1 copy.109
  176.2 0.1 copy.111
  176.3 1.0 fusion.85
  177.3 0.8 copy.112
  178.1 55.7 %reduce-scatter.15.cloned.1.call-done = bf16[64,256]{1,0:T(8,128)(2,1)} async-done(((bf16[1024,256]{1,0:T(8,128)(2,1)}), bf16[64,256]{1,0:T(8,128)(2,1)}) %reduce-scatter.15.cloned.1.call-update) | async-done | bytes 32784
  233.9 0.8 reshape.726
  234.6 0.3 convolution_bitcast_fusion.4
  234.9 0.1 copy.106
  235.0 1.6 fusion.82
  236.7 62.0 %reduce-scatter.13.cloned.1.call-done = bf16[256,256]{1,0:T(8,128)(2,1)} async-done(((bf16[256,4096]{1,0:T(8,128)(2,1)}), bf16[256,256]{1,0:T(8,128)(2,1)}) %reduce-scatter.13.cloned.1.call-update) | async-done | bytes 131088 | tf_op jit(solution)/shard_map/reduce_scatter | solution.py:126
  298.7 56.2 %reduce-scatter.11.cloned.1.call-done = bf16[512,2048]{1,0:T(8,128)(2,1)} async-done(((bf16[512,4096]{1,0:T(8,128)(2,1)}), bf16[512,2048]{1,0:T(8,128)(2,1)}) %reduce-scatter.11.cloned.1.call-update) | async-done | bytes 2097168 | tf_op jit(solution)/shard_map/reduce_scatter | solution.py:120
  (62 shorter events, 0.3 us)
Async XLA Ops:
  7.2 74.7 %copy-start = (bf16[256,4096]{1,0:T(8,128)(2,1)S(1)}, bf16[256,4096]{1,0:T(8,128)(2,1)}, u32[]{:S(2)}) copy-start(bf16[256,4096]{1,0:T(8,128)(2,1)} %param.18) | copy-start | bytes 6291460
  7.2 15.2 %copy-start.19 = (bf16[512,128]{1,0:T(8,128)(2,1)S(1)}, bf16[512,128]{1,0:T(8,128)(2,1)}, u32[]{:S(2)}) copy-start(bf16[512,128]{1,0:T(8,128)(2,1)} %param.15) | copy-start | bytes 393220
  7.2 34.2 %copy-start.25 = (bf16[512,128]{1,0:T(8,128)(2,1)S(1)}, bf16[512,128]{1,0:T(8,128)(2,1)}, u32[]{:S(2)}) copy-start(bf16[512,128]{1,0:T(8,128)(2,1)} %param.16) | copy-start | bytes 393220
  7.2 15.1 %copy-start.23 = (s32[2]{0:T(128)S(1)}, s32[2]{0:T(128)}, u32[]{:S(2)}) copy-start(s32[2]{0:T(128)} %param.17) | copy-start | bytes 28
  7.2 74.7 %all-gather.4.cloned.1.call-start = ((), (), s32[]{:S(2)}) async-start(), calls=%async_computation.5 | async-start | bytes 6291456 | tf_op jit(solution)/shard_map/all_gather | solution.py:123
  7.3 60.3 %collective-permute-start = (bf16[512,128]{1,0:T(8,128)(2,1)}, bf16[512,128]{1,0:T(8,128)(2,1)}, u32[]{:S(2)}, u32[]{:S(2)}) collective-permute-start(bf16[512,128]{1,0:T(8,128)(2,1)} %param.15), channel_id=1, source_target_pairs={{0,4},{2,6},{4,8},{6,10},{8,12},{10,14},{12,16},{14,18},{16,20},{1... | collective-permute-start | bytes 393224 | tf_op jit(solution)/shard_map/ppermute | solution.py:17
  12.9 54.6 %collective-permute-start.1 = (bf16[512,128]{1,0:T(8,128)(2,1)}, bf16[512,128]{1,0:T(8,128)(2,1)}, u32[]{:S(2)}, u32[]{:S(2)}) collective-permute-start(bf16[512,128]{1,0:T(8,128)(2,1)} %param.15), channel_id=1, source_target_pairs={{0,2},{2,4},{4,6},{6,8},{8,10},{10,12},{12,14},{14,16},{16,18},{18... | collective-permute-start | bytes 393224 | tf_op jit(solution)/shard_map/ppermute | solution.py:17
  15.0 59.1 %collective-permute-start.2 = (bf16[512,128]{1,0:T(8,128)(2,1)}, bf16[512,128]{1,0:T(8,128)(2,1)}, u32[]{:S(2)}, u32[]{:S(2)}) collective-permute-start(bf16[512,128]{1,0:T(8,128)(2,1)} %param.16), channel_id=1, source_target_pairs={{0,4},{2,6},{4,8},{6,10},{8,12},{10,14},{12,16},{14,18},{16,20},{1... | collective-permute-start | bytes 393224 | tf_op jit(solution)/shard_map/ppermute | solution.py:17
  18.3 55.9 %collective-permute-start.3 = (bf16[512,128]{1,0:T(8,128)(2,1)}, bf16[512,128]{1,0:T(8,128)(2,1)}, u32[]{:S(2)}, u32[]{:S(2)}) collective-permute-start(bf16[512,128]{1,0:T(8,128)(2,1)} %param.16), channel_id=1, source_target_pairs={{0,2},{2,4},{4,6},{6,8},{8,10},{10,12},{12,14},{14,16},{16,18},{18... | collective-permute-start | bytes 393224 | tf_op jit(solution)/shard_map/ppermute | solution.py:17
  22.2 152.8 %reduce-scatter.17.cloned.1.call-start = ((), (), s32[]{:S(2)}) async-start(), calls=%async_computation.8 | async-start | bytes 557056
  22.3 43.1 %copy-start.21 = (s32[2]{0:T(128)}, s32[2]{0:T(128)S(1)}, u32[]{:S(2)}) copy-start(s32[2]{0:T(128)S(1)} %broadcast_subtract_fusion) | copy-start | bytes 28
  41.4 24.2 %copy-start.17 = (bf16[512,256]{1,0:T(8,128)(2,1)S(1)}, bf16[512,256]{1,0:T(8,128)(2,1)}, u32[]{:S(2)}) copy-start(bf16[512,256]{1,0:T(8,128)(2,1)} %param.14) | copy-start | bytes 786436
  67.5 3.8 %copy-start.6 = (pred[512,1536]{0,1:T(8,128)(4,1)S(1)}, pred[512,1536]{0,1:T(8,128)(4,1)}, u32[]{:S(2)}) copy-start(pred[512,1536]{0,1:T(8,128)(4,1)} %subtract_compare_fusion) | copy-start | bytes 2359300
  67.5 3.8 %copy-start.7 = (pred[512,1536]{0,1:T(8,128)(4,1)S(1)}, pred[512,1536]{0,1:T(8,128)(4,1)}, u32[]{:S(2)}) copy-start(pred[512,1536]{0,1:T(8,128)(4,1)} %compare_and_fusion) | copy-start | bytes 2359300
  71.3 2.8 copy-start.5
  71.4 2.8 copy-start.26
  78.9 7.2 %copy-start.1 = (bf16[1,2,1024,128]{3,2,1,0:T(8,128)(2,1)}, bf16[1,2,1024,128]{3,2,1,0:T(8,128)(2,1)S(1)}, u32[]{:S(2)}) copy-start(bf16[1,2,1024,128]{3,2,1,0:T(8,128)(2,1)S(1)} %get-tuple-element.795) | copy-start | bytes 1572868
  78.9 7.2 %copy-start.3 = (bf16[1,2,1024,128]{3,2,1,0:T(8,128)(2,1)}, bf16[1,2,1024,128]{3,2,1,0:T(8,128)(2,1)S(1)}, u32[]{:S(2)}) copy-start(bf16[1,2,1024,128]{3,2,1,0:T(8,128)(2,1)S(1)} %get-tuple-element.798) | copy-start | bytes 1572868
  93.9 3.0 copy-start.8
  93.9 4.0 %copy-start.20 = (f32[1,2,512]{2,1,0:T(2,128)S(1)}, f32[1,2,512]{2,1,0:T(2,128)}, u32[]{:S(2)}) copy-start(f32[1,2,512]{2,1,0:T(2,128)} %log_add_fusion) | copy-start | bytes 12292
  97.9 0.7 copy-start.24
  103.3 130.6 %reduce-scatter.15.cloned.1.call-start = ((), (), s32[]{:S(2)}) async-start(), calls=%async_computation.7 | async-start | bytes 557056
  108.1 190.6 %reduce-scatter.13.cloned.1.call-start = ((), (), s32[]{:S(2)}) async-start(), calls=%async_computation.6 | async-start | bytes 2228224 | tf_op jit(solution)/shard_map/reduce_scatter | solution.py:126
  113.0 241.9 %reduce-scatter.11.cloned.1.call-start = ((), (), s32[]{:S(2)}) async-start(), calls=%async_computation.4 | async-start | bytes 6291456 | tf_op jit(solution)/shard_map/reduce_scatter | solution.py:120
  116.4 0.9 copy-start.14
  117.3 8.1 %copy-start.9 = (bf16[2,512,1536]{1,2,0:T(8,128)(2,1)S(1)}, bf16[2,512,1536]{1,2,0:T(8,128)(2,1)}, u32[]{:S(2)}) copy-start(bf16[2,512,1536]{1,2,0:T(8,128)(2,1)} %copy-done.8) | copy-start | bytes 9437188
  117.3 8.1 %copy-start.18 = (bf16[512,256]{1,0:T(8,128)(2,1)S(1)}, bf16[512,256]{1,0:T(8,128)(2,1)}, u32[]{:S(2)}) copy-start(bf16[512,256]{1,0:T(8,128)(2,1)} %param.14) | copy-start | bytes 786436
  122.8 53.5 %collective-permute-start.6 = (bf16[512,1,128]{0,2,1:T(8,128)(2,1)}, bf16[512,1,128]{0,2,1:T(8,128)(2,1)}, u32[]{:S(2)}, u32[]{:S(2)}) collective-permute-start(bf16[512,1,128]{0,2,1:T(8,128)(2,1)} %get-tuple-element.567), channel_id=1, source_target_pairs={{2,0},{4,2},{6,4},{8,6},{10,8},{12,10},{14,12},{16,14},{18,16},{20... | collective-permute-start | bytes 393224 | tf_op jit(solution)/shard_map/ppermute | solution.py:17
  124.1 52.2 %collective-permute-start.7 = (bf16[512,1,128]{0,2,1:T(8,128)(2,1)}, bf16[512,1,128]{0,2,1:T(8,128)(2,1)}, u32[]{:S(2)}, u32[]{:S(2)}) collective-permute-start(bf16[512,1,128]{0,2,1:T(8,128)(2,1)} %get-tuple-element.566), channel_id=1, source_target_pairs={{4,0},{6,2},{8,4},{10,6},{12,8},{14,10},{16,12},{18,14},{20,16},{2... | collective-permute-start | bytes 393224 | tf_op jit(solution)/shard_map/ppermute | solution.py:17
  126.4 49.4 %copy-start.22 = (s32[2]{0:T(128)S(1)}, s32[2]{0:T(128)}, u32[]{:S(2)}) copy-start(s32[2]{0:T(128)} %copy-done.21) | copy-start | bytes 28
  126.4 108.6 %collective-permute-start.4 = (bf16[512,1,128]{2,0,1:T(8,128)(2,1)S(1)}, bf16[512,1,128]{2,0,1:T(8,128)(2,1)S(1)}, u32[]{:S(2)}, u32[]{:S(2)}) collective-permute-start(bf16[512,1,128]{2,0,1:T(8,128)(2,1)S(1)} %get-tuple-element.570), channel_id=1, source_target_pairs={{2,0},{4,2},{6,4},{8,6},{10,8},{12,10},{14,12},{16,14},{18,16},{20... | collective-permute-start | bytes 393224 | tf_op jit(solution)/shard_map/ppermute | solution.py:17
  127.7 107.3 %collective-permute-start.5 = (bf16[512,1,128]{2,0,1:T(8,128)(2,1)S(1)}, bf16[512,1,128]{2,0,1:T(8,128)(2,1)}, u32[]{:S(2)}, u32[]{:S(2)}) collective-permute-start(bf16[512,1,128]{2,0,1:T(8,128)(2,1)S(1)} %get-tuple-element.569), channel_id=1, source_target_pairs={{4,0},{6,2},{8,4},{10,6},{12,8},{14,10},{16,12},{18,14},{20,16},{2... | collective-permute-start | bytes 393224 | tf_op jit(solution)/shard_map/ppermute | solution.py:17
Sparse Core Ops, SparseCore 0:
  22.3 54.7 all-gather.3
  103.4 71.5 reduce-scatter.16
  179.0 54.8 reduce-scatter.14
  238.0 60.6 reduce-scatter.12
  301.5 53.2 reduce-scatter.10
where the time goes:
time: 362 us; the launch traced here: 361 us
  waiting for transfers between devices  219 us (60%)
  matrix products  42.5 us (12%)
  blocking collectives  39.2 us (11%)
  starting transfers between devices  20.3 us (6%)
  local copies, waits for them, and re-layouts  15.1 us (4%)
  between operations  14.3 us (4%)
  other arithmetic  10.9 us (3%)
    unnamed x7, waiting for transfers between devices  101 us
    reduce_scatter x1, waiting for transfers between devices, body(): lax.psum_scatter(weight_term.astype(jnp.bfloat16), 'ctx', scatter_dimensi...  62 us
    reduce_scatter x1, waiting for transfers between devices, body(): lax.psum_scatter(head_part.astype(jnp.bfloat16), 'head', scatter_dimensio...  56.2 us
    dot_general x10, matrix products, contract_rows(): return jnp.einsum(form, left, right, preferred_element_type=jnp.float32)  30.9 us
    all_gather x1, blocking collectives, body(): lax.all_gather(pick_rows(value_head_rows), 'ctx', axis=2, tiled=True)  20.4 us
    ppermute x8, starting transfers between devices, shifted(): return lax.ppermute(block, axis, route)  20.1 us
    all_gather x1, blocking collectives, body(): lax.all_gather(pick_rows(rotated_key_rows), 'ctx', axis=2, tiled=True)  18.8 us
    dot_general x4, matrix products, exact_map(): return jnp.einsum(form, left, right, precision=lax.Precision.HIGHEST)  8.25 us
  transfers between devices with their start and end apart: 13, of which 4 were waited for; matrix products, arithmetic and copies ran while one was open for 13% of the time, Pallas kernels for 0%

commit v1 on v0

v1 whole, which is shorter than its diff:
```python
import functools
import math

import jax
import jax.numpy as jnp
from jax import lax
from jax.experimental import pallas as pl
from jax.experimental.pallas import tpu as pltpu
from jax.sharding import PartitionSpec as P

HEAD_SIZE = 128
BLOCK_TOKENS = 64
LOCAL = 16
STRIDE = 8
TILE = 128
BF16 = jnp.bfloat16
F32 = jnp.float32
SCALE = HEAD_SIZE ** (-0.5)
EXP2_SCALE = SCALE * math.log2(math.e)
MASKED = -1e30

VMEM = pl.BlockSpec(memory_space=pltpu.VMEM)
SMEM = pl.BlockSpec(memory_space=pltpu.SMEM)
NN = (((1,), (0,)), ((), ()))
NT = (((1,), (1,)), ((), ()))
TN = (((0,), (0,)), ((), ()))


def mm(left, right, dims=NN):
    return lax.dot_general(left, right, dims, preferred_element_type=F32)


def call(kernel, name, ins, out_shapes, scratch=(), mib=32, flops=0):
    nbytes = sum(a.size * a.dtype.itemsize for a in ins)
    nbytes += sum(math.prod(s.shape) * s.dtype.itemsize for s in out_shapes)
    return pl.pallas_call(
        kernel,
        name=name,
        out_shape=out_shapes,
        in_specs=[SMEM if a.dtype == jnp.int32 else VMEM for a in ins],
        out_specs=[VMEM] * len(out_shapes),
        scratch_shapes=list(scratch),
        compiler_params=pltpu.CompilerParams(vmem_limit_bytes=mib * 2**20),
        cost_estimate=pl.CostEstimate(flops=flops, bytes_accessed=nbytes, transcendentals=0),
    )(*ins)


def shape(dims, dtype):
    return jax.ShapeDtypeStruct(dims, dtype)


def flips(count, bit):
    return [(i, i ^ bit) for i in range(count)]


def slot_owner(ctx, slot, order):
    mask = 0
    for k, bit in enumerate(order):
        if slot >> k & 1:
            mask |= bit
    return ctx ^ mask


def pack_kernel(phase_ref, k_ref, v_ref, kv_ref, pick_ref):
    rows = k_ref.shape[0]
    kv_ref[:rows] = k_ref[...]
    kv_ref[rows:] = v_ref[...]
    for r in range(2):
        start = pl.multiple_of((STRIDE - 1 - phase_ref[r]) * BLOCK_TOKENS, BLOCK_TOKENS)
        at = 2 * r * BLOCK_TOKENS
        pick_ref[at : at + BLOCK_TOKENS] = k_ref[pl.ds(start, BLOCK_TOKENS)]
        pick_ref[at + BLOCK_TOKENS : at + 2 * BLOCK_TOKENS] = v_ref[pl.ds(start, BLOCK_TOKENS)]


def load_window(core, own_ref, core_ref, two_ref, two_core_ref, part, out):
    rows = own_ref.shape[0] // 2
    piece = pl.ds(part * rows, rows)
    out[:rows] = two_ref[piece]
    out[rows : 2 * rows] = jnp.where(core == 0, two_core_ref[piece], core_ref[piece])
    out[2 * rows :] = own_ref[piece]


def band_scores(ctx, tile, chunk, tiles, k_win, q_tile):
    start = (tile + chunk) * TILE
    s = mm(k_win[start : start + TILE], q_tile, NT)
    if chunk == 0 or chunk == 2 * tiles:
        key = lax.broadcasted_iota(jnp.int32, s.shape, 0)
        token = lax.broadcasted_iota(jnp.int32, s.shape, 1) % TILE
        if chunk == 0:
            s = jnp.where(key // BLOCK_TOKENS > token // BLOCK_TOKENS, s, MASKED)
        else:
            s = jnp.where(key <= token, s, MASKED)
    if tile + chunk < 2 * tiles:
        first = 2 - (tile + chunk) // tiles
        s = jnp.where(ctx >= first, s, MASKED)
    return s


def both_heads(ref, tile):
    rows = slice(tile * TILE, (tile + 1) * TILE)
    return jnp.concatenate([ref[rows, :HEAD_SIZE], ref[rows, HEAD_SIZE:]], axis=0)


def band_forward_kernel(q_ref, own_ref, core_ref, two_ref, two_core_ref, out_ref, max_ref, sum_ref, k_win, v_win, s_buf, p_buf):
    ctx = lax.axis_index("ctx")
    core = ctx % 2
    tiles = q_ref.shape[0] // TILE
    chunks = 2 * tiles + 1
    load_window(core, own_ref, core_ref, two_ref, two_core_ref, 0, k_win)
    load_window(core, own_ref, core_ref, two_ref, two_core_ref, 1, v_win)
    for tile in range(tiles):
        q_tile = both_heads(q_ref, tile)
        top = None
        for chunk in range(chunks):
            s = band_scores(ctx, tile, chunk, tiles, k_win, q_tile)
            s_buf[chunk * TILE : (chunk + 1) * TILE] = s
            here = jnp.max(s.reshape(TILE // 8, 8, 2 * TILE), axis=0)
            top = here if top is None else jnp.maximum(top, here)
        top = jnp.max(top, axis=0, keepdims=True)
        total = None
        for chunk in range(chunks):
            p = jnp.exp2((s_buf[chunk * TILE : (chunk + 1) * TILE] - top) * EXP2_SCALE)
            here = jnp.sum(p.reshape(TILE // 8, 8, 2 * TILE), axis=0)
            total = here if total is None else total + here
            p_buf[chunk * TILE : (chunk + 1) * TILE] = p.astype(BF16)
        total = jnp.sum(total, axis=0, keepdims=True)
        out = mm(v_win[tile * TILE : (tile + chunks) * TILE], p_buf[...], TN)
        at = slice(tile * TILE, (tile + 1) * TILE)
        for r in range(2):
            half = slice(r * TILE, (r + 1) * TILE)
            out_ref[r, :, at] = out[:, half]
            max_ref[r : r + 1, at] = top[:, half]
            sum_ref[r : r + 1, at] = total[:, half]


def band_backward_kernel(
    q_ref, do_ref, own_ref, core_ref, two_ref, two_core_ref, lse_ref, dot_ref, dq_in_ref,
    dq_ref, own_out, one_out, two_out, k_win, v_win, dk_acc, dv_acc, p_buf, ds_buf,
):
    ctx = lax.axis_index("ctx")
    core = ctx % 2
    rows = q_ref.shape[0]
    tiles = rows // TILE
    chunks = 2 * tiles + 1
    load_window(core, own_ref, core_ref, two_ref, two_core_ref, 0, k_win)
    load_window(core, own_ref, core_ref, two_ref, two_core_ref, 1, v_win)
    dk_acc[...] = jnp.zeros_like(dk_acc)
    dv_acc[...] = jnp.zeros_like(dv_acc)
    for tile in range(tiles):
        q_tile = both_heads(q_ref, tile)
        do_tile = both_heads(do_ref, tile)
        at = slice(tile * TILE, (tile + 1) * TILE)
        lse = jnp.concatenate([lse_ref[0:1, at], lse_ref[1:2, at]], axis=1)
        dot = jnp.concatenate([dot_ref[0:1, at], dot_ref[1:2, at]], axis=1)
        for chunk in range(chunks):
            s = band_scores(ctx, tile, chunk, tiles, k_win, q_tile)
            p = jnp.exp2((s - lse) * EXP2_SCALE)
            start = (tile + chunk) * TILE
            dp = mm(v_win[start : start + TILE], do_tile, NT)
            piece = slice(chunk * TILE, (chunk + 1) * TILE)
            p_buf[piece] = p.astype(BF16)
            ds_buf[piece] = (p * (dp - dot)).astype(BF16)
        window = slice(tile * TILE, (tile + chunks) * TILE)
        dv_acc[window] += mm(p_buf[...], do_tile)
        dk_acc[window] += mm(ds_buf[...], q_tile)
        dq = mm(k_win[window], ds_buf[...], TN)
        for r in range(2):
            whole = (dq[:, r * TILE : (r + 1) * TILE] + dq_in_ref[r, :, at]) * SCALE
            dq_ref[at, r * HEAD_SIZE : (r + 1) * HEAD_SIZE] = whole.T.astype(BF16)
    for index, out in ((0, two_out), (1, one_out), (2, own_out)):
        part = slice(index * rows, (index + 1) * rows)
        out[:rows] = (dk_acc[part] * SCALE).astype(BF16)
        out[rows:] = dv_acc[part].astype(BF16)


def load_picked(mine_ref, other_ref, r, part, out):
    size = 4 * BLOCK_TOKENS
    slots = mine_ref.shape[0] // size
    for slot in range(2 * slots):
        source = mine_ref if slot < slots else other_ref
        start = (slot % slots) * size + (2 * r + part) * BLOCK_TOKENS
        out[slot * BLOCK_TOKENS : (slot + 1) * BLOCK_TOKENS] = source[start : start + BLOCK_TOKENS]


def slot_scores(ctx, slot, order, phase, token_start, s):
    owner = slot_owner(ctx, slot, order)
    token = token_start + lax.broadcasted_iota(jnp.int32, s.shape, 1)
    first = jnp.where(owner < ctx - 2, 0, jnp.where(owner == ctx - 2, (STRIDE - 1 - phase) * BLOCK_TOKENS, 2**30))
    return jnp.where(token >= first, s, MASKED)


def stride_forward_kernel(order, phase_ref, q_ref, mine_ref, other_ref, out_in_ref, max_in_ref, sum_in_ref, att_ref, lse_ref, k_pick, v_pick, s_buf, p_buf):
    ctx = lax.axis_index("ctx")
    rows = q_ref.shape[0]
    slots = k_pick.shape[0] // BLOCK_TOKENS
    width = 2 * TILE
    for r in range(2):
        load_picked(mine_ref, other_ref, r, 0, k_pick)
        load_picked(mine_ref, other_ref, r, 1, v_pick)
        for token_start in range(0, rows, width):
            at = slice(token_start, token_start + width)
            q_tile = q_ref[at, r * HEAD_SIZE : (r + 1) * HEAD_SIZE]
            old = max_in_ref[r : r + 1, at]
            top = None
            for slot in range(slots):
                piece = slice(slot * BLOCK_TOKENS, (slot + 1) * BLOCK_TOKENS)
                s = slot_scores(ctx, slot, order, phase_ref[r], token_start, mm(k_pick[piece], q_tile, NT))
                s_buf[piece] = s
                here = jnp.max(s.reshape(BLOCK_TOKENS // 8, 8, width), axis=0)
                top = here if top is None else jnp.maximum(top, here)
            top = jnp.maximum(jnp.max(top, axis=0, keepdims=True), old)
            total = None
            for slot in range(slots):
                piece = slice(slot * BLOCK_TOKENS, (slot + 1) * BLOCK_TOKENS)
                p = jnp.exp2((s_buf[piece] - top) * EXP2_SCALE)
                here = jnp.sum(p.reshape(BLOCK_TOKENS // 8, 8, width), axis=0)
                total = here if total is None else total + here
                p_buf[piece] = p.astype(BF16)
            factor = jnp.exp2((old - top) * EXP2_SCALE)
            total = jnp.sum(total, axis=0, keepdims=True) + sum_in_ref[r : r + 1, at] * factor
            out = mm(v_pick[...], p_buf[...], TN) + out_in_ref[r, :, at] * factor
            out = out / total
            att_ref[at, r * HEAD_SIZE : (r + 1) * HEAD_SIZE] = out.T.astype(BF16)
            lse_ref[r : r + 1, at] = top + jnp.log2(total) * (1.0 / EXP2_SCALE)


def stride_backward_kernel(order, phase_ref, q_ref, grad_own_ref, grad_got_ref, att_ref, lse_ref, mine_ref, other_ref, do_ref, dot_ref, dq_ref, keep_ref, send_ref, k_pick, v_pick, p_buf, ds_buf):
    ctx = lax.axis_index("ctx")
    rows = q_ref.shape[0]
    slots = k_pick.shape[0] // BLOCK_TOKENS
    width = 2 * TILE
    size = 4 * BLOCK_TOKENS
    do_ref[...] = (grad_own_ref[...] + grad_got_ref[...].astype(F32)).astype(BF16)
    for r in range(2):
        head = slice(r * HEAD_SIZE, (r + 1) * HEAD_SIZE)
        product = do_ref[:, head].astype(F32) * att_ref[:, head].astype(F32)
        dot_ref[r : r + 1, :] = jnp.sum(product.T, axis=0, keepdims=True)
        load_picked(mine_ref, other_ref, r, 0, k_pick)
        load_picked(mine_ref, other_ref, r, 1, v_pick)
        for token_start in range(0, rows, width):
            at = slice(token_start, token_start + width)
            q_tile = q_ref[at, head]
            do_tile = do_ref[at, head]
            lse = lse_ref[r : r + 1, at]
            dot = dot_ref[r : r + 1, at]
            for slot in range(slots):
                piece = slice(slot * BLOCK_TOKENS, (slot + 1) * BLOCK_TOKENS)
                s = slot_scores(ctx, slot, order, phase_ref[r], token_start, mm(k_pick[piece], q_tile, NT))
                p = jnp.exp2((s - lse) * EXP2_SCALE)
                dp = mm(v_pick[piece], do_tile, NT)
                p_buf[piece, at] = p.astype(BF16)
                ds_buf[piece, at] = (p * (dp - dot)).astype(BF16)
        dv = mm(p_buf[...], do_ref[:, head])
        dk = mm(ds_buf[...], q_ref[:, head]) * SCALE
        dq_ref[r] = mm(k_pick[...], ds_buf[...], TN)
        for slot in range(slots):
            target = keep_ref if slot < slots // 2 else send_ref
            start = (slot % (slots // 2)) * size + 2 * r * BLOCK_TOKENS
            piece = slice(slot * BLOCK_TOKENS, (slot + 1) * BLOCK_TOKENS)
            target[start : start + BLOCK_TOKENS] = dk[piece].astype(BF16)
            target[start + BLOCK_TOKENS : start + 2 * BLOCK_TOKENS] = dv[piece].astype(BF16)


def finish_kernel(phase_ref, own_ref, core_ref, two_ref, stride_a_ref, stride_b_ref, dk_ref, dv_ref, acc):
    even = lax.axis_index("ctx") % 2 == 0
    rows = dk_ref.shape[0]
    acc[...] = own_ref[...].astype(F32) + two_ref[...].astype(F32) + jnp.where(even, core_ref[...].astype(F32), 0.0)
    stride = stride_a_ref[...].astype(F32) + stride_b_ref[...].astype(F32)
    for r in range(2):
        for part in range(2):
            start = pl.multiple_of(part * rows + (STRIDE - 1 - phase_ref[r]) * BLOCK_TOKENS, BLOCK_TOKENS)
            at = (2 * r + part) * BLOCK_TOKENS
            acc[pl.ds(start, BLOCK_TOKENS)] += stride[at : at + BLOCK_TOKENS]
    dk_ref[...] = acc[:rows].astype(BF16)
    dv_ref[...] = acc[rows:].astype(BF16)


def grad_own_kernel(g_ref, w_ref, out_ref):
    width = g_ref.shape[1]
    start = pl.multiple_of(lax.axis_index("head") * width, width)
    out_ref[...] = mm(g_ref[...], w_ref[:, pl.ds(start, width)], NT)


def grad_other_kernel(g_ref, near_ref, far_ref, out_ref):
    core = lax.axis_index("ctx") % 2
    width = near_ref.shape[1]
    near = pl.ds(pl.multiple_of(core * width, width), width)
    far = pl.ds(pl.multiple_of((1 - core) * width, width), width)
    total = mm(g_ref[:, near], near_ref[...], NT) + mm(g_ref[:, far], far_ref[...], NT)
    out_ref[...] = total.astype(BF16)


def layer_out_kernel(own_ref, other_ref, w_ref, near_ref, far_ref, out_ref):
    core = lax.axis_index("ctx") % 2
    width = near_ref.shape[1]
    base = lax.axis_index("head") * 2 * width
    step = 256
    for part, source in ((core, near_ref), (1 - core, far_ref)):
        for at in range(0, width, step):
            start = part * width + at
            w_own = w_ref[:, pl.ds(pl.multiple_of(base + start, step), step)]
            total = mm(own_ref[...], w_own) + mm(other_ref[...], source[:, at : at + step])
            out_ref[:, pl.ds(pl.multiple_of(start, step), step)] = total.astype(BF16)


def weight_grad_kernel(bits, att_ref, g_ref, keep_ref, send_ref):
    ctx = lax.axis_index("ctx")
    _, _, cols = keep_ref.shape
    blocks = 1 << len(bits)
    att = att_ref[...].T
    for slot in range(blocks):
        mask = 0
        for k, bit in enumerate(bits):
            if slot >> (len(bits) - 1 - k) & 1:
                mask |= bit
        block = (ctx % blocks) ^ mask
        term = mm(att, g_ref[:, pl.ds(pl.multiple_of(block * cols, cols), cols)]).astype(BF16)
        if slot < blocks // 2:
            keep_ref[slot] = term
        else:
            send_ref[slot - blocks // 2] = term


def add(left, right):
    return left.astype(F32) + right.astype(F32)


def body(queries, rotated_key_rows, value_head_rows, stride_offset, w_out, grad_out):
    rows = queries.shape[0]
    n_ctx = lax.axis_size("ctx")
    n_head = lax.axis_size("head")
    ctx = lax.axis_index("ctx")
    head = lax.axis_index("head")
    core = ctx % 2
    model = w_out.shape[1]
    width = grad_out.shape[1]
    head_rows = w_out.shape[0]
    ratio = n_ctx // n_head
    cols = model // n_ctx
    flip = functools.partial(flips, n_ctx)
    swap = [(0, 1), (1, 0)]
    scores = rows * 2 * HEAD_SIZE * 2
    proj = 2 * rows * head_rows * width

    kv, picks = call(
        pack_kernel, "pack", [stride_offset, rotated_key_rows, value_head_rows],
        [shape((2 * rows, HEAD_SIZE), BF16), shape((4 * BLOCK_TOKENS, HEAD_SIZE), BF16)],
    )
    if n_head == 2:
        half = width // 2
        piece = lax.dynamic_slice(w_out, (0, (1 - head) * width + core * half), (head_rows, half))
        w_near = lax.ppermute(piece, "head", swap)
        w_far = lax.ppermute(w_near, "ctx", flip(1))
    else:
        w_all = lax.all_to_all(w_out, "head", 1, 0, tiled=True)
    kv_core = lax.ppermute(kv, "ctx", flip(1))
    kv_two = lax.ppermute(kv, "ctx", [(i, i + 2) for i in range(n_ctx - 2)])
    kv_two_core = lax.ppermute(kv_two, "ctx", flip(1))
    order = []
    bit = 4
    while bit < n_ctx:
        order.append(bit)
        bit *= 2
    order += [2, 1]
    for bit in order[:-1]:
        picks = jnp.concatenate([picks, lax.ppermute(picks, "ctx", flip(bit))], axis=0)
    picks_other = lax.ppermute(picks, "ctx", flip(1))

    chunk_rows = (2 * (rows // TILE) + 1) * TILE
    window = pltpu.VMEM((3 * rows, HEAD_SIZE), BF16)
    out, top, total = call(
        band_forward_kernel, "band_forward", [queries, kv, kv_core, kv_two, kv_two_core],
        [shape((2, HEAD_SIZE, rows), F32), shape((2, rows), F32), shape((2, rows), F32)],
        [window, window, pltpu.VMEM((chunk_rows, 2 * TILE), F32), pltpu.VMEM((chunk_rows, 2 * TILE), BF16)],
        flops=2 * scores * chunk_rows,
    )
    if n_head == 2:
        grad_own, = call(
            grad_own_kernel, "grad_own", [grad_out, w_out], [shape((rows, head_rows), F32)], flops=proj
        )
        grad_other, = call(
            grad_other_kernel, "grad_other", [grad_out, w_near, w_far],
            [shape((rows, head_rows), BF16)], flops=proj,
        )
        grad_got = lax.ppermute(grad_other, "head", swap)
    else:
        grad_all = mm(grad_out, w_all, NT).astype(BF16)
        grad_all = lax.all_to_all(grad_all.reshape(rows, n_head, head_rows), "head", 1, 0, tiled=True)
        grad_all = grad_all.reshape(n_head, rows, head_rows).astype(F32)
        grad_own = jnp.sum(grad_all, axis=0)
        grad_got = jnp.zeros((rows, head_rows), BF16)
    picked_rows = n_ctx * BLOCK_TOKENS
    pick = pltpu.VMEM((picked_rows, HEAD_SIZE), BF16)
    attended, lse = call(
        functools.partial(stride_forward_kernel, tuple(order)), "stride_forward",
        [stride_offset, queries, picks, picks_other, out, top, total],
        [shape((rows, head_rows), BF16), shape((2, rows), F32)],
        [pick, pick, pltpu.VMEM((picked_rows, 2 * TILE), F32), pltpu.VMEM((picked_rows, 2 * TILE), BF16)],
        flops=2 * scores * picked_rows,
    )
    if n_head == 2:
        att_other = lax.ppermute(attended, "head", swap)
    grad_att, row_dot, grad_q, stride_keep, stride_send = call(
        functools.partial(stride_backward_kernel, tuple(order)), "stride_backward",
        [stride_offset, queries, grad_own, grad_got, attended, lse, picks, picks_other],
        [
            shape((rows, head_rows), BF16), shape((2, rows), F32), shape((2, HEAD_SIZE, rows), F32),
            shape(picks.shape, BF16), shape(picks.shape, BF16),
        ],
        [pick, pick, pltpu.VMEM((picked_rows, rows), BF16), pltpu.VMEM((picked_rows, rows), BF16)],
        flops=5 * scores * picked_rows,
    )
    for bit in reversed(order):
        got = lax.ppermute(stride_send, "ctx", flip(bit))
        if bit != order[0]:
            both = add(stride_keep, got)
            middle = both.shape[0] // 2
            stride_keep, stride_send = both[:middle], both[middle:].astype(BF16)
    stride_got = got

    grad_queries, own, one, two = call(
        band_backward_kernel, "band_backward",
        [queries, grad_att, kv, kv_core, kv_two, kv_two_core, lse, row_dot, grad_q],
        [shape((rows, head_rows), BF16)] + [shape((2 * rows, HEAD_SIZE), BF16)] * 3,
        [
            window, window, pltpu.VMEM((3 * rows, HEAD_SIZE), F32), pltpu.VMEM((3 * rows, HEAD_SIZE), F32),
            pltpu.VMEM((chunk_rows, 2 * TILE), BF16), pltpu.VMEM((chunk_rows, 2 * TILE), BF16),
        ],
        flops=5 * scores * chunk_rows,
    )
    one_got = lax.ppermute(one, "ctx", flip(1))
    two = jnp.where(core == 1, add(two, one_got), two.astype(F32)).astype(BF16)
    two_got = lax.ppermute(two, "ctx", [(i + 2, i) for i in range(n_ctx - 2)])

    if n_head == 2:
        layer_out, = call(
            layer_out_kernel, "layer_out", [attended, att_other, w_out, w_near, w_far],
            [shape((rows, width), BF16)], flops=2 * proj,
        )
        bits = []
        bit = 1
        while bit < ratio:
            bits.append(bit)
            bit *= 2
        high = n_ctx // 2
        ended = []
        for source, name in ((attended, "weight_grad_own"), (att_other, "weight_grad_other")):
            part = shape((ratio // 2, head_rows, cols), BF16)
            keep, send = call(
                functools.partial(weight_grad_kernel, tuple(bits)), name, [source, grad_out],
                [part, part], flops=proj,
            )
            for bit in bits:
                got = lax.ppermute(send, "ctx", flip(bit))
                both = add(keep, got)
                if bit != bits[-1]:
                    middle = both.shape[0] // 2
                    keep, send = both[:middle], both[middle:].astype(BF16)
            ended.append(both[0])
        sum_own, sum_other = ended
        same = (ctx // high) == head
        first_route, second_route = [], []
        for c in range(n_ctx):
            for h in range(2):
                here = 2 * c + h
                if c // high == h:
                    first_route.append((here, 2 * c + 1 - h))
                else:
                    first_route.append((here, 2 * (c ^ high) + h))
                    second_route.append((here, 2 * (c ^ high) + 1 - h))
        other_low = sum_other.astype(BF16)
        first = lax.ppermute(jnp.where(same, other_low, sum_own.astype(BF16)), ("ctx", "head"), first_route)
        second = lax.ppermute(other_low, ("ctx", "head"), second_route)
        grad_w_out = (first.astype(F32) + jnp.where(same, sum_own, second.astype(F32))).astype(BF16)
    else:
        att_all = lax.all_gather(attended, "head", axis=1, tiled=True)
        layer_out = mm(att_all, w_all).astype(BF16)
        terms = mm(att_all, grad_out, TN).astype(BF16).reshape(n_head, head_rows, ratio, cols)
        terms = jnp.transpose(terms, (0, 2, 1, 3)).reshape(n_ctx, head_rows, cols)
        terms = lax.psum_scatter(terms, "ctx", scatter_dimension=0, tiled=True)[0]
        route = []
        for c in range(n_ctx):
            for h in range(n_head):
                target = (h * ratio + c % ratio) * n_head + c // ratio
                route.append((c * n_head + h, target))
        grad_w_out = lax.ppermute(terms, ("ctx", "head"), route)

    key_gradient, value_gradient = call(
        finish_kernel, "finish", [stride_offset, own, one_got, two_got, stride_keep, stride_got],
        [shape((rows, HEAD_SIZE), BF16)] * 2,
        [pltpu.VMEM((2 * rows, HEAD_SIZE), F32)],
    )
    return (layer_out, grad_queries, key_gradient, value_gradient, grad_w_out)


def solution(mesh):
    placed = (
        P("ctx", "head"),
        P("ctx", "head"),
        P("ctx", "head"),
        P("head"),
        P("head", None),
        P("ctx", "head"),
    )
    return jax.shard_map(
        body,
        mesh=mesh,
        in_specs=placed,
        out_specs=(
            P("ctx", "head"),
            P("ctx", "head"),
            P("ctx", "head"),
            P("ctx", "head"),
            P("head", "ctx"),
        ),
        check_vma=False,
    )
```

time: 362 us -> 116 us (0.32)
  waiting for transfers between devices: 219 us -> 50.7 us
  matrix products: 42.5 us -> 0 us
  blocking collectives: 39.2 us -> 0 us
  Pallas kernels: 0 us -> 29.2 us
  between operations: 14.3 us -> 1.06 us
  local copies, waits for them, and re-layouts: 15.1 us -> 6.24 us
  other arithmetic: 10.9 us -> 2.44 us
  starting transfers between devices: 20.3 us -> 25.8 us
    reduce_scatter x2 -> x0, waiting for transfers between devices: 118 us -> none  [the longest x1 62 us: body(): lax.psum_scatter(weight_term.astype(jnp.bfloat16), 'ctx', scatter_dimensi...]
    unnamed x7 -> x0, waiting for transfers between devices: 101 us -> none
    ppermute x8 -> x25, waiting for transfers between devices: 0.02 us -> 50.7 us  [the longest x4 18.5 us: body(): got = lax.ppermute(stride_send, 'ctx', flip(bit))]
    dot_general x15 -> x0, matrix products: 42.5 us -> none  [the longest x10 30.9 us: contract_rows(): return jnp.einsum(form, left, right, preferred_element_type=jnp.float32)]
    all_gather x2 -> x0, blocking collectives: 39.2 us -> none  [the longest x1 20.4 us: body(): lax.all_gather(pick_rows(value_head_rows), 'ctx', axis=2, tiled=True)]
    pallas_call x0 -> x11, Pallas kernels: none -> 29.2 us  [call(): pl.pallas_call(kernel, name=name, out_shape=out_shapes, in_specs=[SMEM if...]
    ppermute x8 -> x25, starting transfers between devices: 20.1 us -> 25.8 us  [the longest x3 7.05 us: body(): lax.ppermute(picks, 'ctx', flip(bit))]
    while x5 -> x0, local copies, waits for them, and re-layouts: 4.8 us -> none  [the longest x4 3.68 us: body(): lax.fori_loop(0, tile_count, forward_tile, (row_max, row_sum, weighted))]
  transfers between devices with their start and end apart: 13 -> 25, of which waited for: 4 -> 12; matrix products, arithmetic and copies ran while one was open for 13% -> 3% of each run, Pallas kernels for 0% -> 23%
where the time goes in v1:
time: 116 us; the launch traced here: 115 us
  waiting for transfers between devices  50.7 us (44%)
  Pallas kernels  29.2 us (25%)
  starting transfers between devices  25.8 us (22%)
  local copies, waits for them, and re-layouts  6.24 us (5%)
  other arithmetic  2.44 us (2%)
    pallas_call x11, Pallas kernels, call(): pl.pallas_call(kernel, name=name, out_shape=out_shapes, in_specs=[SMEM if...  29.2 us
    ppermute x4, waiting for transfers between devices, body(): got = lax.ppermute(stride_send, 'ctx', flip(bit))  18.5 us
    ppermute x6, waiting for transfers between devices, body(): got = lax.ppermute(send, 'ctx', flip(bit))  14.5 us
    ppermute x3, waiting for transfers between devices, body(): lax.ppermute(picks, 'ctx', flip(bit))  7.84 us
    ppermute x3, starting transfers between devices, body(): lax.ppermute(picks, 'ctx', flip(bit))  7.05 us
    ppermute x6, starting transfers between devices, body(): got = lax.ppermute(send, 'ctx', flip(bit))  5.11 us
    unnamed x43, local copies, waits for them, and re-layouts  4.97 us
    ppermute x1, starting transfers between devices, body(): kv_two = lax.ppermute(kv, 'ctx', [(i, i + 2) for i in range(n_ctx - 2)])  4.11 us
  transfers between devices with their start and end apart: 25, of which 12 were waited for; matrix products, arithmetic and copies ran while one was open for 3% of the time, Pallas kernels for 23%

profile of v1, /device:TPU:0, one launch (start us, length us, event | category | flops | bytes accessed | tf_op | source)
XLA Modules:
  0.0 115.5 jit_solution(901104381487458709)
XLA Ops:
  0.6 0.9 copy-done.5
  1.5 0.9 copy-done.6
  2.4 0.7 copy-done.9
  3.1 1.2 %pack.1 = (bf16[1024,128]{1,0:T(8,128)(2,1)}, bf16[256,128]{1,0:T(8,128)(2,1)S(1)}) custom-call(s32[2]{0:T(128)S(1)} %copy-done.9, bf16[512,128]{1,0:T(8,128)(2,1)S(1)} %copy-done.5, bf16[512,128]{1,0:T(8,128)(2,1)S(1)} %copy-done.6), custom_call_target="tpu_custom_call" | custom-call | bytes 589832 | tf_op jit(solution)/shard_map/pack/pallas_call | solution.py:36
  4.3 3.0 %collective-permute-start = (bf16[256,128]{1,0:T(8,128)(2,1)S(1)}, bf16[256,128]{1,0:T(8,128)(2,1)S(1)}, u32[]{:S(2)}, u32[]{:S(2)}) collective-permute-start(bf16[256,128]{1,0:T(8,128)(2,1)S(1)} %get-tuple-element.27), channel_id=1, source_target_pairs={{0,8},{2,10},{4,12},{6,14},{8,0},{10,2},{12,4},{14,6},{16,24},{18,... | collective-permute-start | bytes 196616 | tf_op jit(solution)/shard_map/ppermute | solution.py:366
  7.4 2.2 %collective-permute-done = bf16[256,128]{1,0:T(8,128)(2,1)S(1)} collective-permute-done((bf16[256,128]{1,0:T(8,128)(2,1)S(1)}, bf16[256,128]{1,0:T(8,128)(2,1)S(1)}, u32[]{:S(2)}, u32[]{:S(2)}) %collective-permute-start) | collective-permute-done | bytes 65568 | tf_op jit(solution)/shard_map/ppermute | solution.py:366
  9.6 3.1 %collective-permute-start.1 = (bf16[512,128]{1,0:T(8,128)(2,1)S(1)}, bf16[512,128]{1,0:T(8,128)(2,1)S(1)}, u32[]{:S(2)}, u32[]{:S(2)}) collective-permute-start(bf16[512,128]{1,0:T(8,128)(2,1)S(1)} %pad_maximum_fusion.1), channel_id=1, source_target_pairs={{0,16},{2,18},{4,20},{6,22},{8,24},{10,26},{12,28},{14,30},{16,0},... | collective-permute-start | bytes 393224 | tf_op jit(solution)/shard_map/ppermute | solution.py:366
  12.7 4.1 %collective-permute-start.5 = (bf16[1024,128]{1,0:T(8,128)(2,1)}, bf16[1024,128]{1,0:T(8,128)(2,1)}, u32[]{:S(2)}, u32[]{:S(2)}) collective-permute-start(bf16[1024,128]{1,0:T(8,128)(2,1)} %get-tuple-element.28.own_ref), channel_id=1, source_target_pairs={{0,4},{2,6},{4,8},{6,10},{8,12},{10,14},{12,16},{14,18},{16,20},{1... | collective-permute-start | bytes 786440 | tf_op jit(solution)/shard_map/ppermute | solution.py:357
  16.8 1.1 constant_dynamic-slice_fusion
  17.9 0.0 copy-start.10
  17.9 0.0 copy-start.14
  17.9 1.6 %collective-permute-start.8 = (bf16[256,1024]{1,0:T(8,128)(2,1)S(1)}, bf16[256,1024]{1,0:T(8,128)(2,1)S(1)}, u32[]{:S(2)}, u32[]{:S(2)}) collective-permute-start(bf16[256,1024]{1,0:T(8,128)(2,1)S(1)} %constant_dynamic-slice_fusion), channel_id=1, source_target_pairs={{0,1},{1,0},{2,3},{3,2},{4,5},{5,4},{6,7},{7,6},{8,9},{9,8},{10,11... | collective-permute-start | bytes 1572872 | tf_op jit(solution)/shard_map/ppermute | solution.py:352
  19.5 0.9 collective-permute-start.2
  20.5 5.6 %collective-permute-done.2 = bf16[1024,128]{1,0:T(8,128)(2,1)S(1)} collective-permute-done((bf16[1024,128]{1,0:T(8,128)(2,1)S(1)}, bf16[1024,128]{1,0:T(8,128)(2,1)S(1)}, u32[]{:S(2)}, u32[]{:S(2)}) %collective-permute-start.2) | collective-permute-done | bytes 262176 | tf_op jit(solution)/shard_map/ppermute | solution.py:366
  26.1 0.0 copy-start
  26.2 0.1 collective-permute-start.3
  26.2 3.7 %collective-permute-done.8.near_ref = bf16[256,1024]{1,0:T(8,128)(2,1)S(1)} collective-permute-done((bf16[256,1024]{1,0:T(8,128)(2,1)S(1)}, bf16[256,1024]{1,0:T(8,128)(2,1)S(1)}, u32[]{:S(2)}, u32[]{:S(2)}) %collective-permute-start.8) | collective-permute-done | bytes 524320 | tf_op jit(solution)/shard_map/ppermute | solution.py:352
  30.0 0.5 collective-permute-start.4
  30.5 1.6 %collective-permute-done.4.core_ref = bf16[1024,128]{1,0:T(8,128)(2,1)S(1)} collective-permute-done((bf16[1024,128]{1,0:T(8,128)(2,1)}, bf16[1024,128]{1,0:T(8,128)(2,1)S(1)}, u32[]{:S(2)}, u32[]{:S(2)}) %collective-permute-start.4) | collective-permute-done | bytes 262176 | tf_op jit(solution)/shard_map/ppermute | solution.py:356
  32.1 0.7 collective-permute-done.6.two_core_ref
  32.8 3.7 %band_forward.1 = (f32[2,128,512]{2,1,0:T(8,128)S(1)}, f32[2,512]{1,0:T(2,128)S(1)}, f32[2,512]{1,0:T(2,128)S(1)}) custom-call(bf16[512,256]{1,0:T(8,128)(2,1)S(1)} %copy-done.13, bf16[1024,128]{1,0:T(8,128)(2,1)} %get-tuple-element.28.own_ref, bf16[1024,128]{1,0:T(8,128)(2,1)S(1)} %collective-permute-done.4.core_ref, ...), custom_call_target="tpu_custom_call" | custom-call | flops 603979776 | bytes 1843200 | tf_op jit(solution)/shard_map/band_forward/pallas_call | solution.py:36
  36.6 3.5 %stride_forward.1 = (bf16[512,256]{1,0:T(8,128)(2,1)S(1)}, f32[2,512]{1,0:T(2,128)S(1)}) custom-call(s32[2]{0:T(128)S(1)} %copy-done.10, bf16[512,256]{1,0:T(8,128)(2,1)S(1)} %copy-done.14, bf16[2048,128]{1,0:T(8,128)(2,1)S(1)} %constant_dynamic-update-slice_fusion.mine_ref, bf16[2048,128]{1,0:T(8,128)(2,1)S(1)} %collective-permute-done.3.other_ref, ...), custom_call_target="tpu_custom_call" | custom-call | flops 536870912 | bytes 2109448 | tf_op jit(solution)/shard_map/stride_forward/pallas_call | solution.py:36
  40.2 1.6 %collective-permute-start.7 = (bf16[512,256]{1,0:T(8,128)(2,1)S(1)}, bf16[512,256]{1,0:T(8,128)(2,1)}, u32[]{:S(2)}, u32[]{:S(2)}) collective-permute-start(bf16[512,256]{1,0:T(8,128)(2,1)S(1)} %get-tuple-element.32.own_ref.att_ref), channel_id=1, source_target_pairs={{0,1},{1,0},{2,3},{3,2},{4,5},{5,4},{6,7},{7,6},{8,9},{9,8},{10,11... | collective-permute-start | bytes 786440 | tf_op jit(solution)/shard_map/ppermute | solution.py:402
  41.8 1.4 %grad_other.1 = bf16[512,256]{1,0:T(8,128)(2,1)} custom-call(bf16[512,2048]{1,0:T(8,128)(2,1)S(1)} %copy-done, bf16[256,1024]{1,0:T(8,128)(2,1)S(1)} %collective-permute-done.8.near_ref, bf16[256,1024]{1,0:T(8,128)(2,1)S(1)} %collective-permute-done.9.far_ref), custom_call_target="tpu_custom_call" | custom-call | flops 536870912 | bytes 3407872 | tf_op jit(solution)/shard_map/grad_other/pallas_call | solution.py:36
  43.2 0.5 collective-permute-start.10
  43.7 1.5 %weight_grad_own.1 = (bf16[4,256,256]{2,1,0:T(8,128)(2,1)S(1)}, bf16[4,256,256]{2,1,0:T(8,128)(2,1)}) custom-call(bf16[512,256]{1,0:T(8,128)(2,1)S(1)} %get-tuple-element.32.own_ref.att_ref, bf16[512,2048]{1,0:T(8,128)(2,1)S(1)} %copy-done), custom_call_target="tpu_custom_call" | custom-call | flops 536870912 | bytes 3407872 | tf_op jit(solution)/shard_map/weight_grad_own/pallas_call | solution.py:36
  45.3 0.8 copy-done.3
  46.1 1.6 %copy-done.1 = bf16[256,4096]{1,0:T(8,128)(2,1)S(1)} copy-done((bf16[256,4096]{1,0:T(8,128)(2,1)S(1)}, bf16[256,4096]{1,0:T(8,128)(2,1)}, u32[]{:S(2)}) %copy-start.1) | copy-done | bytes 2097176
  47.7 0.7 grad_own.1.grad_own_ref
  48.4 0.0 copy-start.2
  48.5 1.1 collective-permute-done.7.other_ref.att_ref
  49.5 1.7 %weight_grad_other.1 = (bf16[4,256,256]{2,1,0:T(8,128)(2,1)S(1)}, bf16[4,256,256]{2,1,0:T(8,128)(2,1)S(1)}) custom-call(bf16[512,256]{1,0:T(8,128)(2,1)} %collective-permute-done.7.other_ref.att_ref, bf16[512,2048]{1,0:T(8,128)(2,1)S(1)} %copy-done), custom_call_target="tpu_custom_call" | custom-call | flops 536870912 | bytes 3407872 | tf_op jit(solution)/shard_map/weight_grad_other/pallas_call | solution.py:36
  51.2 0.0 copy-start.15
  51.2 0.1 collective-permute-start.17
  51.3 3.6 %layer_out.1 = bf16[512,2048]{1,0:T(8,128)(2,1)} custom-call(bf16[512,256]{1,0:T(8,128)(2,1)S(1)} %get-tuple-element.32.own_ref.att_ref, bf16[512,256]{1,0:T(8,128)(2,1)} %collective-permute-done.7.other_ref.att_ref, bf16[256,4096]{1,0:T(8,128)(2,1)S(1)} %copy-done.2, bf16[256,1024]{1,0:T(8,128)(2,1)S(1)} %collective-permute-done.8.near_ref, ...), custom_call_target="tpu_custom_call" | custom-call | flops 1073741824 | bytes 5767168 | tf_op jit(solution)/shard_map/layer_out/pallas_call | solution.py:36
  55.0 5.3 %stride_backward.1 = (bf16[512,256]{1,0:T(8,128)(2,1)S(1)}, f32[2,512]{1,0:T(2,128)S(1)}, f32[2,128,512]{2,1,0:T(8,128)S(1)}, bf16[2048,128]{1,0:T(8,128)(2,1)S(1)}, bf16[2048,128]{1,0:T(8,128)(2,1)S(1)}) custom-call(s32[2]{0:T(128)S(1)} %copy-done.10, bf16[512,256]{1,0:T(8,128)(2,1)S(1)} %copy-done.15, f32[512,256]{1,0:T(8,128)S(1)} %grad_own.1.grad_own_ref, ...), custom_call_target="tpu_custom_call" | custom-call | flops 1342177280 | bytes 4202504 | tf_op jit(solution)/shard_map/stride_backward/pallas_call | solution.py:36
  60.3 4.9 %band_backward.1 = (bf16[512,256]{1,0:T(8,128)(2,1)}, bf16[1024,128]{1,0:T(8,128)(2,1)S(1)}, bf16[1024,128]{1,0:T(8,128)(2,1)S(1)}, bf16[1024,128]{1,0:T(8,128)(2,1)S(1)}) custom-call(bf16[512,256]{1,0:T(8,128)(2,1)S(1)} %copy-done.15, bf16[512,256]{1,0:T(8,128)(2,1)S(1)} %get-tuple-element.34.do_ref, bf16[1024,128]{1,0:T(8,128)(2,1)} %get-tuple-element.28.own_ref, ...), custom_call_target="tpu_custom_call" | custom-call | flops 1509949440 | bytes 3153920 | tf_op jit(solution)/shard_map/band_backward/pallas_call | solution.py:36
  65.2 0.4 collective-permute-start.11
  65.6 0.1 collective-permute-start.13
  65.8 1.1 convert_add_fusion
  66.9 0.9 collective-permute-start.21
  67.9 0.1 fusion
  68.0 1.3 %collective-permute-start.12 = (bf16[1024,128]{1,0:T(8,128)(2,1)S(1)}, bf16[1024,128]{1,0:T(8,128)(2,1)S(1)}, u32[]{:S(2)}, u32[]{:S(2)}) collective-permute-start(bf16[1024,128]{1,0:T(8,128)(2,1)S(1)} %fusion), channel_id=1, source_target_pairs={{4,0},{6,2},{8,4},{10,6},{12,8},{14,10},{16,12},{18,14},{20,16},{2... | collective-permute-start | bytes 786440 | tf_op jit(solution)/shard_map/ppermute | solution.py:433
  69.3 0.1 convert_add_fusion.1
  69.4 2.7 %collective-permute-start.18 = (bf16[2,256,256]{2,1,0:T(8,128)(2,1)S(1)}, bf16[2,256,256]{2,1,0:T(8,128)(2,1)S(1)}, u32[]{:S(2)}, u32[]{:S(2)}) collective-permute-start(bf16[2,256,256]{2,1,0:T(8,128)(2,1)S(1)} %slice.103), channel_id=1, source_target_pairs={{0,4},{2,6},{4,0},{6,2},{8,12},{10,14},{12,8},{14,10},{16,20},{18,... | collective-permute-start | bytes 786440 | tf_op jit(solution)/shard_map/ppermute | solution.py:454
  72.2 0.1 convert_add_fusion.2
  72.3 0.1 collective-permute-start.14
  72.4 7.7 %collective-permute-done.21 = bf16[2,256,256]{2,1,0:T(8,128)(2,1)S(1)} collective-permute-done((bf16[2,256,256]{2,1,0:T(8,128)(2,1)S(1)}, bf16[2,256,256]{2,1,0:T(8,128)(2,1)S(1)}, u32[]{:S(2)}, u32[]{:S(2)}) %collective-permute-start.21) | collective-permute-done | bytes 262176 | tf_op jit(solution)/shard_map/ppermute | solution.py:454
  80.1 0.1 slice_add_fusion
  80.2 0.4 collective-permute-start.22
  80.6 6.7 %collective-permute-done.18 = bf16[2,256,256]{2,1,0:T(8,128)(2,1)S(1)} collective-permute-done((bf16[2,256,256]{2,1,0:T(8,128)(2,1)S(1)}, bf16[2,256,256]{2,1,0:T(8,128)(2,1)S(1)}, u32[]{:S(2)}, u32[]{:S(2)}) %collective-permute-start.18) | collective-permute-done | bytes 262176 | tf_op jit(solution)/shard_map/ppermute | solution.py:454
  87.4 0.1 slice_add_fusion.1
  87.4 1.0 collective-permute-start.19
  88.4 4.1 %collective-permute-done.14 = bf16[1024,128]{1,0:T(8,128)(2,1)S(1)} collective-permute-done((bf16[1024,128]{1,0:T(8,128)(2,1)S(1)}, bf16[1024,128]{1,0:T(8,128)(2,1)S(1)}, u32[]{:S(2)}, u32[]{:S(2)}) %collective-permute-start.14) | collective-permute-done | bytes 262176 | tf_op jit(solution)/shard_map/ppermute | solution.py:414
  92.6 1.9 %collective-permute-start.15 = (bf16[512,128]{1,0:T(8,128)(2,1)S(1)}, bf16[512,128]{1,0:T(8,128)(2,1)S(1)}, u32[]{:S(2)}, u32[]{:S(2)}) collective-permute-start(bf16[512,128]{1,0:T(8,128)(2,1)S(1)} %slice.107), channel_id=1, source_target_pairs={{0,16},{2,18},{4,20},{6,22},{8,24},{10,26},{12,28},{14,30},{16,0},... | collective-permute-start | bytes 393224 | tf_op jit(solution)/shard_map/ppermute | solution.py:414
  94.5 0.1 fusion.4
  94.6 0.8 collective-permute-start.23
  95.3 0.7 collective-permute-start.24
  96.0 11.5 %collective-permute-done.15 = bf16[512,128]{1,0:T(8,128)(2,1)S(1)} collective-permute-done((bf16[512,128]{1,0:T(8,128)(2,1)S(1)}, bf16[512,128]{1,0:T(8,128)(2,1)S(1)}, u32[]{:S(2)}, u32[]{:S(2)}) %collective-permute-start.15) | collective-permute-done | bytes 131104 | tf_op jit(solution)/shard_map/ppermute | solution.py:414
  107.6 0.1 collective-permute-start.16
  107.6 2.8 %collective-permute-done.23 = bf16[256,256]{1,0:T(8,128)(2,1)S(1)} collective-permute-done((bf16[256,256]{1,0:T(8,128)(2,1)S(1)}, bf16[256,256]{1,0:T(8,128)(2,1)S(1)}, u32[]{:S(2)}, u32[]{:S(2)}) %collective-permute-start.23) | collective-permute-done | bytes 131104 | tf_op jit(solution)/shard_map/ppermute | solution.py:472
  110.4 0.7 add_convert_fusion
  111.1 2.9 %collective-permute-done.16.stride_b_ref = bf16[256,128]{1,0:T(8,128)(2,1)S(1)} collective-permute-done((bf16[256,128]{1,0:T(8,128)(2,1)S(1)}, bf16[256,128]{1,0:T(8,128)(2,1)S(1)}, u32[]{:S(2)}, u32[]{:S(2)}) %collective-permute-start.16) | collective-permute-done | bytes 65568 | tf_op jit(solution)/shard_map/ppermute | solution.py:414
  114.0 1.4 %finish.1 = (bf16[512,128]{1,0:T(8,128)(2,1)}, bf16[512,128]{1,0:T(8,128)(2,1)}) custom-call(s32[2]{0:T(128)S(1)} %copy-done.10, bf16[1024,128]{1,0:T(8,128)(2,1)S(1)} %get-tuple-element.38.own_ref, bf16[1024,128]{1,0:T(8,128)(2,1)S(1)} %collective-permute-done.11.core_ref, bf16[1024,128]{1,0:T(8,128)(2,1)S(1)} %collective-permute-done.12.two_ref, ...), custom_call_target="tpu_custom_call" | custom-call | bytes 1245192 | tf_op jit(solution)/shard_map/finish/pallas_call | solution.py:36
  (62 shorter events, 0.4 us)
Async XLA Ops:
  0.6 0.9 copy-start.5
  1.5 0.9 copy-start.6
  2.4 0.7 copy-start.9
  3.1 29.7 %copy-start.13 = (bf16[512,256]{1,0:T(8,128)(2,1)S(1)}, bf16[512,256]{1,0:T(8,128)(2,1)}, u32[]{:S(2)}) copy-start(bf16[512,256]{1,0:T(8,128)(2,1)} %q_ref.7) | copy-start | bytes 786436
  4.3 5.3 %collective-permute-start = (bf16[256,128]{1,0:T(8,128)(2,1)S(1)}, bf16[256,128]{1,0:T(8,128)(2,1)S(1)}, u32[]{:S(2)}, u32[]{:S(2)}) collective-permute-start(bf16[256,128]{1,0:T(8,128)(2,1)S(1)} %get-tuple-element.27), channel_id=1, source_target_pairs={{0,8},{2,10},{4,12},{6,14},{8,0},{10,2},{12,4},{14,6},{16,24},{18,... | collective-permute-start | bytes 196616 | tf_op jit(solution)/shard_map/ppermute | solution.py:366
  9.6 9.9 %collective-permute-start.1 = (bf16[512,128]{1,0:T(8,128)(2,1)S(1)}, bf16[512,128]{1,0:T(8,128)(2,1)S(1)}, u32[]{:S(2)}, u32[]{:S(2)}) collective-permute-start(bf16[512,128]{1,0:T(8,128)(2,1)S(1)} %pad_maximum_fusion.1), channel_id=1, source_target_pairs={{0,16},{2,18},{4,20},{6,22},{8,24},{10,26},{12,28},{14,30},{16,0},... | collective-permute-start | bytes 393224 | tf_op jit(solution)/shard_map/ppermute | solution.py:366
  12.7 17.7 %collective-permute-start.5 = (bf16[1024,128]{1,0:T(8,128)(2,1)}, bf16[1024,128]{1,0:T(8,128)(2,1)}, u32[]{:S(2)}, u32[]{:S(2)}) collective-permute-start(bf16[1024,128]{1,0:T(8,128)(2,1)} %get-tuple-element.28.own_ref), channel_id=1, source_target_pairs={{0,4},{2,6},{4,8},{6,10},{8,12},{10,14},{12,16},{14,18},{16,20},{1... | collective-permute-start | bytes 786440 | tf_op jit(solution)/shard_map/ppermute | solution.py:357
  17.9 18.7 %copy-start.10 = (s32[2]{0:T(128)S(1)}, s32[2]{0:T(128)}, u32[]{:S(2)}) copy-start(s32[2]{0:T(128)} %phase_ref.7) | copy-start | bytes 28
  17.9 18.7 %copy-start.14 = (bf16[512,256]{1,0:T(8,128)(2,1)S(1)}, bf16[512,256]{1,0:T(8,128)(2,1)}, u32[]{:S(2)}) copy-start(bf16[512,256]{1,0:T(8,128)(2,1)} %q_ref.7) | copy-start | bytes 786436
  17.9 12.0 %collective-permute-start.8 = (bf16[256,1024]{1,0:T(8,128)(2,1)S(1)}, bf16[256,1024]{1,0:T(8,128)(2,1)S(1)}, u32[]{:S(2)}, u32[]{:S(2)}) collective-permute-start(bf16[256,1024]{1,0:T(8,128)(2,1)S(1)} %constant_dynamic-slice_fusion), channel_id=1, source_target_pairs={{0,1},{1,0},{2,3},{3,2},{4,5},{5,4},{6,7},{7,6},{8,9},{9,8},{10,11... | collective-permute-start | bytes 1572872 | tf_op jit(solution)/shard_map/ppermute | solution.py:352
  19.5 6.6 %collective-permute-start.2 = (bf16[1024,128]{1,0:T(8,128)(2,1)S(1)}, bf16[1024,128]{1,0:T(8,128)(2,1)S(1)}, u32[]{:S(2)}, u32[]{:S(2)}) collective-permute-start(bf16[1024,128]{1,0:T(8,128)(2,1)S(1)} %pad_maximum_fusion), channel_id=1, source_target_pairs={{0,4},{2,6},{4,0},{6,2},{8,12},{10,14},{12,8},{14,10},{16,20},{18,... | collective-permute-start | bytes 786440 | tf_op jit(solution)/shard_map/ppermute | solution.py:366
  26.1 14.0 %copy-start.7 = (bf16[2048,128]{1,0:T(8,128)(2,1)}, bf16[2048,128]{1,0:T(8,128)(2,1)S(1)}, u32[]{:S(2)}) copy-start(bf16[2048,128]{1,0:T(8,128)(2,1)S(1)} %constant_dynamic-update-slice_fusion.mine_ref) | copy-start | bytes 1572868
  26.1 15.6 %copy-start = (bf16[512,2048]{1,0:T(8,128)(2,1)S(1)}, bf16[512,2048]{1,0:T(8,128)(2,1)}, u32[]{:S(2)}) copy-start(bf16[512,2048]{1,0:T(8,128)(2,1)} %g_ref.7) | copy-start | bytes 6291460
  26.2 10.4 %collective-permute-start.3 = (bf16[2048,128]{1,0:T(8,128)(2,1)S(1)}, bf16[2048,128]{1,0:T(8,128)(2,1)S(1)}, u32[]{:S(2)}, u32[]{:S(2)}) collective-permute-start(bf16[2048,128]{1,0:T(8,128)(2,1)S(1)} %constant_dynamic-update-slice_fusion.mine_ref), channel_id=1, source_target_pairs={{0,2},{2,0},{4,6},{6,4},{8,10},{10,8},{12,14},{14,12},{16,18},{18,... | collective-permute-start | bytes 1572872 | tf_op jit(solution)/shard_map/ppermute | solution.py:367
  30.0 11.8 %collective-permute-start.9 = (bf16[256,1024]{1,0:T(8,128)(2,1)S(1)}, bf16[256,1024]{1,0:T(8,128)(2,1)S(1)}, u32[]{:S(2)}, u32[]{:S(2)}) collective-permute-start(bf16[256,1024]{1,0:T(8,128)(2,1)S(1)} %collective-permute-done.8.near_ref), channel_id=1, source_target_pairs={{0,2},{2,0},{4,6},{6,4},{8,10},{10,8},{12,14},{14,12},{16,18},{18,... | collective-permute-start | bytes 1572872 | tf_op jit(solution)/shard_map/ppermute | solution.py:353
  30.0 2.2 %collective-permute-start.4 = (bf16[1024,128]{1,0:T(8,128)(2,1)}, bf16[1024,128]{1,0:T(8,128)(2,1)S(1)}, u32[]{:S(2)}, u32[]{:S(2)}) collective-permute-start(bf16[1024,128]{1,0:T(8,128)(2,1)} %get-tuple-element.28.own_ref), channel_id=1, source_target_pairs={{0,2},{2,0},{4,6},{6,4},{8,10},{10,8},{12,14},{14,12},{16,18},{18,... | collective-permute-start | bytes 786440 | tf_op jit(solution)/shard_map/ppermute | solution.py:356
  30.5 2.4 %collective-permute-start.6 = (bf16[1024,128]{1,0:T(8,128)(2,1)}, bf16[1024,128]{1,0:T(8,128)(2,1)S(1)}, u32[]{:S(2)}, u32[]{:S(2)}) collective-permute-start(bf16[1024,128]{1,0:T(8,128)(2,1)} %collective-permute-done.5.two_ref), channel_id=1, source_target_pairs={{0,2},{2,0},{4,6},{6,4},{8,10},{10,8},{12,14},{14,12},{16,18},{18,... | collective-permute-start | bytes 786440 | tf_op jit(solution)/shard_map/ppermute | solution.py:358
  32.1 4.5 %copy-start.16 = (bf16[1024,128]{1,0:T(8,128)(2,1)}, bf16[1024,128]{1,0:T(8,128)(2,1)S(1)}, u32[]{:S(2)}) copy-start(bf16[1024,128]{1,0:T(8,128)(2,1)S(1)} %collective-permute-done.4.core_ref) | copy-start | bytes 786436
  32.8 3.8 %copy-start.18 = (bf16[1024,128]{1,0:T(8,128)(2,1)}, bf16[1024,128]{1,0:T(8,128)(2,1)S(1)}, u32[]{:S(2)}) copy-start(bf16[1024,128]{1,0:T(8,128)(2,1)S(1)} %collective-permute-done.6.two_core_ref) | copy-start | bytes 786436
  36.6 3.6 %copy-start.11 = (bf16[2048,128]{1,0:T(8,128)(2,1)}, bf16[2048,128]{1,0:T(8,128)(2,1)S(1)}, u32[]{:S(2)}) copy-start(bf16[2048,128]{1,0:T(8,128)(2,1)S(1)} %collective-permute-done.3.other_ref) | copy-start | bytes 1572868
  40.2 9.3 %collective-permute-start.7 = (bf16[512,256]{1,0:T(8,128)(2,1)S(1)}, bf16[512,256]{1,0:T(8,128)(2,1)}, u32[]{:S(2)}, u32[]{:S(2)}) collective-permute-start(bf16[512,256]{1,0:T(8,128)(2,1)S(1)} %get-tuple-element.32.own_ref.att_ref), channel_id=1, source_target_pairs={{0,1},{1,0},{2,3},{3,2},{4,5},{5,4},{6,7},{7,6},{8,9},{9,8},{10,11... | collective-permute-start | bytes 786440 | tf_op jit(solution)/shard_map/ppermute | solution.py:402
  43.2 11.7 %collective-permute-start.10 = (bf16[512,256]{1,0:T(8,128)(2,1)}, bf16[512,256]{1,0:T(8,128)(2,1)}, u32[]{:S(2)}, u32[]{:S(2)}) collective-permute-start(bf16[512,256]{1,0:T(8,128)(2,1)} %grad_other.1), channel_id=1, source_target_pairs={{0,1},{1,0},{2,3},{3,2},{4,5},{5,4},{6,7},{7,6},{8,9},{9,8},{10,11... | collective-permute-start | bytes 786440 | tf_op jit(solution)/shard_map/ppermute | solution.py:385
  45.3 0.8 copy-start.3
  46.1 19.7 %collective-permute-start.20 = (bf16[4,256,256]{2,1,0:T(8,128)(2,1)}, bf16[4,256,256]{2,1,0:T(8,128)(2,1)}, u32[]{:S(2)}, u32[]{:S(2)}) collective-permute-start(bf16[4,256,256]{2,1,0:T(8,128)(2,1)} %get-tuple-element.48), channel_id=1, source_target_pairs={{0,2},{2,0},{4,6},{6,4},{8,10},{10,8},{12,14},{14,12},{16,18},{18,... | collective-permute-start | bytes 1572872 | tf_op jit(solution)/shard_map/ppermute | solution.py:454
  46.1 1.6 %copy-start.1 = (bf16[256,4096]{1,0:T(8,128)(2,1)S(1)}, bf16[256,4096]{1,0:T(8,128)(2,1)}, u32[]{:S(2)}) copy-start(bf16[256,4096]{1,0:T(8,128)(2,1)} %w_ref.3) | copy-start | bytes 6291460
  48.4 2.9 %copy-start.2 = (bf16[256,4096]{1,0:T(8,128)(2,1)S(1)}, bf16[256,4096]{1,0:T(8,128)(2,1)}, u32[]{:S(2)}) copy-start(bf16[256,4096]{1,0:T(8,128)(2,1)} %w_ref.3) | copy-start | bytes 6291460
  51.2 3.7 %copy-start.8 = (bf16[2048,128]{1,0:T(8,128)(2,1)S(1)}, bf16[2048,128]{1,0:T(8,128)(2,1)}, u32[]{:S(2)}) copy-start(bf16[2048,128]{1,0:T(8,128)(2,1)} %copy-done.7) | copy-start | bytes 1572868
  51.2 3.7 %copy-start.12 = (bf16[2048,128]{1,0:T(8,128)(2,1)S(1)}, bf16[2048,128]{1,0:T(8,128)(2,1)}, u32[]{:S(2)}) copy-start(bf16[2048,128]{1,0:T(8,128)(2,1)} %copy-done.11) | copy-start | bytes 1572868
  51.2 3.7 %copy-start.15 = (bf16[512,256]{1,0:T(8,128)(2,1)S(1)}, bf16[512,256]{1,0:T(8,128)(2,1)}, u32[]{:S(2)}) copy-start(bf16[512,256]{1,0:T(8,128)(2,1)} %q_ref.7) | copy-start | bytes 786436
  51.2 18.0 %collective-permute-start.17 = (bf16[4,256,256]{2,1,0:T(8,128)(2,1)S(1)}, bf16[4,256,256]{2,1,0:T(8,128)(2,1)S(1)}, u32[]{:S(2)}, u32[]{:S(2)}) collective-permute-start(bf16[4,256,256]{2,1,0:T(8,128)(2,1)S(1)} %get-tuple-element.46), channel_id=1, source_target_pairs={{0,2},{2,0},{4,6},{6,4},{8,10},{10,8},{12,14},{14,12},{16,18},{18,... | collective-permute-start | bytes 1572872 | tf_op jit(solution)/shard_map/ppermute | solution.py:454
  55.0 5.3 %copy-start.17 = (bf16[1024,128]{1,0:T(8,128)(2,1)S(1)}, bf16[1024,128]{1,0:T(8,128)(2,1)}, u32[]{:S(2)}) copy-start(bf16[1024,128]{1,0:T(8,128)(2,1)} %copy-done.16) | copy-start | bytes 786436
  55.0 5.3 %copy-start.19 = (bf16[1024,128]{1,0:T(8,128)(2,1)S(1)}, bf16[1024,128]{1,0:T(8,128)(2,1)}, u32[]{:S(2)}) copy-start(bf16[1024,128]{1,0:T(8,128)(2,1)} %copy-done.18) | copy-start | bytes 786436
  60.3 5.5 %copy-start.4 = (bf16[4,256,256]{2,1,0:T(8,128)(2,1)S(1)}, bf16[4,256,256]{2,1,0:T(8,128)(2,1)}, u32[]{:S(2)}) copy-start(bf16[4,256,256]{2,1,0:T(8,128)(2,1)} %copy-done.3) | copy-start | bytes 1572868
  65.2 2.6 %collective-permute-start.11 = (bf16[1024,128]{1,0:T(8,128)(2,1)S(1)}, bf16[1024,128]{1,0:T(8,128)(2,1)S(1)}, u32[]{:S(2)}, u32[]{:S(2)}) collective-permute-start(bf16[1024,128]{1,0:T(8,128)(2,1)S(1)} %get-tuple-element.39), channel_id=1, source_target_pairs={{0,2},{2,0},{4,6},{6,4},{8,10},{10,8},{12,14},{14,12},{16,18},{18,... | collective-permute-start | bytes 786440 | tf_op jit(solution)/shard_map/ppermute | solution.py:431
  65.6 6.5 %collective-permute-start.13 = (bf16[2048,128]{1,0:T(8,128)(2,1)S(1)}, bf16[2048,128]{1,0:T(8,128)(2,1)S(1)}, u32[]{:S(2)}, u32[]{:S(2)}) collective-permute-start(bf16[2048,128]{1,0:T(8,128)(2,1)S(1)} %get-tuple-element.42), channel_id=1, source_target_pairs={{0,2},{2,0},{4,6},{6,4},{8,10},{10,8},{12,14},{14,12},{16,18},{18,... | collective-permute-start | bytes 1572872 | tf_op jit(solution)/shard_map/ppermute | solution.py:414
  66.9 13.2 %collective-permute-start.21 = (bf16[2,256,256]{2,1,0:T(8,128)(2,1)S(1)}, bf16[2,256,256]{2,1,0:T(8,128)(2,1)S(1)}, u32[]{:S(2)}, u32[]{:S(2)}) collective-permute-start(bf16[2,256,256]{2,1,0:T(8,128)(2,1)S(1)} %slice.102), channel_id=1, source_target_pairs={{0,4},{2,6},{4,0},{6,2},{8,12},{10,14},{12,8},{14,10},{16,20},{18,... | collective-permute-start | bytes 786440 | tf_op jit(solution)/shard_map/ppermute | solution.py:454
  68.0 43.1 %collective-permute-start.12 = (bf16[1024,128]{1,0:T(8,128)(2,1)S(1)}, bf16[1024,128]{1,0:T(8,128)(2,1)S(1)}, u32[]{:S(2)}, u32[]{:S(2)}) collective-permute-start(bf16[1024,128]{1,0:T(8,128)(2,1)S(1)} %fusion), channel_id=1, source_target_pairs={{4,0},{6,2},{8,4},{10,6},{12,8},{14,10},{16,12},{18,14},{20,16},{2... | collective-permute-start | bytes 786440 | tf_op jit(solution)/shard_map/ppermute | solution.py:433
  69.4 17.9 %collective-permute-start.18 = (bf16[2,256,256]{2,1,0:T(8,128)(2,1)S(1)}, bf16[2,256,256]{2,1,0:T(8,128)(2,1)S(1)}, u32[]{:S(2)}, u32[]{:S(2)}) collective-permute-start(bf16[2,256,256]{2,1,0:T(8,128)(2,1)S(1)} %slice.103), channel_id=1, source_target_pairs={{0,4},{2,6},{4,0},{6,2},{8,12},{10,14},{12,8},{14,10},{16,20},{18,... | collective-permute-start | bytes 786440 | tf_op jit(solution)/shard_map/ppermute | solution.py:454
  72.3 20.2 %collective-permute-start.14 = (bf16[1024,128]{1,0:T(8,128)(2,1)S(1)}, bf16[1024,128]{1,0:T(8,128)(2,1)S(1)}, u32[]{:S(2)}, u32[]{:S(2)}) collective-permute-start(bf16[1024,128]{1,0:T(8,128)(2,1)S(1)} %slice.104), channel_id=1, source_target_pairs={{0,4},{2,6},{4,0},{6,2},{8,12},{10,14},{12,8},{14,10},{16,20},{18,... | collective-permute-start | bytes 786440 | tf_op jit(solution)/shard_map/ppermute | solution.py:414
  80.2 14.3 %collective-permute-start.22 = (bf16[1,256,256]{2,1,0:T(8,128)(2,1)S(1)}, bf16[1,256,256]{2,1,0:T(8,128)(2,1)S(1)}, u32[]{:S(2)}, u32[]{:S(2)}) collective-permute-start(bf16[1,256,256]{2,1,0:T(8,128)(2,1)S(1)} %slice.105), channel_id=1, source_target_pairs={{0,8},{2,10},{4,12},{6,14},{8,0},{10,2},{12,4},{14,6},{16,24},{18,... | collective-permute-start | bytes 393224 | tf_op jit(solution)/shard_map/ppermute | solution.py:454
  87.4 7.1 %collective-permute-start.19 = (bf16[1,256,256]{2,1,0:T(8,128)(2,1)S(1)}, bf16[1,256,256]{2,1,0:T(8,128)(2,1)S(1)}, u32[]{:S(2)}, u32[]{:S(2)}) collective-permute-start(bf16[1,256,256]{2,1,0:T(8,128)(2,1)S(1)} %slice.106), channel_id=1, source_target_pairs={{0,8},{2,10},{4,12},{6,14},{8,0},{10,2},{12,4},{14,6},{16,24},{18,... | collective-permute-start | bytes 393224 | tf_op jit(solution)/shard_map/ppermute | solution.py:454
  92.6 14.9 %collective-permute-start.15 = (bf16[512,128]{1,0:T(8,128)(2,1)S(1)}, bf16[512,128]{1,0:T(8,128)(2,1)S(1)}, u32[]{:S(2)}, u32[]{:S(2)}) collective-permute-start(bf16[512,128]{1,0:T(8,128)(2,1)S(1)} %slice.107), channel_id=1, source_target_pairs={{0,16},{2,18},{4,20},{6,22},{8,24},{10,26},{12,28},{14,30},{16,0},... | collective-permute-start | bytes 393224 | tf_op jit(solution)/shard_map/ppermute | solution.py:414
  94.6 15.8 %collective-permute-start.23 = (bf16[256,256]{1,0:T(8,128)(2,1)S(1)}, bf16[256,256]{1,0:T(8,128)(2,1)S(1)}, u32[]{:S(2)}, u32[]{:S(2)}) collective-permute-start(bf16[256,256]{1,0:T(8,128)(2,1)S(1)} %get-tuple-element.49), channel_id=1, source_target_pairs={{0,1},{1,17},{2,3},{3,19},{4,5},{5,21},{6,7},{7,23},{8,9},{9,25},{... | collective-permute-start | bytes 393224 | tf_op jit(solution)/shard_map/ppermute | solution.py:472
  95.3 15.1 %collective-permute-start.24 = (bf16[256,256]{1,0:T(8,128)(2,1)S(1)}, bf16[256,256]{1,0:T(8,128)(2,1)S(1)}, u32[]{:S(2)}, u32[]{:S(2)}) collective-permute-start(bf16[256,256]{1,0:T(8,128)(2,1)S(1)} %get-tuple-element.50), channel_id=1, source_target_pairs={{1,16},{3,18},{5,20},{7,22},{9,24},{11,26},{13,28},{15,30},{16,1},... | collective-permute-start | bytes 393224 | tf_op jit(solution)/shard_map/ppermute | solution.py:473
  107.6 6.5 %collective-permute-start.16 = (bf16[256,128]{1,0:T(8,128)(2,1)S(1)}, bf16[256,128]{1,0:T(8,128)(2,1)S(1)}, u32[]{:S(2)}, u32[]{:S(2)}) collective-permute-start(bf16[256,128]{1,0:T(8,128)(2,1)S(1)} %slice.108), channel_id=1, source_target_pairs={{0,8},{2,10},{4,12},{6,14},{8,0},{10,2},{12,4},{14,6},{16,24},{18,... | collective-permute-start | bytes 196616 | tf_op jit(solution)/shard_map/ppermute | solution.py:414

commit v2 on v1

--- a/solution.py
+++ b/solution.py
@@ -20,6 +20,8 @@
 MASKED = -1e30
 
 VMEM = pl.BlockSpec(memory_space=pltpu.VMEM)
+ANY = pl.BlockSpec(memory_space=pl.ANY)
+HBM = pl.BlockSpec(memory_space=pltpu.HBM)
 SMEM = pl.BlockSpec(memory_space=pltpu.SMEM)
 NN = (((1,), (0,)), ((), ()))
 NT = (((1,), (1,)), ((), ()))
@@ -30,19 +32,59 @@
     return lax.dot_general(left, right, dims, preferred_element_type=F32)
 
 
-def call(kernel, name, ins, out_shapes, scratch=(), mib=32, flops=0):
-    nbytes = sum(a.size * a.dtype.itemsize for a in ins)
-    nbytes += sum(math.prod(s.shape) * s.dtype.itemsize for s in out_shapes)
-    return pl.pallas_call(
-        kernel,
-        name=name,
-        out_shape=out_shapes,
-        in_specs=[SMEM if a.dtype == jnp.int32 else VMEM for a in ins],
-        out_specs=[VMEM] * len(out_shapes),
-        scratch_shapes=list(scratch),
-        compiler_params=pltpu.CompilerParams(vmem_limit_bytes=mib * 2**20),
-        cost_estimate=pl.CostEstimate(flops=flops, bytes_accessed=nbytes, transcendentals=0),
-    )(*ins)
+USEC = {'pack': 2, 'grad_own': 2, 'grad_other': 0.1, 'band_forward': 0.1, 'stride_forward': 36, 'stride_backward': 46, 'band_backward': 40, 'layer_out': 26, 'finish': 15, 'last_sum': 7, 'weight_grad_own': 8, 'weight_grad_other': 8}
+
+
+class Sequence:
+    def __init__(self):
+        self.last = []
+
+    def __call__(self, kernel, name, ins, out_shapes, scratch=(), mib=32, flops=0, after=(), far=(), out_space=VMEM):
+        extra = self.last + list(after)
+        count = len(ins)
+
+        def wrapped(*refs):
+            rest = refs[count + len(extra) :]
+            kernel(*refs[:count], *rest[: len(out_shapes)], *rest[len(out_shapes) + 1 :])
+            token = rest[len(out_shapes)]
+            token[...] = jnp.zeros_like(token)
+
+        specs = [SMEM if a.dtype == jnp.int32 else VMEM for a in ins]
+        for index in far:
+            specs[index] = HBM
+        outs = pl.pallas_call(
+            wrapped,
+            name=name,
+            out_shape=list(out_shapes) + [shape((8, 128), F32)],
+            in_specs=specs + [ANY] * len(extra),
+            out_specs=[out_space] * len(out_shapes) + [VMEM],
+            scratch_shapes=list(scratch),
+            compiler_params=pltpu.CompilerParams(vmem_limit_bytes=mib * 2**20),
+            cost_estimate=pl.CostEstimate(flops=int(1e9 * USEC.get(name, 0.1)), bytes_accessed=1, transcendentals=0),
+        )(*ins, *extra)
+        self.last = [outs[-1]]
+        return outs[:-1]
+
+
+    def hold(self, array, after=()):
+        extra = self.last + list(after)
+
+        def kernel(*refs):
+            token = refs[-1]
+            token[...] = jnp.zeros_like(token)
+
+        held, token = pl.pallas_call(
+            kernel,
+            name="hold",
+            out_shape=[shape(array.shape, array.dtype), shape((8, 128), F32)],
+            in_specs=[ANY] * (1 + len(extra)),
+            out_specs=[ANY, VMEM],
+            input_output_aliases={0: 0},
+            compiler_params=pltpu.CompilerParams(vmem_limit_bytes=2**20),
+            cost_estimate=pl.CostEstimate(flops=1, bytes_accessed=1, transcendentals=0),
+        )(array, *extra)
+        self.last = [token]
+        return held
 
 
 def shape(dims, dtype):
@@ -61,15 +103,52 @@
     return ctx ^ mask
 
 
-def pack_kernel(phase_ref, k_ref, v_ref, kv_ref, pick_ref):
+def run_copies(pairs, sem):
+    copies = [pltpu.make_async_copy(src, dst, sem.at[i]) for i, (src, dst) in enumerate(pairs)]
+    for copy in copies:
+        copy.start()
+    return copies
+
+
+def pack_kernel(phase_ref, k_ref, v_ref, *refs):
+    if len(refs) == 5:
+        kv_ref, pick_ref, kv_buf, in_sem, out_sem = refs
+        inward = []
+    else:
+        w_ref, kv_ref, pick_ref, piece_ref, kv_buf, piece_buf, in_sem, out_sem = refs
+        cols = piece_ref.shape[1]
+        start = (1 - lax.axis_index("head")) * 2 * cols + lax.axis_index("ctx") % 2 * cols
+        inward = [(w_ref.at[:, pl.ds(pl.multiple_of(start, cols), cols)], piece_buf)]
     rows = k_ref.shape[0]
-    kv_ref[:rows] = k_ref[...]
-    kv_ref[rows:] = v_ref[...]
+    inward = [(k_ref, kv_buf.at[pl.ds(0, rows)]), (v_ref, kv_buf.at[pl.ds(rows, rows)])] + inward
+    outward = []
     for r in range(2):
-        start = pl.multiple_of((STRIDE - 1 - phase_ref[r]) * BLOCK_TOKENS, BLOCK_TOKENS)
-        at = 2 * r * BLOCK_TOKENS
-        pick_ref[at : at + BLOCK_TOKENS] = k_ref[pl.ds(start, BLOCK_TOKENS)]
-        pick_ref[at + BLOCK_TOKENS : at + 2 * BLOCK_TOKENS] = v_ref[pl.ds(start, BLOCK_TOKENS)]
+        for part in range(2):
+            start = pl.multiple_of(part * rows + (STRIDE - 1 - phase_ref[r]) * BLOCK_TOKENS, BLOCK_TOKENS)
+            at = (2 * r + part) * BLOCK_TOKENS
+            outward.append((kv_buf.at[pl.ds(start, BLOCK_TOKENS)], pick_ref.at[pl.ds(at, BLOCK_TOKENS)]))
+    outward.append((kv_buf, kv_ref))
+    coming = run_copies(inward, in_sem)
+    coming[0].wait()
+    coming[1].wait()
+    going = run_copies(outward, out_sem)
+    for copy in coming[2:]:
+        copy.wait()
+        last = pltpu.make_async_copy(piece_buf, piece_ref, out_sem.at[len(outward)])
+        last.start()
+        going.append(last)
+    for copy in going:
+        copy.wait()
+
+
+def join_kernel(first_ref, second_ref, out_ref):
+    middle = first_ref.shape[0]
+    out_ref[:middle] = first_ref[...]
+    out_ref[middle:] = second_ref[...]
+
+
+def join(run, name, first, second, after=()):
+    return run(join_kernel, name, [first, second], [shape((2 * first.shape[0],) + first.shape[1:], BF16)], after=after)[0]
 
 
 def load_window(core, own_ref, core_ref, two_ref, two_core_ref, part, out):
@@ -275,10 +354,24 @@
     dv_ref[...] = acc[rows:].astype(BF16)
 
 
-def grad_own_kernel(g_ref, w_ref, out_ref):
+def grad_own_kernel(g_ref, w_ref, out_ref, g_out, w_own, sem):
     width = g_ref.shape[1]
-    start = pl.multiple_of(lax.axis_index("head") * width, width)
-    out_ref[...] = mm(g_ref[...], w_ref[:, pl.ds(start, width)], NT)
+    start = lax.axis_index("head") * width
+    step = width // 4
+    pairs = []
+    for at in range(0, width, step):
+        cols = pl.ds(at, step)
+        pairs.append((g_ref.at[:, cols], g_out.at[:, cols]))
+        pairs.append((w_ref.at[:, pl.ds(pl.multiple_of(start + at, step), step)], w_own.at[:, cols]))
+    copies = run_copies(pairs, sem)
+    total = None
+    for index in range(4):
+        copies[2 * index].wait()
+        copies[2 * index + 1].wait()
+        cols = slice(index * step, (index + 1) * step)
+        term = mm(g_out[:, cols], w_own[:, cols], NT)
+        total = term if total is None else total + term
+    out_ref[...] = total
 
 
 def grad_other_kernel(g_ref, near_ref, far_ref, out_ref):
@@ -293,14 +386,12 @@
 def layer_out_kernel(own_ref, other_ref, w_ref, near_ref, far_ref, out_ref):
     core = lax.axis_index("ctx") % 2
     width = near_ref.shape[1]
-    base = lax.axis_index("head") * 2 * width
-    step = 256
+    step = min(width, 256)
     for part, source in ((core, near_ref), (1 - core, far_ref)):
         for at in range(0, width, step):
-            start = part * width + at
-            w_own = w_ref[:, pl.ds(pl.multiple_of(base + start, step), step)]
-            total = mm(own_ref[...], w_own) + mm(other_ref[...], source[:, at : at + step])
-            out_ref[:, pl.ds(pl.multiple_of(start, step), step)] = total.astype(BF16)
+            cols = pl.ds(pl.multiple_of(part * width + at, step), step)
+            total = mm(own_ref[...], w_ref[:, cols]) + mm(other_ref[...], source[:, at : at + step])
+            out_ref[:, cols] = total.astype(BF16)
 
 
 def weight_grad_kernel(bits, att_ref, g_ref, keep_ref, send_ref):
@@ -321,87 +412,145 @@
             send_ref[slot - blocks // 2] = term
 
 
-def add(left, right):
-    return left.astype(F32) + right.astype(F32)
+def halve_kernel(keep_ref, got_ref, keep_out, send_out):
+    middle = keep_out.shape[0]
+    keep_out[...] = keep_ref[:middle].astype(F32) + got_ref[:middle].astype(F32)
+    send_out[...] = (keep_ref[middle:].astype(F32) + got_ref[middle:].astype(F32)).astype(BF16)
+
+
+def halve(run, name, keep, got, after=()):
+    half = (keep.shape[0] // 2,) + keep.shape[1:]
+    return run(halve_kernel, name, [keep, got], [shape(half, F32), shape(half, BF16)], after=after)
+
+
+def add_kernel(core, left_ref, right_ref, out_ref):
+    here = lax.axis_index("ctx") % 2 == core
+    left = left_ref[...].astype(F32)
+    out_ref[...] = jnp.where(here, left + right_ref[...].astype(F32), left).astype(BF16)
+
+
+def end_kernel(left_ref, right_ref, low_ref):
+    low_ref[...] = (left_ref[0].astype(F32) + right_ref[0].astype(F32)).astype(BF16)
+
+
+def choose_kernel(own_ref, own_got_ref, other_ref, keep_ref, send_ref):
+    same = lax.axis_index("ctx") // (lax.axis_size("ctx") // 2) == lax.axis_index("head")
+    own = own_ref[0].astype(F32) + own_got_ref[0].astype(F32)
+    other = other_ref[...].astype(F32)
+    keep_ref[...] = jnp.where(same, own, other)
+    send_ref[...] = jnp.where(same, other, own).astype(BF16)
+
+
+def last_sum_kernel(keep_ref, got_ref, out_ref):
+    out_ref[...] = (keep_ref[...] + got_ref[...].astype(F32)).astype(BF16)
 
 
 def body(queries, rotated_key_rows, value_head_rows, stride_offset, w_out, grad_out):
     rows = queries.shape[0]
     n_ctx = lax.axis_size("ctx")
     n_head = lax.axis_size("head")
-    ctx = lax.axis_index("ctx")
-    head = lax.axis_index("head")
-    core = ctx % 2
     model = w_out.shape[1]
     width = grad_out.shape[1]
     head_rows = w_out.shape[0]
     ratio = n_ctx // n_head
     cols = model // n_ctx
+    pair = n_head == 2
     flip = functools.partial(flips, n_ctx)
     swap = [(0, 1), (1, 0)]
     scores = rows * 2 * HEAD_SIZE * 2
     proj = 2 * rows * head_rows * width
-
-    kv, picks = call(
-        pack_kernel, "pack", [stride_offset, rotated_key_rows, value_head_rows],
-        [shape((2 * rows, HEAD_SIZE), BF16), shape((4 * BLOCK_TOKENS, HEAD_SIZE), BF16)],
-    )
-    if n_head == 2:
-        half = width // 2
-        piece = lax.dynamic_slice(w_out, (0, (1 - head) * width + core * half), (head_rows, half))
-        w_near = lax.ppermute(piece, "head", swap)
-        w_far = lax.ppermute(w_near, "ctx", flip(1))
+    run = Sequence()
+
+    packed = run(
+        pack_kernel, "pack",
+        [stride_offset, rotated_key_rows, value_head_rows] + ([w_out] if pair else []),
+        [shape((2 * rows, HEAD_SIZE), BF16), shape((4 * BLOCK_TOKENS, HEAD_SIZE), BF16)]
+        + ([shape((head_rows, width // 2), BF16)] if pair else []),
+        [pltpu.VMEM((2 * rows, HEAD_SIZE), BF16)]
+        + ([pltpu.VMEM((head_rows, width // 2), BF16)] if pair else [])
+        + [pltpu.SemaphoreType.DMA((3,)), pltpu.SemaphoreType.DMA((6,))],
+        far=(1, 2, 3) if pair else (1, 2), mib=60, out_space=HBM,
+    )
+    run.last = []
+    kv, picks = packed[:2]
+    if pair:
+        w_near = lax.ppermute(packed[2], "head", swap)
     else:
         w_all = lax.all_to_all(w_out, "head", 1, 0, tiled=True)
-    kv_core = lax.ppermute(kv, "ctx", flip(1))
-    kv_two = lax.ppermute(kv, "ctx", [(i, i + 2) for i in range(n_ctx - 2)])
-    kv_two_core = lax.ppermute(kv_two, "ctx", flip(1))
     order = []
     bit = 4
     while bit < n_ctx:
         order.append(bit)
         bit *= 2
-    order += [2, 1]
-    for bit in order[:-1]:
-        picks = jnp.concatenate([picks, lax.ppermute(picks, "ctx", flip(bit))], axis=0)
-    picks_other = lax.ppermute(picks, "ctx", flip(1))
+    order = tuple(order + [2, 1])
+    picks_got = lax.ppermute(picks, "ctx", flip(order[0]))
+    kv_two = lax.ppermute(kv, "ctx", [(i, i + 2) for i in range(n_ctx - 2)])
+    kv_core = lax.ppermute(kv, "ctx", flip(1))
+    picks = join(run, "stride_join", picks, picks_got)
+    picks_got = lax.ppermute(picks, "ctx", flip(order[1]))
+    if pair:
+        grad_own, grad_out, w_own = run(
+            grad_own_kernel, "grad_own", [grad_out, w_out],
+            [shape((rows, head_rows), F32), shape(grad_out.shape, BF16), shape((head_rows, width), BF16)],
+            [pltpu.SemaphoreType.DMA((8,))], flops=proj, after=[kv_core], far=(0, 1),
+        )
+    for bit in order[2:-1]:
+        picks = join(run, "stride_join", picks, picks_got)
+        picks_got = lax.ppermute(picks, "ctx", flip(bit))
+    kv_two = run.hold(kv_two)
+    kv_two_core = lax.ppermute(kv_two, "ctx", flip(1))
 
     chunk_rows = (2 * (rows // TILE) + 1) * TILE
     window = pltpu.VMEM((3 * rows, HEAD_SIZE), BF16)
-    out, top, total = call(
+    picked_rows = n_ctx * BLOCK_TOKENS
+    pick = pltpu.VMEM((picked_rows, HEAD_SIZE), BF16)
+    out, top, total = run(
         band_forward_kernel, "band_forward", [queries, kv, kv_core, kv_two, kv_two_core],
         [shape((2, HEAD_SIZE, rows), F32), shape((2, rows), F32), shape((2, rows), F32)],
         [window, window, pltpu.VMEM((chunk_rows, 2 * TILE), F32), pltpu.VMEM((chunk_rows, 2 * TILE), BF16)],
         flops=2 * scores * chunk_rows,
     )
-    if n_head == 2:
-        grad_own, = call(
-            grad_own_kernel, "grad_own", [grad_out, w_out], [shape((rows, head_rows), F32)], flops=proj
-        )
-        grad_other, = call(
+    picks = join(run, "stride_join", picks, picks_got)
+    picks_other = lax.ppermute(picks, "ctx", flip(1))
+    if pair:
+        w_near = run.hold(w_near)
+        w_far = lax.ppermute(w_near, "ctx", flip(1))
+        grad_other, = run(
             grad_other_kernel, "grad_other", [grad_out, w_near, w_far],
             [shape((rows, head_rows), BF16)], flops=proj,
         )
         grad_got = lax.ppermute(grad_other, "head", swap)
-    else:
+    if not pair:
         grad_all = mm(grad_out, w_all, NT).astype(BF16)
         grad_all = lax.all_to_all(grad_all.reshape(rows, n_head, head_rows), "head", 1, 0, tiled=True)
         grad_all = grad_all.reshape(n_head, rows, head_rows).astype(F32)
         grad_own = jnp.sum(grad_all, axis=0)
         grad_got = jnp.zeros((rows, head_rows), BF16)
-    picked_rows = n_ctx * BLOCK_TOKENS
-    pick = pltpu.VMEM((picked_rows, HEAD_SIZE), BF16)
-    attended, lse = call(
-        functools.partial(stride_forward_kernel, tuple(order)), "stride_forward",
+    attended, lse = run(
+        functools.partial(stride_forward_kernel, order), "stride_forward",
         [stride_offset, queries, picks, picks_other, out, top, total],
         [shape((rows, head_rows), BF16), shape((2, rows), F32)],
         [pick, pick, pltpu.VMEM((picked_rows, 2 * TILE), F32), pltpu.VMEM((picked_rows, 2 * TILE), BF16)],
         flops=2 * scores * picked_rows,
     )
-    if n_head == 2:
+    if pair:
         att_other = lax.ppermute(attended, "head", swap)
-    grad_att, row_dot, grad_q, stride_keep, stride_send = call(
-        functools.partial(stride_backward_kernel, tuple(order)), "stride_backward",
+        bits = [1]
+        while 2 * bits[-1] < ratio:
+            bits.append(2 * bits[-1])
+        own_bits = tuple(bits[:1] + bits[:0:-1])
+        other_bits = tuple(bits)
+
+        def weight_grad(source, name, bits):
+            part = shape((ratio // 2, head_rows, cols), BF16)
+            return run(
+                functools.partial(weight_grad_kernel, bits), name, [source, grad_out], [part, part], flops=proj
+            )
+
+        own_keep, own_send = weight_grad(attended, "weight_grad_own", own_bits)
+        own_got = lax.ppermute(own_send, "ctx", flip(1))
+    grad_att, row_dot, grad_q, stride_keep, stride_send = run(
+        functools.partial(stride_backward_kernel, order), "stride_backward",
         [stride_offset, queries, grad_own, grad_got, attended, lse, picks, picks_other],
         [
             shape((rows, head_rows), BF16), shape((2, rows), F32), shape((2, HEAD_SIZE, rows), F32),
@@ -410,15 +559,18 @@
         [pick, pick, pltpu.VMEM((picked_rows, rows), BF16), pltpu.VMEM((picked_rows, rows), BF16)],
         flops=5 * scores * picked_rows,
     )
-    for bit in reversed(order):
-        got = lax.ppermute(stride_send, "ctx", flip(bit))
-        if bit != order[0]:
-            both = add(stride_keep, got)
-            middle = both.shape[0] // 2
-            stride_keep, stride_send = both[:middle], both[middle:].astype(BF16)
-    stride_got = got
-
-    grad_queries, own, one, two = call(
+    stride_got = lax.ppermute(stride_send, "ctx", flip(1))
+    if pair:
+        own_keep, own_send = halve(run, "weight_grad_own_core", own_keep, own_got, after=[att_other])
+        own_got = lax.ppermute(own_send, "ctx", flip(own_bits[1]))
+        other_keep, other_send = weight_grad(att_other, "weight_grad_other", other_bits)
+        other_got = lax.ppermute(other_send, "ctx", flip(1))
+    stride_keep, stride_send = halve(run, "stride_core", stride_keep, stride_got)
+    stride_got = lax.ppermute(stride_send, "ctx", flip(2))
+    if pair:
+        other_keep, other_send = halve(run, "weight_grad_other_core", other_keep, other_got)
+        other_got = lax.ppermute(other_send, "ctx", flip(other_bits[1]))
+    grad_queries, own, one, two = run(
         band_backward_kernel, "band_backward",
         [queries, grad_att, kv, kv_core, kv_two, kv_two_core, lse, row_dot, grad_q],
         [shape((rows, head_rows), BF16)] + [shape((2 * rows, HEAD_SIZE), BF16)] * 3,
@@ -429,49 +581,35 @@
         flops=5 * scores * chunk_rows,
     )
     one_got = lax.ppermute(one, "ctx", flip(1))
-    two = jnp.where(core == 1, add(two, one_got), two.astype(F32)).astype(BF16)
+    stride_bits = list(reversed(order))[1:]
+    if pair:
+        for bit in own_bits[2:]:
+            own_keep, own_send = halve(run, "weight_grad_own_low", own_keep, own_got)
+            own_got = lax.ppermute(own_send, "ctx", flip(bit))
+    stride_keep, stride_send = halve(run, "stride_y", stride_keep, stride_got)
+    stride_got = lax.ppermute(stride_send, "ctx", flip(stride_bits[1]))
+    if pair:
+        for bit in other_bits[2:]:
+            other_keep, other_send = halve(run, "weight_grad_other_low", other_keep, other_got)
+            other_got = lax.ppermute(other_send, "ctx", flip(bit))
+    two, = run(functools.partial(add_kernel, 1), "band_two", [two, one_got], [shape(two.shape, BF16)])
     two_got = lax.ppermute(two, "ctx", [(i + 2, i) for i in range(n_ctx - 2)])
-
-    if n_head == 2:
-        layer_out, = call(
-            layer_out_kernel, "layer_out", [attended, att_other, w_out, w_near, w_far],
+    if pair:
+        layer_out, = run(
+            layer_out_kernel, "layer_out", [attended, att_other, w_own, w_near, w_far],
             [shape((rows, width), BF16)], flops=2 * proj,
         )
-        bits = []
-        bit = 1
-        while bit < ratio:
-            bits.append(bit)
-            bit *= 2
-        high = n_ctx // 2
-        ended = []
-        for source, name in ((attended, "weight_grad_own"), (att_other, "weight_grad_other")):
-            part = shape((ratio // 2, head_rows, cols), BF16)
-            keep, send = call(
-                functools.partial(weight_grad_kernel, tuple(bits)), name, [source, grad_out],
-                [part, part], flops=proj,
-            )
-            for bit in bits:
-                got = lax.ppermute(send, "ctx", flip(bit))
-                both = add(keep, got)
-                if bit != bits[-1]:
-                    middle = both.shape[0] // 2
-                    keep, send = both[:middle], both[middle:].astype(BF16)
-            ended.append(both[0])
-        sum_own, sum_other = ended
-        same = (ctx // high) == head
-        first_route, second_route = [], []
-        for c in range(n_ctx):
-            for h in range(2):
-                here = 2 * c + h
-                if c // high == h:
-                    first_route.append((here, 2 * c + 1 - h))
-                else:
-                    first_route.append((here, 2 * (c ^ high) + h))
-                    second_route.append((here, 2 * (c ^ high) + 1 - h))
-        other_low = sum_other.astype(BF16)
-        first = lax.ppermute(jnp.where(same, other_low, sum_own.astype(BF16)), ("ctx", "head"), first_route)
-        second = lax.ppermute(other_low, ("ctx", "head"), second_route)
-        grad_w_out = (first.astype(F32) + jnp.where(same, sum_own, second.astype(F32))).astype(BF16)
+    for bit in stride_bits[2:]:
+        stride_keep, stride_send = halve(run, "stride_z", stride_keep, stride_got)
+        stride_got = lax.ppermute(stride_send, "ctx", flip(bit))
+    if pair:
+        block = (head_rows, cols)
+        other_low, = run(end_kernel, "weight_grad_other_end", [other_keep, other_got], [shape(block, BF16)])
+        other_got = lax.ppermute(other_low, "head", swap)
+        sum_keep, sum_send = run(
+            choose_kernel, "choose", [own_keep, own_got, other_got], [shape(block, F32), shape(block, BF16)]
+        )
+        sum_got = lax.ppermute(sum_send, "ctx", flip(n_ctx // 2))
     else:
         att_all = lax.all_gather(attended, "head", axis=1, tiled=True)
         layer_out = mm(att_all, w_all).astype(BF16)
@@ -485,11 +623,13 @@
                 route.append((c * n_head + h, target))
         grad_w_out = lax.ppermute(terms, ("ctx", "head"), route)
 
-    key_gradient, value_gradient = call(
+    key_gradient, value_gradient = run(
         finish_kernel, "finish", [stride_offset, own, one_got, two_got, stride_keep, stride_got],
         [shape((rows, HEAD_SIZE), BF16)] * 2,
         [pltpu.VMEM((2 * rows, HEAD_SIZE), F32)],
     )
+    if pair:
+        grad_w_out, = run(last_sum_kernel, "last_sum", [sum_keep, sum_got], [shape(block, BF16)])
     return (layer_out, grad_queries, key_gradient, value_gradient, grad_w_out)
 
 

time: 116 us -> 84.4 us (0.73)
  waiting for transfers between devices: 50.7 us -> 20.3 us
  starting transfers between devices: 25.8 us -> 32.5 us
  local copies, waits for them, and re-layouts: 6.24 us -> 2.45 us
  other arithmetic: 2.44 us -> 0 us
    ppermute x16, waiting for transfers between devices: 47.3 us -> 15.2 us  [the longest x1 4.53 us: body(): picks_got = lax.ppermute(picks, 'ctx', flip(bit))]
    ppermute x16, starting transfers between devices: 17.3 us -> 24.4 us  [the longest x1 3.42 us: body(): stride_got = lax.ppermute(stride_send, 'ctx', flip(stride_bits[1]))]
    ppermute x1, waiting for transfers between devices: 0.01 us -> 2.67 us  [body(): grad_got = lax.ppermute(grad_other, 'head', swap)]
    unnamed x43 -> x12, local copies, waits for them, and re-layouts: 4.97 us -> 2.45 us
    ppermute x1, waiting for transfers between devices: 1.64 us -> 0.01 us  [body(): kv_core = lax.ppermute(kv, 'ctx', flip(1))]
    add x7 -> x0, other arithmetic: 1.55 us -> none  [add(): return left.astype(F32) + right.astype(F32)]
    ppermute x1, waiting for transfers between devices: 0.01 us -> 1.4 us  [body(): w_far = lax.ppermute(w_near, 'ctx', flip(1))]
    pallas_call x11 -> x27, Pallas kernels: 29.2 us -> 28.1 us  [the longest x25 28.1 us: __call__(): pl.pallas_call(wrapped, name=name, out_shape=list(out_shapes) + [shape((8...]
  transfers between devices with their start and end apart: 25 -> 25, of which waited for: 12 -> 11; matrix products, arithmetic and copies ran while one was open for 3% -> 0% of each run, Pallas kernels for 23% -> 28%
where the time goes in v2:
time: 84.4 us; the launch traced here: 84.1 us
  starting transfers between devices  32.5 us (39%)
  Pallas kernels  28.1 us (33%)
  waiting for transfers between devices  20.3 us (24%)
  local copies, waits for them, and re-layouts  2.45 us (3%)
    pallas_call x25, Pallas kernels, __call__(): pl.pallas_call(wrapped, name=name, out_shape=list(out_shapes) + [shape((8...  28.1 us
    ppermute x1, waiting for transfers between devices, body(): picks_got = lax.ppermute(picks, 'ctx', flip(bit))  4.53 us
    ppermute x1, starting transfers between devices, body(): kv_two = lax.ppermute(kv, 'ctx', [(i, i + 2) for i in range(n_ctx - 2)])  3.43 us
    ppermute x1, starting transfers between devices, body(): stride_got = lax.ppermute(stride_send, 'ctx', flip(stride_bits[1]))  3.42 us
    ppermute x1, starting transfers between devices, body(): sum_got = lax.ppermute(sum_send, 'ctx', flip(n_ctx // 2))  3.09 us
    ppermute x1, waiting for transfers between devices, body(): grad_got = lax.ppermute(grad_other, 'head', swap)  2.67 us
    ppermute x1, starting transfers between devices, body(): picks_got = lax.ppermute(picks, 'ctx', flip(order[0]))  2.65 us
    ppermute x1, starting transfers between devices, body(): picks_got = lax.ppermute(picks, 'ctx', flip(order[1]))  2.64 us
  transfers between devices with their start and end apart: 25, of which 11 were waited for; matrix products, arithmetic and copies ran while one was open for 0% of the time, Pallas kernels for 28%

profile of v2, /device:TPU:0, one launch (start us, length us, event | category | flops | bytes accessed | tf_op | source)
XLA Modules:
  0.0 84.1 jit_solution(14272445517506807587)
XLA Ops:
  0.6 3.4 %pack.1 = (bf16[1024,128]{1,0:T(8,128)(2,1)}, bf16[256,128]{1,0:T(8,128)(2,1)}, bf16[256,1024]{1,0:T(8,128)(2,1)}, f32[8,128]{1,0:T(8,128)}) custom-call(s32[2]{0:T(128)} %refs_0_.13, bf16[512,128]{1,0:T(8,128)(2,1)} %refs_1_.4, bf16[512,128]{1,0:T(8,128)(2,1)} %refs_2_.1, bf16[256,4096]{1,0:T(8,128)(2,1)} %refs_1_.5), custom_call_target="tpu_custom_call" | custom-call | flops 2000000000 | bytes 1 | tf_op jit(solution)/shard_map/pack/pallas_call | solution.py:55
  4.1 0.5 collective-permute-start.2
  4.6 2.6 %collective-permute-start = (bf16[256,128]{1,0:T(8,128)(2,1)}, bf16[256,128]{1,0:T(8,128)(2,1)S(1)}, u32[]{:S(2)}, u32[]{:S(2)}) collective-permute-start(bf16[256,128]{1,0:T(8,128)(2,1)} %get-tuple-element.82.refs_0_), channel_id=1, source_target_pairs={{0,8},{2,10},{4,12},{6,14},{8,0},{10,2},{12,4},{14,6},{16,24},{18,... | collective-permute-start | bytes 196616 | tf_op jit(solution)/shard_map/ppermute | solution.py:486
  7.3 3.4 %collective-permute-start.4 = (bf16[1024,128]{1,0:T(8,128)(2,1)}, bf16[1024,128]{1,0:T(8,128)(2,1)S(1)}, u32[]{:S(2)}, u32[]{:S(2)}) collective-permute-start(bf16[1024,128]{1,0:T(8,128)(2,1)} %get-tuple-element.85.refs_1_.refs_2_), channel_id=1, source_target_pairs={{0,4},{2,6},{4,8},{6,10},{8,12},{10,14},{12,16},{14,18},{16,20},{1... | collective-permute-start | bytes 786440 | tf_op jit(solution)/shard_map/ppermute | solution.py:487
  10.7 1.6 %collective-permute-start.7 = (bf16[256,1024]{1,0:T(8,128)(2,1)}, bf16[256,1024]{1,0:T(8,128)(2,1)S(1)}, u32[]{:S(2)}, u32[]{:S(2)}) collective-permute-start(bf16[256,1024]{1,0:T(8,128)(2,1)} %get-tuple-element.97), channel_id=1, source_target_pairs={{0,1},{1,0},{2,3},{3,2},{4,5},{5,4},{6,7},{7,6},{8,9},{9,8},{10,11... | collective-permute-start | bytes 1572872 | tf_op jit(solution)/shard_map/ppermute | solution.py:477
  12.2 0.0 collective-permute-done.refs_1_
  12.3 0.8 copy-done.4
  13.1 2.6 %collective-permute-start.1 = (bf16[512,128]{1,0:T(8,128)(2,1)S(1)}, bf16[512,128]{1,0:T(8,128)(2,1)S(1)}, u32[]{:S(2)}, u32[]{:S(2)}) collective-permute-start(bf16[512,128]{1,0:T(8,128)(2,1)S(1)} %get-tuple-element.83.refs_0_), channel_id=1, source_target_pairs={{0,16},{2,18},{4,20},{6,22},{8,24},{10,26},{12,28},{14,30},{16,0},... | collective-permute-start | bytes 393224 | tf_op jit(solution)/shard_map/ppermute | solution.py:490
  15.8 0.0 collective-permute-done.2.refs_3_.refs_2_
  15.8 1.6 %copy-done.3 = bf16[512,2048]{1,0:T(8,128)(2,1)S(1)} copy-done((bf16[512,2048]{1,0:T(8,128)(2,1)S(1)}, bf16[512,2048]{1,0:T(8,128)(2,1)}, u32[]{:S(2)}) %copy-start.3) | copy-done | bytes 2097176
  17.4 2.0 %grad_own.1 = (f32[512,256]{1,0:T(8,128)S(1)}, bf16[512,2048]{1,0:T(8,128)(2,1)S(1)}, bf16[256,2048]{1,0:T(8,128)(2,1)S(1)}, f32[8,128]{1,0:T(8,128)S(1)}) custom-call(bf16[512,2048]{1,0:T(8,128)(2,1)S(1)} %copy-done.3, bf16[256,4096]{1,0:T(8,128)(2,1)S(1)} %copy-done.2, f32[8,128]{1,0:T(8,128)S(1)} %get-tuple-element.84.refs_2_, ...), custom_call_target="tpu_custom_call" | custom-call | flops 2000000000 | bytes 1 | tf_op jit(solution)/shard_map/grad_own/pallas_call | solution.py:55
  19.4 2.4 %collective-permute-done.1.refs_1_ = bf16[512,128]{1,0:T(8,128)(2,1)S(1)} collective-permute-done((bf16[512,128]{1,0:T(8,128)(2,1)S(1)}, bf16[512,128]{1,0:T(8,128)(2,1)S(1)}, u32[]{:S(2)}, u32[]{:S(2)}) %collective-permute-start.1) | collective-permute-done | bytes 131104 | tf_op jit(solution)/shard_map/ppermute | solution.py:490
  21.8 0.1 collective-permute-start.5
  21.9 0.6 collective-permute-start.3
  22.5 0.9 %collective-permute-done.5.refs_4_.refs_5_ = bf16[1024,128]{1,0:T(8,128)(2,1)S(1)} collective-permute-done((bf16[1024,128]{1,0:T(8,128)(2,1)S(1)}, bf16[1024,128]{1,0:T(8,128)(2,1)S(1)}, u32[]{:S(2)}, u32[]{:S(2)}) %collective-permute-start.5) | collective-permute-done | bytes 262176 | tf_op jit(solution)/shard_map/ppermute | solution.py:501
  23.4 2.7 %band_forward.1 = (f32[2,128,512]{2,1,0:T(8,128)S(1)}, f32[2,512]{1,0:T(2,128)S(1)}, f32[2,512]{1,0:T(2,128)S(1)}, f32[8,128]{1,0:T(8,128)S(1)}) custom-call(bf16[512,256]{1,0:T(8,128)(2,1)S(1)} %copy-done, bf16[1024,128]{1,0:T(8,128)(2,1)S(1)} %copy-done.1, bf16[1024,128]{1,0:T(8,128)(2,1)S(1)} %collective-permute-done.2.refs_3_.refs_2_, ...), custom_call_target="tpu_custom_call" | custom-call | flops 100000000 | bytes 1 | tf_op jit(solution)/shard_map/band_forward/pallas_call | solution.py:55
  26.1 4.5 %collective-permute-done.3.refs_1_ = bf16[1024,128]{1,0:T(8,128)(2,1)S(1)} collective-permute-done((bf16[1024,128]{1,0:T(8,128)(2,1)S(1)}, bf16[1024,128]{1,0:T(8,128)(2,1)S(1)}, u32[]{:S(2)}, u32[]{:S(2)}) %collective-permute-start.3) | collective-permute-done | bytes 262176 | tf_op jit(solution)/shard_map/ppermute | solution.py:499
  30.6 0.0 collective-permute-done.7.refs_0_
  30.7 0.1 collective-permute-start.8
  30.7 0.5 collective-permute-start.6
  31.2 1.4 %collective-permute-done.8.refs_2_.refs_4_ = bf16[256,1024]{1,0:T(8,128)(2,1)S(1)} collective-permute-done((bf16[256,1024]{1,0:T(8,128)(2,1)S(1)}, bf16[256,1024]{1,0:T(8,128)(2,1)S(1)}, u32[]{:S(2)}, u32[]{:S(2)}) %collective-permute-start.8) | collective-permute-done | bytes 524320 | tf_op jit(solution)/shard_map/ppermute | solution.py:517
  32.6 0.7 grad_other.1
  33.4 0.7 collective-permute-start.10
  34.1 3.6 %stride_forward.1 = (bf16[512,256]{1,0:T(8,128)(2,1)S(1)}, f32[2,512]{1,0:T(2,128)S(1)}, f32[8,128]{1,0:T(8,128)S(1)}) custom-call(s32[2]{0:T(128)S(1)} %copy-done.5, bf16[512,256]{1,0:T(8,128)(2,1)S(1)} %copy-done, bf16[2048,128]{1,0:T(8,128)(2,1)S(1)} %get-tuple-element.92.refs_2_.refs_6_, bf16[2048,128]{1,0:T(8,128)(2,1)S(1)} %collective-permute-done.6.refs_3_.refs_7_, ...), custom_call_target="tpu_custom_call" | custom-call | flops 35999997952 | bytes 1 | tf_op jit(solution)/shard_map/stride_forward/pallas_call | solution.py:55
  37.7 1.4 %collective-permute-start.9 = (bf16[512,256]{1,0:T(8,128)(2,1)S(1)}, bf16[512,256]{1,0:T(8,128)(2,1)S(1)}, u32[]{:S(2)}, u32[]{:S(2)}) collective-permute-start(bf16[512,256]{1,0:T(8,128)(2,1)S(1)} %get-tuple-element.102.refs_0_.refs_4_), channel_id=1, source_target_pairs={{0,1},{1,0},{2,3},{3,2},{4,5},{5,4},{6,7},{7,6},{8,9},{9,8},{10,11... | collective-permute-start | bytes 786440 | tf_op jit(solution)/shard_map/ppermute | solution.py:537
  39.1 0.7 weight_grad_own.1
  39.9 0.1 collective-permute-start.11
  39.9 2.7 %collective-permute-done.10.refs_3_ = bf16[512,256]{1,0:T(8,128)(2,1)S(1)} collective-permute-done((bf16[512,256]{1,0:T(8,128)(2,1)S(1)}, bf16[512,256]{1,0:T(8,128)(2,1)S(1)}, u32[]{:S(2)}, u32[]{:S(2)}) %collective-permute-start.10) | collective-permute-done | bytes 262176 | tf_op jit(solution)/shard_map/ppermute | solution.py:522
  42.6 4.6 %stride_backward.1 = (bf16[512,256]{1,0:T(8,128)(2,1)S(1)}, f32[2,512]{1,0:T(2,128)S(1)}, f32[2,128,512]{2,1,0:T(8,128)S(1)}, bf16[2048,128]{1,0:T(8,128)(2,1)S(...) custom-call(s32[2]{0:T(128)S(1)} %copy-done.5, bf16[512,256]{1,0:T(8,128)(2,1)S(1)} %copy-done, ...), custom_call_target="tpu_custom_call" | custom-call | flops 46000001024 | bytes 1 | tf_op jit(solution)/shard_map/stride_backward/pallas_call | solution.py:55
  47.2 0.1 collective-permute-start.13
  47.3 0.1 collective-permute-done.9.refs_3_.refs_0_.refs_1_
  47.4 0.0 collective-permute-done.11.refs_1_
  47.4 0.1 weight_grad_own_core.1
  47.5 0.7 weight_grad_other.1
  48.3 0.4 collective-permute-start.12
  48.7 1.9 %collective-permute-start.17 = (bf16[2,256,256]{2,1,0:T(8,128)(2,1)S(1)}, bf16[2,256,256]{2,1,0:T(8,128)(2,1)S(1)}, u32[]{:S(2)}, u32[]{:S(2)}) collective-permute-start(bf16[2,256,256]{2,1,0:T(8,128)(2,1)S(1)} %get-tuple-element.130), channel_id=1, source_target_pairs={{0,8},{2,10},{4,12},{6,14},{8,0},{10,2},{12,4},{14,6},{16,24},{18,... | collective-permute-start | bytes 786440 | tf_op jit(solution)/shard_map/ppermute | solution.py:565
  50.6 0.1 stride_core.1
  50.7 1.8 %collective-permute-start.16 = (bf16[1024,128]{1,0:T(8,128)(2,1)S(1)}, bf16[1024,128]{1,0:T(8,128)(2,1)S(1)}, u32[]{:S(2)}, u32[]{:S(2)}) collective-permute-start(bf16[1024,128]{1,0:T(8,128)(2,1)S(1)} %get-tuple-element.128), channel_id=1, source_target_pairs={{0,4},{2,6},{4,0},{6,2},{8,12},{10,14},{12,8},{14,10},{16,20},{18,... | collective-permute-start | bytes 786440 | tf_op jit(solution)/shard_map/ppermute | solution.py:569
  52.5 0.3 weight_grad_other_core.1
  52.9 0.3 collective-permute-start.15
  53.2 3.9 %band_backward.1 = (bf16[512,256]{1,0:T(8,128)(2,1)}, bf16[1024,128]{1,0:T(8,128)(2,1)S(1)}, bf16[1024,128]{1,0:T(8,128)(2,1)S(1)}, bf16[1024,128]{1,0:T(8,128)(2,1)S(1)}, f32[8,128]{1,0:T(8,128)S(1)}) custom-call(bf16[512,256]{1,0:T(8,128)(2,1)S(1)} %copy-done, bf16[512,256]{1,0:T(8,128)(2,1)S(1)} %get-tuple-element.109.refs_1_, ...), custom_call_target="tpu_custom_call" | custom-call | flops 40000000000 | bytes 1 | tf_op jit(solution)/shard_map/band_backward/pallas_call | solution.py:55
  57.1 0.0 collective-permute-start.14
  57.1 0.2 collective-permute-done.17.refs_1_
  57.3 0.1 weight_grad_own_low.1
  57.4 2.6 %collective-permute-done.16.refs_1_ = bf16[1024,128]{1,0:T(8,128)(2,1)S(1)} collective-permute-done((bf16[1024,128]{1,0:T(8,128)(2,1)S(1)}, bf16[1024,128]{1,0:T(8,128)(2,1)S(1)}, u32[]{:S(2)}, u32[]{:S(2)}) %collective-permute-start.16) | collective-permute-done | bytes 262176 | tf_op jit(solution)/shard_map/ppermute | solution.py:569
  60.0 3.4 %collective-permute-start.19 = (bf16[512,128]{1,0:T(8,128)(2,1)S(1)}, bf16[512,128]{1,0:T(8,128)(2,1)S(1)}, u32[]{:S(2)}, u32[]{:S(2)}) collective-permute-start(bf16[512,128]{1,0:T(8,128)(2,1)S(1)} %get-tuple-element.141), channel_id=1, source_target_pairs={{0,16},{2,18},{4,20},{6,22},{8,24},{10,26},{12,28},{14,30},{16,0},... | collective-permute-start | bytes 393224 | tf_op jit(solution)/shard_map/ppermute | solution.py:590
  63.4 1.8 %collective-permute-start.21 = (bf16[1,256,256]{2,1,0:T(8,128)(2,1)S(1)}, bf16[1,256,256]{2,1,0:T(8,128)(2,1)S(1)}, u32[]{:S(2)}, u32[]{:S(2)}) collective-permute-start(bf16[1,256,256]{2,1,0:T(8,128)(2,1)S(1)} %get-tuple-element.146), channel_id=1, source_target_pairs={{0,4},{2,6},{4,0},{6,2},{8,12},{10,14},{12,8},{14,10},{16,20},{18,... | collective-permute-start | bytes 393224 | tf_op jit(solution)/shard_map/ppermute | solution.py:588
  65.2 0.1 weight_grad_other_low.1
  65.3 0.5 collective-permute-start.22
  65.8 0.0 collective-permute-done.14.refs_1_.refs_2_
  65.8 0.1 band_two.1
  65.8 1.3 %collective-permute-start.18 = (bf16[1024,128]{1,0:T(8,128)(2,1)S(1)}, bf16[1024,128]{1,0:T(8,128)(2,1)S(1)}, u32[]{:S(2)}, u32[]{:S(2)}) collective-permute-start(bf16[1024,128]{1,0:T(8,128)(2,1)S(1)} %get-tuple-element.139), channel_id=1, source_target_pairs={{4,0},{6,2},{8,4},{10,6},{12,8},{14,10},{16,12},{18,14},{20,16},{2... | collective-permute-start | bytes 786440 | tf_op jit(solution)/shard_map/ppermute | solution.py:596
  67.1 2.6 %layer_out.1 = (bf16[512,2048]{1,0:T(8,128)(2,1)}, f32[8,128]{1,0:T(8,128)S(1)}) custom-call(bf16[512,256]{1,0:T(8,128)(2,1)S(1)} %get-tuple-element.102.refs_0_.refs_4_, bf16[512,256]{1,0:T(8,128)(2,1)S(1)} %collective-permute-done.9.refs_3_.refs_0_.refs_1_, bf16[256,2048]{1,0:T(8,128)(2,1)S(1)} %get-tuple-element.103.refs_2_, ...), custom_call_target="tpu_custom_call" | custom-call | flops 25999998976 | bytes 1 | tf_op jit(solution)/shard_map/layer_out/pallas_call | solution.py:55
  69.8 1.9 %collective-permute-done.22.refs_1_ = bf16[1,256,256]{2,1,0:T(8,128)(2,1)S(1)} collective-permute-done((bf16[1,256,256]{2,1,0:T(8,128)(2,1)S(1)}, bf16[1,256,256]{2,1,0:T(8,128)(2,1)S(1)}, u32[]{:S(2)}, u32[]{:S(2)}) %collective-permute-start.22) | collective-permute-done | bytes 131104 | tf_op jit(solution)/shard_map/ppermute | solution.py:594
  71.7 1.0 %collective-permute-start.23 = (bf16[256,256]{1,0:T(8,128)(2,1)S(1)}, bf16[256,256]{1,0:T(8,128)(2,1)S(1)}, u32[]{:S(2)}, u32[]{:S(2)}) collective-permute-start(bf16[256,256]{1,0:T(8,128)(2,1)S(1)} %get-tuple-element.150), channel_id=1, source_target_pairs={{0,1},{1,0},{2,3},{3,2},{4,5},{5,4},{6,7},{7,6},{8,9},{9,8},{10,11... | collective-permute-start | bytes 393224 | tf_op jit(solution)/shard_map/ppermute | solution.py:608
  72.7 2.6 %collective-permute-start.20 = (bf16[256,128]{1,0:T(8,128)(2,1)S(1)}, bf16[256,128]{1,0:T(8,128)(2,1)S(1)}, u32[]{:S(2)}, u32[]{:S(2)}) collective-permute-start(bf16[256,128]{1,0:T(8,128)(2,1)S(1)} %get-tuple-element.144), channel_id=1, source_target_pairs={{0,8},{2,10},{4,12},{6,14},{8,0},{10,2},{12,4},{14,6},{16,24},{18,... | collective-permute-start | bytes 196616 | tf_op jit(solution)/shard_map/ppermute | solution.py:604
  75.3 1.4 %collective-permute-done.23.refs_2_ = bf16[256,256]{1,0:T(8,128)(2,1)S(1)} collective-permute-done((bf16[256,256]{1,0:T(8,128)(2,1)S(1)}, bf16[256,256]{1,0:T(8,128)(2,1)S(1)}, u32[]{:S(2)}, u32[]{:S(2)}) %collective-permute-start.23) | collective-permute-done | bytes 131104 | tf_op jit(solution)/shard_map/ppermute | solution.py:608
  76.7 0.1 choose.1
  76.8 3.1 %collective-permute-start.24 = (bf16[256,256]{1,0:T(8,128)(2,1)S(1)}, bf16[256,256]{1,0:T(8,128)(2,1)S(1)}, u32[]{:S(2)}, u32[]{:S(2)}) collective-permute-start(bf16[256,256]{1,0:T(8,128)(2,1)S(1)} %get-tuple-element.156), channel_id=1, source_target_pairs={{0,16},{2,18},{4,20},{6,22},{8,24},{10,26},{12,28},{14,30},{16,0},... | collective-permute-start | bytes 393224 | tf_op jit(solution)/shard_map/ppermute | solution.py:612
  79.9 0.0 collective-permute-done.20.refs_5_
  79.9 0.0 collective-permute-done.18.refs_3_
  79.9 1.4 %finish.1 = (bf16[512,128]{1,0:T(8,128)(2,1)}, bf16[512,128]{1,0:T(8,128)(2,1)}, f32[8,128]{1,0:T(8,128)S(1)}) custom-call(s32[2]{0:T(128)S(1)} %copy-done.5, bf16[1024,128]{1,0:T(8,128)(2,1)S(1)} %get-tuple-element.138.refs_1_, bf16[1024,128]{1,0:T(8,128)(2,1)S(1)} %collective-permute-done.14.refs_1_.refs_2_, ...), custom_call_target="tpu_custom_call" | custom-call | flops 15000000512 | bytes 1 | tf_op jit(solution)/shard_map/finish/pallas_call | solution.py:55
  81.3 2.1 %collective-permute-done.24.refs_1_ = bf16[256,256]{1,0:T(8,128)(2,1)S(1)} collective-permute-done((bf16[256,256]{1,0:T(8,128)(2,1)S(1)}, bf16[256,256]{1,0:T(8,128)(2,1)S(1)}, u32[]{:S(2)}, u32[]{:S(2)}) %collective-permute-start.24) | collective-permute-done | bytes 131104 | tf_op jit(solution)/shard_map/ppermute | solution.py:612
  83.5 0.7 last_sum.1
  (25 shorter events, 0.2 us)
Async XLA Ops:
  0.6 15.1 %copy-start.2 = (bf16[256,4096]{1,0:T(8,128)(2,1)S(1)}, bf16[256,4096]{1,0:T(8,128)(2,1)}, u32[]{:S(2)}) copy-start(bf16[256,4096]{1,0:T(8,128)(2,1)} %refs_1_.5) | copy-start | bytes 6291460
  4.1 11.7 %collective-permute-start.2 = (bf16[1024,128]{1,0:T(8,128)(2,1)}, bf16[1024,128]{1,0:T(8,128)(2,1)S(1)}, u32[]{:S(2)}, u32[]{:S(2)}) collective-permute-start(bf16[1024,128]{1,0:T(8,128)(2,1)} %get-tuple-element.85.refs_1_.refs_2_), channel_id=1, source_target_pairs={{0,2},{2,0},{4,6},{6,4},{8,10},{10,8},{12,14},{14,12},{16,18},{18,... | collective-permute-start | bytes 786440 | tf_op jit(solution)/shard_map/ppermute | solution.py:488
  4.6 7.6 %collective-permute-start = (bf16[256,128]{1,0:T(8,128)(2,1)}, bf16[256,128]{1,0:T(8,128)(2,1)S(1)}, u32[]{:S(2)}, u32[]{:S(2)}) collective-permute-start(bf16[256,128]{1,0:T(8,128)(2,1)} %get-tuple-element.82.refs_0_), channel_id=1, source_target_pairs={{0,8},{2,10},{4,12},{6,14},{8,0},{10,2},{12,4},{14,6},{16,24},{18,... | collective-permute-start | bytes 196616 | tf_op jit(solution)/shard_map/ppermute | solution.py:486
  7.3 14.5 %collective-permute-start.4 = (bf16[1024,128]{1,0:T(8,128)(2,1)}, bf16[1024,128]{1,0:T(8,128)(2,1)S(1)}, u32[]{:S(2)}, u32[]{:S(2)}) collective-permute-start(bf16[1024,128]{1,0:T(8,128)(2,1)} %get-tuple-element.85.refs_1_.refs_2_), channel_id=1, source_target_pairs={{0,4},{2,6},{4,8},{6,10},{8,12},{10,14},{12,16},{14,18},{16,20},{1... | collective-permute-start | bytes 786440 | tf_op jit(solution)/shard_map/ppermute | solution.py:487
  10.7 20.0 %collective-permute-start.7 = (bf16[256,1024]{1,0:T(8,128)(2,1)}, bf16[256,1024]{1,0:T(8,128)(2,1)S(1)}, u32[]{:S(2)}, u32[]{:S(2)}) collective-permute-start(bf16[256,1024]{1,0:T(8,128)(2,1)} %get-tuple-element.97), channel_id=1, source_target_pairs={{0,1},{1,0},{2,3},{3,2},{4,5},{5,4},{6,7},{7,6},{8,9},{9,8},{10,11... | collective-permute-start | bytes 1572872 | tf_op jit(solution)/shard_map/ppermute | solution.py:477
  12.3 0.8 copy-start.4
  13.1 8.7 %collective-permute-start.1 = (bf16[512,128]{1,0:T(8,128)(2,1)S(1)}, bf16[512,128]{1,0:T(8,128)(2,1)S(1)}, u32[]{:S(2)}, u32[]{:S(2)}) collective-permute-start(bf16[512,128]{1,0:T(8,128)(2,1)S(1)} %get-tuple-element.83.refs_0_), channel_id=1, source_target_pairs={{0,16},{2,18},{4,20},{6,22},{8,24},{10,26},{12,28},{14,30},{16,0},... | collective-permute-start | bytes 393224 | tf_op jit(solution)/shard_map/ppermute | solution.py:490
  15.8 1.6 %copy-start.3 = (bf16[512,2048]{1,0:T(8,128)(2,1)S(1)}, bf16[512,2048]{1,0:T(8,128)(2,1)}, u32[]{:S(2)}) copy-start(bf16[512,2048]{1,0:T(8,128)(2,1)} %refs_0_.8) | copy-start | bytes 6291460
  17.3 6.1 %copy-start = (bf16[512,256]{1,0:T(8,128)(2,1)S(1)}, bf16[512,256]{1,0:T(8,128)(2,1)}, u32[]{:S(2)}) copy-start(bf16[512,256]{1,0:T(8,128)(2,1)} %refs_0_.12) | copy-start | bytes 786436
  17.4 6.1 %copy-start.1 = (bf16[1024,128]{1,0:T(8,128)(2,1)S(1)}, bf16[1024,128]{1,0:T(8,128)(2,1)}, u32[]{:S(2)}) copy-start(bf16[1024,128]{1,0:T(8,128)(2,1)} %get-tuple-element.85.refs_1_.refs_2_) | copy-start | bytes 786436
  21.8 1.6 %collective-permute-start.5 = (bf16[1024,128]{1,0:T(8,128)(2,1)S(1)}, bf16[1024,128]{1,0:T(8,128)(2,1)S(1)}, u32[]{:S(2)}, u32[]{:S(2)}) collective-permute-start(bf16[1024,128]{1,0:T(8,128)(2,1)S(1)} %get-tuple-element.89.refs_3_.refs_4_), channel_id=1, source_target_pairs={{0,2},{2,0},{4,6},{6,4},{8,10},{10,8},{12,14},{14,12},{16,18},{18,... | collective-permute-start | bytes 786440 | tf_op jit(solution)/shard_map/ppermute | solution.py:501
  21.9 8.7 %collective-permute-start.3 = (bf16[1024,128]{1,0:T(8,128)(2,1)S(1)}, bf16[1024,128]{1,0:T(8,128)(2,1)S(1)}, u32[]{:S(2)}, u32[]{:S(2)}) collective-permute-start(bf16[1024,128]{1,0:T(8,128)(2,1)S(1)} %get-tuple-element.87.refs_0_), channel_id=1, source_target_pairs={{0,4},{2,6},{4,0},{6,2},{8,12},{10,14},{12,8},{14,10},{16,20},{18,... | collective-permute-start | bytes 786440 | tf_op jit(solution)/shard_map/ppermute | solution.py:499
  30.6 3.5 %copy-start.5 = (s32[2]{0:T(128)S(1)}, s32[2]{0:T(128)}, u32[]{:S(2)}) copy-start(s32[2]{0:T(128)} %refs_0_.13) | copy-start | bytes 28
  30.7 2.0 %collective-permute-start.8 = (bf16[256,1024]{1,0:T(8,128)(2,1)S(1)}, bf16[256,1024]{1,0:T(8,128)(2,1)S(1)}, u32[]{:S(2)}, u32[]{:S(2)}) collective-permute-start(bf16[256,1024]{1,0:T(8,128)(2,1)S(1)} %get-tuple-element.99.refs_1_.refs_3_), channel_id=1, source_target_pairs={{0,2},{2,0},{4,6},{6,4},{8,10},{10,8},{12,14},{14,12},{16,18},{18,... | collective-permute-start | bytes 1572872 | tf_op jit(solution)/shard_map/ppermute | solution.py:517
  30.7 3.4 %collective-permute-start.6 = (bf16[2048,128]{1,0:T(8,128)(2,1)S(1)}, bf16[2048,128]{1,0:T(8,128)(2,1)S(1)}, u32[]{:S(2)}, u32[]{:S(2)}) collective-permute-start(bf16[2048,128]{1,0:T(8,128)(2,1)S(1)} %get-tuple-element.92.refs_2_.refs_6_), channel_id=1, source_target_pairs={{0,2},{2,0},{4,6},{6,4},{8,10},{10,8},{12,14},{14,12},{16,18},{18,... | collective-permute-start | bytes 1572872 | tf_op jit(solution)/shard_map/ppermute | solution.py:514
  33.4 9.2 %collective-permute-start.10 = (bf16[512,256]{1,0:T(8,128)(2,1)S(1)}, bf16[512,256]{1,0:T(8,128)(2,1)S(1)}, u32[]{:S(2)}, u32[]{:S(2)}) collective-permute-start(bf16[512,256]{1,0:T(8,128)(2,1)S(1)} %get-tuple-element.105), channel_id=1, source_target_pairs={{0,1},{1,0},{2,3},{3,2},{4,5},{5,4},{6,7},{7,6},{8,9},{9,8},{10,11... | collective-permute-start | bytes 786440 | tf_op jit(solution)/shard_map/ppermute | solution.py:522
  37.7 9.7 %collective-permute-start.9 = (bf16[512,256]{1,0:T(8,128)(2,1)S(1)}, bf16[512,256]{1,0:T(8,128)(2,1)S(1)}, u32[]{:S(2)}, u32[]{:S(2)}) collective-permute-start(bf16[512,256]{1,0:T(8,128)(2,1)S(1)} %get-tuple-element.102.refs_0_.refs_4_), channel_id=1, source_target_pairs={{0,1},{1,0},{2,3},{3,2},{4,5},{5,4},{6,7},{7,6},{8,9},{9,8},{10,11... | collective-permute-start | bytes 786440 | tf_op jit(solution)/shard_map/ppermute | solution.py:537
  39.9 7.6 %collective-permute-start.11 = (bf16[4,256,256]{2,1,0:T(8,128)(2,1)S(1)}, bf16[4,256,256]{2,1,0:T(8,128)(2,1)S(1)}, u32[]{:S(2)}, u32[]{:S(2)}) collective-permute-start(bf16[4,256,256]{2,1,0:T(8,128)(2,1)S(1)} %get-tuple-element.113), channel_id=1, source_target_pairs={{0,2},{2,0},{4,6},{6,4},{8,10},{10,8},{12,14},{14,12},{16,18},{18,... | collective-permute-start | bytes 1572872 | tf_op jit(solution)/shard_map/ppermute | solution.py:551
  47.2 3.4 %collective-permute-start.13 = (bf16[2048,128]{1,0:T(8,128)(2,1)S(1)}, bf16[2048,128]{1,0:T(8,128)(2,1)S(1)}, u32[]{:S(2)}, u32[]{:S(2)}) collective-permute-start(bf16[2048,128]{1,0:T(8,128)(2,1)S(1)} %get-tuple-element.119), channel_id=1, source_target_pairs={{0,2},{2,0},{4,6},{6,4},{8,10},{10,8},{12,14},{14,12},{16,18},{18,... | collective-permute-start | bytes 1572872 | tf_op jit(solution)/shard_map/ppermute | solution.py:562
  48.3 4.2 %collective-permute-start.12 = (bf16[4,256,256]{2,1,0:T(8,128)(2,1)S(1)}, bf16[4,256,256]{2,1,0:T(8,128)(2,1)S(1)}, u32[]{:S(2)}, u32[]{:S(2)}) collective-permute-start(bf16[4,256,256]{2,1,0:T(8,128)(2,1)S(1)} %get-tuple-element.117), channel_id=1, source_target_pairs={{0,2},{2,0},{4,6},{6,4},{8,10},{10,8},{12,14},{14,12},{16,18},{18,... | collective-permute-start | bytes 1572872 | tf_op jit(solution)/shard_map/ppermute | solution.py:567
  48.7 8.6 %collective-permute-start.17 = (bf16[2,256,256]{2,1,0:T(8,128)(2,1)S(1)}, bf16[2,256,256]{2,1,0:T(8,128)(2,1)S(1)}, u32[]{:S(2)}, u32[]{:S(2)}) collective-permute-start(bf16[2,256,256]{2,1,0:T(8,128)(2,1)S(1)} %get-tuple-element.130), channel_id=1, source_target_pairs={{0,8},{2,10},{4,12},{6,14},{8,0},{10,2},{12,4},{14,6},{16,24},{18,... | collective-permute-start | bytes 786440 | tf_op jit(solution)/shard_map/ppermute | solution.py:565
  50.7 9.2 %collective-permute-start.16 = (bf16[1024,128]{1,0:T(8,128)(2,1)S(1)}, bf16[1024,128]{1,0:T(8,128)(2,1)S(1)}, u32[]{:S(2)}, u32[]{:S(2)}) collective-permute-start(bf16[1024,128]{1,0:T(8,128)(2,1)S(1)} %get-tuple-element.128), channel_id=1, source_target_pairs={{0,4},{2,6},{4,0},{6,2},{8,12},{10,14},{12,8},{14,10},{16,20},{18,... | collective-permute-start | bytes 786440 | tf_op jit(solution)/shard_map/ppermute | solution.py:569
  52.9 12.4 %collective-permute-start.15 = (bf16[2,256,256]{2,1,0:T(8,128)(2,1)S(1)}, bf16[2,256,256]{2,1,0:T(8,128)(2,1)S(1)}, u32[]{:S(2)}, u32[]{:S(2)}) collective-permute-start(bf16[2,256,256]{2,1,0:T(8,128)(2,1)S(1)} %get-tuple-element.126), channel_id=1, source_target_pairs={{0,4},{2,6},{4,0},{6,2},{8,12},{10,14},{12,8},{14,10},{16,20},{18,... | collective-permute-start | bytes 786440 | tf_op jit(solution)/shard_map/ppermute | solution.py:572
  57.1 8.7 %collective-permute-start.14 = (bf16[1024,128]{1,0:T(8,128)(2,1)S(1)}, bf16[1024,128]{1,0:T(8,128)(2,1)S(1)}, u32[]{:S(2)}, u32[]{:S(2)}) collective-permute-start(bf16[1024,128]{1,0:T(8,128)(2,1)S(1)} %get-tuple-element.124), channel_id=1, source_target_pairs={{0,2},{2,0},{4,6},{6,4},{8,10},{10,8},{12,14},{14,12},{16,18},{18,... | collective-permute-start | bytes 786440 | tf_op jit(solution)/shard_map/ppermute | solution.py:583
  60.0 9.7 %collective-permute-start.19 = (bf16[512,128]{1,0:T(8,128)(2,1)S(1)}, bf16[512,128]{1,0:T(8,128)(2,1)S(1)}, u32[]{:S(2)}, u32[]{:S(2)}) collective-permute-start(bf16[512,128]{1,0:T(8,128)(2,1)S(1)} %get-tuple-element.141), channel_id=1, source_target_pairs={{0,16},{2,18},{4,20},{6,22},{8,24},{10,26},{12,28},{14,30},{16,0},... | collective-permute-start | bytes 393224 | tf_op jit(solution)/shard_map/ppermute | solution.py:590
  63.4 11.9 %collective-permute-start.21 = (bf16[1,256,256]{2,1,0:T(8,128)(2,1)S(1)}, bf16[1,256,256]{2,1,0:T(8,128)(2,1)S(1)}, u32[]{:S(2)}, u32[]{:S(2)}) collective-permute-start(bf16[1,256,256]{2,1,0:T(8,128)(2,1)S(1)} %get-tuple-element.146), channel_id=1, source_target_pairs={{0,4},{2,6},{4,0},{6,2},{8,12},{10,14},{12,8},{14,10},{16,20},{18,... | collective-permute-start | bytes 393224 | tf_op jit(solution)/shard_map/ppermute | solution.py:588
  65.3 6.3 %collective-permute-start.22 = (bf16[1,256,256]{2,1,0:T(8,128)(2,1)S(1)}, bf16[1,256,256]{2,1,0:T(8,128)(2,1)S(1)}, u32[]{:S(2)}, u32[]{:S(2)}) collective-permute-start(bf16[1,256,256]{2,1,0:T(8,128)(2,1)S(1)} %get-tuple-element.148), channel_id=1, source_target_pairs={{0,8},{2,10},{4,12},{6,14},{8,0},{10,2},{12,4},{14,6},{16,24},{18,... | collective-permute-start | bytes 393224 | tf_op jit(solution)/shard_map/ppermute | solution.py:594
  65.8 14.0 %collective-permute-start.18 = (bf16[1024,128]{1,0:T(8,128)(2,1)S(1)}, bf16[1024,128]{1,0:T(8,128)(2,1)S(1)}, u32[]{:S(2)}, u32[]{:S(2)}) collective-permute-start(bf16[1024,128]{1,0:T(8,128)(2,1)S(1)} %get-tuple-element.139), channel_id=1, source_target_pairs={{4,0},{6,2},{8,4},{10,6},{12,8},{14,10},{16,12},{18,14},{20,16},{2... | collective-permute-start | bytes 786440 | tf_op jit(solution)/shard_map/ppermute | solution.py:596
  71.7 5.0 %collective-permute-start.23 = (bf16[256,256]{1,0:T(8,128)(2,1)S(1)}, bf16[256,256]{1,0:T(8,128)(2,1)S(1)}, u32[]{:S(2)}, u32[]{:S(2)}) collective-permute-start(bf16[256,256]{1,0:T(8,128)(2,1)S(1)} %get-tuple-element.150), channel_id=1, source_target_pairs={{0,1},{1,0},{2,3},{3,2},{4,5},{5,4},{6,7},{7,6},{8,9},{9,8},{10,11... | collective-permute-start | bytes 393224 | tf_op jit(solution)/shard_map/ppermute | solution.py:608
  72.7 7.2 %collective-permute-start.20 = (bf16[256,128]{1,0:T(8,128)(2,1)S(1)}, bf16[256,128]{1,0:T(8,128)(2,1)S(1)}, u32[]{:S(2)}, u32[]{:S(2)}) collective-permute-start(bf16[256,128]{1,0:T(8,128)(2,1)S(1)} %get-tuple-element.144), channel_id=1, source_target_pairs={{0,8},{2,10},{4,12},{6,14},{8,0},{10,2},{12,4},{14,6},{16,24},{18,... | collective-permute-start | bytes 196616 | tf_op jit(solution)/shard_map/ppermute | solution.py:604
  76.8 6.7 %collective-permute-start.24 = (bf16[256,256]{1,0:T(8,128)(2,1)S(1)}, bf16[256,256]{1,0:T(8,128)(2,1)S(1)}, u32[]{:S(2)}, u32[]{:S(2)}) collective-permute-start(bf16[256,256]{1,0:T(8,128)(2,1)S(1)} %get-tuple-element.156), channel_id=1, source_target_pairs={{0,16},{2,18},{4,20},{6,22},{8,24},{10,26},{12,28},{14,30},{16,0},... | collective-permute-start | bytes 393224 | tf_op jit(solution)/shard_map/ppermute | solution.py:612

commit v3 on v2

--- a/solution.py
+++ b/solution.py
@@ -32,7 +32,7 @@
     return lax.dot_general(left, right, dims, preferred_element_type=F32)
 
 
-USEC = {'pack': 2, 'grad_own': 2, 'grad_other': 0.1, 'band_forward': 0.1, 'stride_forward': 36, 'stride_backward': 46, 'band_backward': 40, 'layer_out': 26, 'finish': 15, 'last_sum': 7, 'weight_grad_own': 8, 'weight_grad_other': 8}
+USEC = {'pack': 2, 'grad_own': 2, 'grad_other': 0.1, 'band_forward': 2.7, 'stride_forward': 36, 'stride_backward': 46, 'band_backward': 40, 'layer_out': 26, 'finish': 0.1, 'last_sum': 7, 'weight_grad_own': 8, 'weight_grad_other': 8, 'hold_grad': 10, 'weight_grad_own_low': 10}
 
 
 class Sequence:
@@ -49,7 +49,7 @@
             token = rest[len(out_shapes)]
             token[...] = jnp.zeros_like(token)
 
-        specs = [SMEM if a.dtype == jnp.int32 else VMEM for a in ins]
+        specs = [SMEM if a.ndim == 1 else VMEM for a in ins]
         for index in far:
             specs[index] = HBM
         outs = pl.pallas_call(
@@ -66,8 +66,8 @@
         return outs[:-1]
 
 
-    def hold(self, array, after=()):
-        extra = self.last + list(after)
+    def hold(self, array, name="hold"):
+        extra = self.last
 
         def kernel(*refs):
             token = refs[-1]
@@ -75,13 +75,13 @@
 
         held, token = pl.pallas_call(
             kernel,
-            name="hold",
+            name=name,
             out_shape=[shape(array.shape, array.dtype), shape((8, 128), F32)],
             in_specs=[ANY] * (1 + len(extra)),
             out_specs=[ANY, VMEM],
             input_output_aliases={0: 0},
             compiler_params=pltpu.CompilerParams(vmem_limit_bytes=2**20),
-            cost_estimate=pl.CostEstimate(flops=1, bytes_accessed=1, transcendentals=0),
+            cost_estimate=pl.CostEstimate(flops=int(1e9 * USEC.get(name, 0.1)), bytes_accessed=1, transcendentals=0),
         )(array, *extra)
         self.last = [token]
         return held
@@ -111,33 +111,25 @@
 
 
 def pack_kernel(phase_ref, k_ref, v_ref, *refs):
-    if len(refs) == 5:
-        kv_ref, pick_ref, kv_buf, in_sem, out_sem = refs
-        inward = []
+    if len(refs) == 4:
+        kv_ref, pick_ref, phases, sem = refs
+        pairs = []
     else:
-        w_ref, kv_ref, pick_ref, piece_ref, kv_buf, piece_buf, in_sem, out_sem = refs
+        w_ref, kv_ref, pick_ref, piece_ref, phases, sem = refs
         cols = piece_ref.shape[1]
         start = (1 - lax.axis_index("head")) * 2 * cols + lax.axis_index("ctx") % 2 * cols
-        inward = [(w_ref.at[:, pl.ds(pl.multiple_of(start, cols), cols)], piece_buf)]
+        pairs = [(w_ref.at[:, pl.ds(pl.multiple_of(start, cols), cols)], piece_ref)]
     rows = k_ref.shape[0]
-    inward = [(k_ref, kv_buf.at[pl.ds(0, rows)]), (v_ref, kv_buf.at[pl.ds(rows, rows)])] + inward
-    outward = []
+    pairs = [(phase_ref, phases), (k_ref, kv_ref.at[pl.ds(0, rows)]), (v_ref, kv_ref.at[pl.ds(rows, rows)])] + pairs
+    copies = run_copies(pairs, sem)
+    for copy in copies[:3]:
+        copy.wait()
     for r in range(2):
         for part in range(2):
-            start = pl.multiple_of(part * rows + (STRIDE - 1 - phase_ref[r]) * BLOCK_TOKENS, BLOCK_TOKENS)
+            start = pl.multiple_of(part * rows + (STRIDE - 1 - phases[r]) * BLOCK_TOKENS, BLOCK_TOKENS)
             at = (2 * r + part) * BLOCK_TOKENS
-            outward.append((kv_buf.at[pl.ds(start, BLOCK_TOKENS)], pick_ref.at[pl.ds(at, BLOCK_TOKENS)]))
-    outward.append((kv_buf, kv_ref))
-    coming = run_copies(inward, in_sem)
-    coming[0].wait()
-    coming[1].wait()
-    going = run_copies(outward, out_sem)
-    for copy in coming[2:]:
-        copy.wait()
-        last = pltpu.make_async_copy(piece_buf, piece_ref, out_sem.at[len(outward)])
-        last.start()
-        going.append(last)
-    for copy in going:
+            pick_ref[at : at + BLOCK_TOKENS] = kv_ref[pl.ds(start, BLOCK_TOKENS)]
+    for copy in copies[3:]:
         copy.wait()
 
 
@@ -180,13 +172,15 @@
     return jnp.concatenate([ref[rows, :HEAD_SIZE], ref[rows, HEAD_SIZE:]], axis=0)
 
 
-def band_forward_kernel(q_ref, own_ref, core_ref, two_ref, two_core_ref, out_ref, max_ref, sum_ref, k_win, v_win, s_buf, p_buf):
+def band_forward_kernel(phase_ref, q_ref, own_ref, core_ref, two_ref, two_core_ref, out_ref, max_ref, sum_ref, first_ref, k_win, v_win, s_buf, p_buf):
     ctx = lax.axis_index("ctx")
     core = ctx % 2
     tiles = q_ref.shape[0] // TILE
     chunks = 2 * tiles + 1
     load_window(core, own_ref, core_ref, two_ref, two_core_ref, 0, k_win)
     load_window(core, own_ref, core_ref, two_ref, two_core_ref, 1, v_win)
+    for r in range(2):
+        first_ref[r : r + 1, :] = jnp.full((1, first_ref.shape[1]), (STRIDE - 1 - phase_ref[r]) * BLOCK_TOKENS, jnp.int32)
     for tile in range(tiles):
         q_tile = both_heads(q_ref, tile)
         top = None
@@ -261,49 +255,66 @@
         out[slot * BLOCK_TOKENS : (slot + 1) * BLOCK_TOKENS] = source[start : start + BLOCK_TOKENS]
 
 
-def slot_scores(ctx, slot, order, phase, token_start, s):
+def slot_scores(ctx, slot, order, nearest, token_start, s):
     owner = slot_owner(ctx, slot, order)
     token = token_start + lax.broadcasted_iota(jnp.int32, s.shape, 1)
-    first = jnp.where(owner < ctx - 2, 0, jnp.where(owner == ctx - 2, (STRIDE - 1 - phase) * BLOCK_TOKENS, 2**30))
+    first = jnp.where(owner < ctx - 2, 0, jnp.where(owner == ctx - 2, nearest, 2**30))
     return jnp.where(token >= first, s, MASKED)
 
 
-def stride_forward_kernel(order, phase_ref, q_ref, mine_ref, other_ref, out_in_ref, max_in_ref, sum_in_ref, att_ref, lse_ref, k_pick, v_pick, s_buf, p_buf):
+def stride_forward_kernel(order, first_ref, q_ref, mine_ref, other_ref, out_in_ref, max_in_ref, sum_in_ref, att_ref, lse_ref, k_pick, v_pick, s_buf, p_buf):
     ctx = lax.axis_index("ctx")
     rows = q_ref.shape[0]
-    slots = k_pick.shape[0] // BLOCK_TOKENS
+    slots = k_pick.shape[1] // BLOCK_TOKENS
     width = 2 * TILE
+    steps = [(r, token_start) for r in range(2) for token_start in range(0, rows, width)]
     for r in range(2):
-        load_picked(mine_ref, other_ref, r, 0, k_pick)
-        load_picked(mine_ref, other_ref, r, 1, v_pick)
-        for token_start in range(0, rows, width):
-            at = slice(token_start, token_start + width)
-            q_tile = q_ref[at, r * HEAD_SIZE : (r + 1) * HEAD_SIZE]
-            old = max_in_ref[r : r + 1, at]
-            top = None
-            for slot in range(slots):
-                piece = slice(slot * BLOCK_TOKENS, (slot + 1) * BLOCK_TOKENS)
-                s = slot_scores(ctx, slot, order, phase_ref[r], token_start, mm(k_pick[piece], q_tile, NT))
-                s_buf[piece] = s
-                here = jnp.max(s.reshape(BLOCK_TOKENS // 8, 8, width), axis=0)
-                top = here if top is None else jnp.maximum(top, here)
-            top = jnp.maximum(jnp.max(top, axis=0, keepdims=True), old)
-            total = None
-            for slot in range(slots):
-                piece = slice(slot * BLOCK_TOKENS, (slot + 1) * BLOCK_TOKENS)
-                p = jnp.exp2((s_buf[piece] - top) * EXP2_SCALE)
-                here = jnp.sum(p.reshape(BLOCK_TOKENS // 8, 8, width), axis=0)
-                total = here if total is None else total + here
-                p_buf[piece] = p.astype(BF16)
-            factor = jnp.exp2((old - top) * EXP2_SCALE)
-            total = jnp.sum(total, axis=0, keepdims=True) + sum_in_ref[r : r + 1, at] * factor
-            out = mm(v_pick[...], p_buf[...], TN) + out_in_ref[r, :, at] * factor
-            out = out / total
-            att_ref[at, r * HEAD_SIZE : (r + 1) * HEAD_SIZE] = out.T.astype(BF16)
-            lse_ref[r : r + 1, at] = top + jnp.log2(total) * (1.0 / EXP2_SCALE)
-
-
-def stride_backward_kernel(order, phase_ref, q_ref, grad_own_ref, grad_got_ref, att_ref, lse_ref, mine_ref, other_ref, do_ref, dot_ref, dq_ref, keep_ref, send_ref, k_pick, v_pick, p_buf, ds_buf):
+        load_picked(mine_ref, other_ref, r, 0, k_pick.at[r])
+        load_picked(mine_ref, other_ref, r, 1, v_pick.at[r])
+
+    def scores(step):
+        r, token_start = steps[step]
+        q_tile = q_ref[token_start : token_start + width, r * HEAD_SIZE : (r + 1) * HEAD_SIZE]
+        s_buf[step] = mm(k_pick[r], q_tile, NT)
+
+    def weigh(step):
+        r, token_start = steps[step]
+        at = slice(token_start, token_start + width)
+        old = max_in_ref[r : r + 1, at]
+        top = None
+        for slot in range(slots):
+            piece = slice(slot * BLOCK_TOKENS, (slot + 1) * BLOCK_TOKENS)
+            s = slot_scores(ctx, slot, order, first_ref[r : r + 1, at], token_start, s_buf[step, piece])
+            s_buf[step, piece] = s
+            here = jnp.max(s.reshape(BLOCK_TOKENS // 8, 8, width), axis=0)
+            top = here if top is None else jnp.maximum(top, here)
+        top = jnp.maximum(jnp.max(top, axis=0, keepdims=True), old)
+        total = None
+        for slot in range(slots):
+            piece = slice(slot * BLOCK_TOKENS, (slot + 1) * BLOCK_TOKENS)
+            p = jnp.exp2((s_buf[step, piece] - top) * EXP2_SCALE)
+            here = jnp.sum(p.reshape(BLOCK_TOKENS // 8, 8, width), axis=0)
+            total = here if total is None else total + here
+            p_buf[step, piece] = p.astype(BF16)
+        factor = jnp.exp2((old - top) * EXP2_SCALE)
+        total = jnp.sum(total, axis=0, keepdims=True) + sum_in_ref[r : r + 1, at] * factor
+        lse_ref[r : r + 1, at] = top + jnp.log2(total) * (1.0 / EXP2_SCALE)
+        return factor, total
+
+    def mix(step, factor, total):
+        r, token_start = steps[step]
+        at = slice(token_start, token_start + width)
+        out = mm(v_pick[r], p_buf[step], TN) + out_in_ref[r, :, at] * factor
+        att_ref[at, r * HEAD_SIZE : (r + 1) * HEAD_SIZE] = (out / total).T.astype(BF16)
+
+    scores(0)
+    for step in range(len(steps)):
+        if step + 1 < len(steps):
+            scores(step + 1)
+        mix(step, *weigh(step))
+
+
+def stride_backward_kernel(order, first_ref, q_ref, grad_own_ref, grad_got_ref, att_ref, lse_ref, mine_ref, other_ref, do_ref, dot_ref, dq_ref, keep_ref, send_ref, k_pick, v_pick, p_buf, ds_buf, s_buf, dp_buf):
     ctx = lax.axis_index("ctx")
     rows = q_ref.shape[0]
     slots = k_pick.shape[0] // BLOCK_TOKENS
@@ -322,13 +333,14 @@
             do_tile = do_ref[at, head]
             lse = lse_ref[r : r + 1, at]
             dot = dot_ref[r : r + 1, at]
+            s_buf[...] = mm(k_pick[...], q_tile, NT)
+            dp_buf[...] = mm(v_pick[...], do_tile, NT)
             for slot in range(slots):
                 piece = slice(slot * BLOCK_TOKENS, (slot + 1) * BLOCK_TOKENS)
-                s = slot_scores(ctx, slot, order, phase_ref[r], token_start, mm(k_pick[piece], q_tile, NT))
+                s = slot_scores(ctx, slot, order, first_ref[r : r + 1, at], token_start, s_buf[piece])
                 p = jnp.exp2((s - lse) * EXP2_SCALE)
-                dp = mm(v_pick[piece], do_tile, NT)
                 p_buf[piece, at] = p.astype(BF16)
-                ds_buf[piece, at] = (p * (dp - dot)).astype(BF16)
+                ds_buf[piece, at] = (p * (dp_buf[piece] - dot)).astype(BF16)
         dv = mm(p_buf[...], do_ref[:, head])
         dk = mm(ds_buf[...], q_ref[:, head]) * SCALE
         dq_ref[r] = mm(k_pick[...], ds_buf[...], TN)
@@ -433,16 +445,14 @@
     low_ref[...] = (left_ref[0].astype(F32) + right_ref[0].astype(F32)).astype(BF16)
 
 
-def choose_kernel(own_ref, own_got_ref, other_ref, keep_ref, send_ref):
+def choose_kernel(own_ref, other_ref, keep_ref, send_ref):
     same = lax.axis_index("ctx") // (lax.axis_size("ctx") // 2) == lax.axis_index("head")
-    own = own_ref[0].astype(F32) + own_got_ref[0].astype(F32)
-    other = other_ref[...].astype(F32)
-    keep_ref[...] = jnp.where(same, own, other)
-    send_ref[...] = jnp.where(same, other, own).astype(BF16)
+    keep_ref[...] = jnp.where(same, own_ref[...], other_ref[...])
+    send_ref[...] = jnp.where(same, other_ref[...], own_ref[...])
 
 
 def last_sum_kernel(keep_ref, got_ref, out_ref):
-    out_ref[...] = (keep_ref[...] + got_ref[...].astype(F32)).astype(BF16)
+    out_ref[...] = (keep_ref[...].astype(F32) + got_ref[...].astype(F32)).astype(BF16)
 
 
 def body(queries, rotated_key_rows, value_head_rows, stride_offset, w_out, grad_out):
@@ -466,10 +476,7 @@
         [stride_offset, rotated_key_rows, value_head_rows] + ([w_out] if pair else []),
         [shape((2 * rows, HEAD_SIZE), BF16), shape((4 * BLOCK_TOKENS, HEAD_SIZE), BF16)]
         + ([shape((head_rows, width // 2), BF16)] if pair else []),
-        [pltpu.VMEM((2 * rows, HEAD_SIZE), BF16)]
-        + ([pltpu.VMEM((head_rows, width // 2), BF16)] if pair else [])
-        + [pltpu.SemaphoreType.DMA((3,)), pltpu.SemaphoreType.DMA((6,))],
-        far=(1, 2, 3) if pair else (1, 2), mib=60, out_space=HBM,
+        [pltpu.SMEM((2,), jnp.int32), pltpu.SemaphoreType.DMA((4,))], far=(0, 1, 2, 3) if pair else (0, 1, 2), mib=54,
     )
     run.last = []
     kv, picks = packed[:2]
@@ -500,18 +507,6 @@
     kv_two = run.hold(kv_two)
     kv_two_core = lax.ppermute(kv_two, "ctx", flip(1))
 
-    chunk_rows = (2 * (rows // TILE) + 1) * TILE
-    window = pltpu.VMEM((3 * rows, HEAD_SIZE), BF16)
-    picked_rows = n_ctx * BLOCK_TOKENS
-    pick = pltpu.VMEM((picked_rows, HEAD_SIZE), BF16)
-    out, top, total = run(
-        band_forward_kernel, "band_forward", [queries, kv, kv_core, kv_two, kv_two_core],
-        [shape((2, HEAD_SIZE, rows), F32), shape((2, rows), F32), shape((2, rows), F32)],
-        [window, window, pltpu.VMEM((chunk_rows, 2 * TILE), F32), pltpu.VMEM((chunk_rows, 2 * TILE), BF16)],
-        flops=2 * scores * chunk_rows,
-    )
-    picks = join(run, "stride_join", picks, picks_got)
-    picks_other = lax.ppermute(picks, "ctx", flip(1))
     if pair:
         w_near = run.hold(w_near)
         w_far = lax.ppermute(w_near, "ctx", flip(1))
@@ -520,17 +515,33 @@
             [shape((rows, head_rows), BF16)], flops=proj,
         )
         grad_got = lax.ppermute(grad_other, "head", swap)
+
+    chunk_rows = (2 * (rows // TILE) + 1) * TILE
+    window = pltpu.VMEM((3 * rows, HEAD_SIZE), BF16)
+    picked_rows = n_ctx * BLOCK_TOKENS
+    pick = pltpu.VMEM((picked_rows, HEAD_SIZE), BF16)
+    out, top, total, first = run(
+        band_forward_kernel, "band_forward", [stride_offset, queries, kv, kv_core, kv_two, kv_two_core],
+        [shape((2, HEAD_SIZE, rows), F32), shape((2, rows), F32), shape((2, rows), F32), shape((2, rows), jnp.int32)],
+        [window, window, pltpu.VMEM((chunk_rows, 2 * TILE), F32), pltpu.VMEM((chunk_rows, 2 * TILE), BF16)],
+        flops=2 * scores * chunk_rows,
+    )
+    picks = join(run, "stride_join", picks, picks_got)
+    picks_other = lax.ppermute(picks, "ctx", flip(1))
     if not pair:
         grad_all = mm(grad_out, w_all, NT).astype(BF16)
         grad_all = lax.all_to_all(grad_all.reshape(rows, n_head, head_rows), "head", 1, 0, tiled=True)
         grad_all = grad_all.reshape(n_head, rows, head_rows).astype(F32)
         grad_own = jnp.sum(grad_all, axis=0)
         grad_got = jnp.zeros((rows, head_rows), BF16)
+    if pair:
+        grad_got = run.hold(grad_got, "hold_grad")
     attended, lse = run(
         functools.partial(stride_forward_kernel, order), "stride_forward",
-        [stride_offset, queries, picks, picks_other, out, top, total],
+        [first, queries, picks, picks_other, out, top, total],
         [shape((rows, head_rows), BF16), shape((2, rows), F32)],
-        [pick, pick, pltpu.VMEM((picked_rows, 2 * TILE), F32), pltpu.VMEM((picked_rows, 2 * TILE), BF16)],
+        [pltpu.VMEM((2, picked_rows, HEAD_SIZE), BF16)] * 2
+        + [pltpu.VMEM((rows // TILE, picked_rows, 2 * TILE), F32), pltpu.VMEM((rows // TILE, picked_rows, 2 * TILE), BF16)],
         flops=2 * scores * picked_rows,
     )
     if pair:
@@ -539,7 +550,7 @@
         while 2 * bits[-1] < ratio:
             bits.append(2 * bits[-1])
         own_bits = tuple(bits[:1] + bits[:0:-1])
-        other_bits = tuple(bits)
+        other_bits = own_bits
 
         def weight_grad(source, name, bits):
             part = shape((ratio // 2, head_rows, cols), BF16)
@@ -549,27 +560,35 @@
 
         own_keep, own_send = weight_grad(attended, "weight_grad_own", own_bits)
         own_got = lax.ppermute(own_send, "ctx", flip(1))
+    if pair:
+        own_keep, own_send = halve(run, "weight_grad_own_core", own_keep, own_got)
+        own_got = lax.ppermute(own_send, "ctx", flip(own_bits[1]))
     grad_att, row_dot, grad_q, stride_keep, stride_send = run(
         functools.partial(stride_backward_kernel, order), "stride_backward",
-        [stride_offset, queries, grad_own, grad_got, attended, lse, picks, picks_other],
+        [first, queries, grad_own, grad_got, attended, lse, picks, picks_other],
         [
             shape((rows, head_rows), BF16), shape((2, rows), F32), shape((2, HEAD_SIZE, rows), F32),
             shape(picks.shape, BF16), shape(picks.shape, BF16),
         ],
-        [pick, pick, pltpu.VMEM((picked_rows, rows), BF16), pltpu.VMEM((picked_rows, rows), BF16)],
+        [
+            pick, pick, pltpu.VMEM((picked_rows, rows), BF16), pltpu.VMEM((picked_rows, rows), BF16),
+            pltpu.VMEM((picked_rows, 2 * TILE), F32), pltpu.VMEM((picked_rows, 2 * TILE), F32),
+        ],
         flops=5 * scores * picked_rows,
     )
     stride_got = lax.ppermute(stride_send, "ctx", flip(1))
     if pair:
-        own_keep, own_send = halve(run, "weight_grad_own_core", own_keep, own_got, after=[att_other])
-        own_got = lax.ppermute(own_send, "ctx", flip(own_bits[1]))
         other_keep, other_send = weight_grad(att_other, "weight_grad_other", other_bits)
         other_got = lax.ppermute(other_send, "ctx", flip(1))
+    if pair:
+        for bit in own_bits[2:]:
+            own_keep, own_send = halve(run, "weight_grad_own_low", own_keep, own_got)
+            own_got = lax.ppermute(own_send, "ctx", flip(bit))
+    if pair:
+        other_keep, other_send = halve(run, "weight_grad_other_core", other_keep, other_got)
+        other_got = lax.ppermute(other_send, "ctx", flip(other_bits[1]))
     stride_keep, stride_send = halve(run, "stride_core", stride_keep, stride_got)
     stride_got = lax.ppermute(stride_send, "ctx", flip(2))
-    if pair:
-        other_keep, other_send = halve(run, "weight_grad_other_core", other_keep, other_got)
-        other_got = lax.ppermute(other_send, "ctx", flip(other_bits[1]))
     grad_queries, own, one, two = run(
         band_backward_kernel, "band_backward",
         [queries, grad_att, kv, kv_core, kv_two, kv_two_core, lse, row_dot, grad_q],
@@ -583,34 +602,36 @@
     one_got = lax.ppermute(one, "ctx", flip(1))
     stride_bits = list(reversed(order))[1:]
     if pair:
-        for bit in own_bits[2:]:
-            own_keep, own_send = halve(run, "weight_grad_own_low", own_keep, own_got)
-            own_got = lax.ppermute(own_send, "ctx", flip(bit))
-    stride_keep, stride_send = halve(run, "stride_y", stride_keep, stride_got)
-    stride_got = lax.ppermute(stride_send, "ctx", flip(stride_bits[1]))
-    if pair:
         for bit in other_bits[2:]:
             other_keep, other_send = halve(run, "weight_grad_other_low", other_keep, other_got)
             other_got = lax.ppermute(other_send, "ctx", flip(bit))
-    two, = run(functools.partial(add_kernel, 1), "band_two", [two, one_got], [shape(two.shape, BF16)])
-    two_got = lax.ppermute(two, "ctx", [(i + 2, i) for i in range(n_ctx - 2)])
-    if pair:
+    stride_keep, stride_send = halve(run, "stride_y", stride_keep, stride_got)
+    stride_got = lax.ppermute(stride_send, "ctx", flip(stride_bits[1]))
+    if pair:
+        block = (head_rows, cols)
+        own_low, = run(end_kernel, "weight_grad_own_end", [own_keep, own_got], [shape(block, BF16)])
+    if pair:
+        other_low, = run(end_kernel, "weight_grad_other_end", [other_keep, other_got], [shape(block, BF16)])
+        other_got = lax.ppermute(other_low, "head", swap)
+        two, = run(functools.partial(add_kernel, 1), "band_two", [two, one_got], [shape(two.shape, BF16)])
+        two_got = lax.ppermute(two, "ctx", [(i + 2, i) for i in range(n_ctx - 2)])
         layer_out, = run(
             layer_out_kernel, "layer_out", [attended, att_other, w_own, w_near, w_far],
             [shape((rows, width), BF16)], flops=2 * proj,
         )
-    for bit in stride_bits[2:]:
-        stride_keep, stride_send = halve(run, "stride_z", stride_keep, stride_got)
-        stride_got = lax.ppermute(stride_send, "ctx", flip(bit))
-    if pair:
-        block = (head_rows, cols)
-        other_low, = run(end_kernel, "weight_grad_other_end", [other_keep, other_got], [shape(block, BF16)])
-        other_got = lax.ppermute(other_low, "head", swap)
         sum_keep, sum_send = run(
-            choose_kernel, "choose", [own_keep, own_got, other_got], [shape(block, F32), shape(block, BF16)]
+            choose_kernel, "choose", [own_low, other_got], [shape(block, BF16)] * 2
         )
         sum_got = lax.ppermute(sum_send, "ctx", flip(n_ctx // 2))
+        for bit in stride_bits[2:]:
+            stride_keep, stride_send = halve(run, "stride_z", stride_keep, stride_got)
+            stride_got = lax.ppermute(stride_send, "ctx", flip(bit))
     else:
+        two, = run(functools.partial(add_kernel, 1), "band_two", [two, one_got], [shape(two.shape, BF16)])
+        two_got = lax.ppermute(two, "ctx", [(i + 2, i) for i in range(n_ctx - 2)])
+        for bit in stride_bits[2:]:
+            stride_keep, stride_send = halve(run, "stride_z", stride_keep, stride_got)
+            stride_got = lax.ppermute(stride_send, "ctx", flip(bit))
         att_all = lax.all_gather(attended, "head", axis=1, tiled=True)
         layer_out = mm(att_all, w_all).astype(BF16)
         terms = mm(att_all, grad_out, TN).astype(BF16).reshape(n_head, head_rows, ratio, cols)

time: 84.4 us -> 83 us (0.983)
  Pallas kernels: 28.1 us -> 24.1 us
  starting transfers between devices: 32.5 us -> 35.2 us
  local copies, waits for them, and re-layouts: 2.45 us -> 0.88 us
  waiting for transfers between devices: 20.3 us -> 21.7 us
    pallas_call x25 -> x26, Pallas kernels: 28.1 us -> 24.1 us  [__call__(): pl.pallas_call(wrapped, name=name, out_shape=list(out_shapes) + [shape((8...]
    ppermute x1, waiting for transfers between devices: 2.58 us -> 0.01 us  [body(): stride_got = lax.ppermute(stride_send, 'ctx', flip(2))]
    ppermute x1, waiting for transfers between devices: 0.01 us -> 2.48 us  [body(): stride_got = lax.ppermute(stride_send, 'ctx', flip(bit))]
    ppermute x1, starting transfers between devices: 0.33 us -> 2.72 us  [body(): other_got = lax.ppermute(other_send, 'ctx', flip(other_bits[1]))]
    ppermute x1, waiting for transfers between devices: 4.53 us -> 2.31 us  [body(): picks_got = lax.ppermute(picks, 'ctx', flip(bit))]
    ppermute x1, waiting for transfers between devices: 2.4 us -> 4.44 us  [body(): picks_got = lax.ppermute(picks, 'ctx', flip(order[1]))]
    unnamed x12 -> x18, local copies, waits for them, and re-layouts: 2.45 us -> 0.88 us
    ppermute x1, waiting for transfers between devices: 0.24 us -> 1.79 us  [body(): own_got = lax.ppermute(own_send, 'ctx', flip(own_bits[1]))]
  transfers between devices with their start and end apart: 25 -> 25, of which waited for: 11 -> 13; matrix products, arithmetic and copies ran while one was open for 0% -> 0% of each run, Pallas kernels for 28% -> 22%
where the time goes in v3:
time: 83 us; the launch traced here: 82.8 us
  starting transfers between devices  35.2 us (42%)
  Pallas kernels  24.1 us (29%)
  waiting for transfers between devices  21.7 us (26%)
  between operations  0.95 us (1%)
  local copies, waits for them, and re-layouts  0.88 us (1%)
    pallas_call x26, Pallas kernels, __call__(): pl.pallas_call(wrapped, name=name, out_shape=list(out_shapes) + [shape((8...  24.1 us
    ppermute x1, waiting for transfers between devices, body(): picks_got = lax.ppermute(picks, 'ctx', flip(order[1]))  4.44 us
    ppermute x1, starting transfers between devices, body(): sum_got = lax.ppermute(sum_send, 'ctx', flip(n_ctx // 2))  3.49 us
    ppermute x1, starting transfers between devices, body(): stride_got = lax.ppermute(stride_send, 'ctx', flip(stride_bits[1]))  3.44 us
    ppermute x1, starting transfers between devices, body(): kv_two = lax.ppermute(kv, 'ctx', [(i, i + 2) for i in range(n_ctx - 2)])  3.43 us
    ppermute x1, starting transfers between devices, body(): own_got = lax.ppermute(own_send, 'ctx', flip(own_bits[1]))  3.2 us
    ppermute x1, starting transfers between devices, body(): w_near = lax.ppermute(packed[2], 'head', swap)  3 us
    ppermute x1, starting transfers between devices, body(): other_got = lax.ppermute(other_send, 'ctx', flip(other_bits[1]))  2.72 us
  transfers between devices with their start and end apart: 25, of which 13 were waited for; matrix products, arithmetic and copies ran while one was open for 0% of the time, Pallas kernels for 22%

profile of v3, /device:TPU:0, one launch (start us, length us, event | category | flops | bytes accessed | tf_op | source)
XLA Modules:
  0.0 82.8 jit_solution(9476906662396751408)
XLA Ops:
  0.7 2.3 %pack.1 = (bf16[1024,128]{1,0:T(8,128)(2,1)}, bf16[256,128]{1,0:T(8,128)(2,1)}, bf16[256,1024]{1,0:T(8,128)(2,1)}, f32[8,128]{1,0:T(8,128)}) custom-call(s32[2]{0:T(128)} %refs_0_.9, bf16[512,128]{1,0:T(8,128)(2,1)} %refs_1_.5, bf16[512,128]{1,0:T(8,128)(2,1)} %refs_2_.1, bf16[256,4096]{1,0:T(8,128)(2,1)} %refs_1_.6), custom_call_target="tpu_custom_call" | custom-call | flops 2000000000 | bytes 1 | tf_op jit(solution)/shard_map/pack/pallas_call | solution.py:55
  2.9 3.0 %collective-permute-start.5 = (bf16[256,1024]{1,0:T(8,128)(2,1)}, bf16[256,1024]{1,0:T(8,128)(2,1)S(1)}, u32[]{:S(2)}, u32[]{:S(2)}) collective-permute-start(bf16[256,1024]{1,0:T(8,128)(2,1)} %get-tuple-element.95), channel_id=1, source_target_pairs={{0,1},{1,0},{2,3},{3,2},{4,5},{5,4},{6,7},{7,6},{8,9},{9,8},{10,11... | collective-permute-start | bytes 1572872 | tf_op jit(solution)/shard_map/ppermute | solution.py:484
  5.9 1.6 %collective-permute-start.2 = (bf16[256,128]{1,0:T(8,128)(2,1)}, bf16[256,128]{1,0:T(8,128)(2,1)S(1)}, u32[]{:S(2)}, u32[]{:S(2)}) collective-permute-start(bf16[256,128]{1,0:T(8,128)(2,1)} %get-tuple-element.88.refs_0_), channel_id=1, source_target_pairs={{0,8},{2,10},{4,12},{6,14},{8,0},{10,2},{12,4},{14,6},{16,24},{18,... | collective-permute-start | bytes 196616 | tf_op jit(solution)/shard_map/ppermute | solution.py:493
  7.5 3.4 %collective-permute-start.1 = (bf16[1024,128]{1,0:T(8,128)(2,1)}, bf16[1024,128]{1,0:T(8,128)(2,1)S(1)}, u32[]{:S(2)}, u32[]{:S(2)}) collective-permute-start(bf16[1024,128]{1,0:T(8,128)(2,1)} %get-tuple-element.87.refs_2_), channel_id=1, source_target_pairs={{0,4},{2,6},{4,8},{6,10},{8,12},{10,14},{12,16},{14,18},{16,20},{1... | collective-permute-start | bytes 786440 | tf_op jit(solution)/shard_map/ppermute | solution.py:494
  10.9 0.0 copy-start.8
  11.0 0.8 %copy-done.8 = bf16[256,128]{1,0:T(8,128)(2,1)S(1)} copy-done((bf16[256,128]{1,0:T(8,128)(2,1)S(1)}, bf16[256,128]{1,0:T(8,128)(2,1)}, u32[]{:S(2)}) %copy-start.8) | copy-done | bytes 65560
  11.8 2.6 %collective-permute-start.3 = (bf16[512,128]{1,0:T(8,128)(2,1)S(1)}, bf16[512,128]{1,0:T(8,128)(2,1)S(1)}, u32[]{:S(2)}, u32[]{:S(2)}) collective-permute-start(bf16[512,128]{1,0:T(8,128)(2,1)S(1)} %get-tuple-element.89.refs_0_), channel_id=1, source_target_pairs={{0,16},{2,18},{4,20},{6,22},{8,24},{10,26},{12,28},{14,30},{16,0},... | collective-permute-start | bytes 393224 | tf_op jit(solution)/shard_map/ppermute | solution.py:497
  14.5 2.0 %grad_own.1 = (f32[512,256]{1,0:T(8,128)S(1)}, bf16[512,2048]{1,0:T(8,128)(2,1)S(1)}, bf16[256,2048]{1,0:T(8,128)(2,1)S(1)}, f32[8,128]{1,0:T(8,128)S(1)}) custom-call(bf16[512,2048]{1,0:T(8,128)(2,1)S(1)} %copy-done.5, bf16[256,4096]{1,0:T(8,128)(2,1)S(1)} %copy-done.4, f32[8,128]{1,0:T(8,128)S(1)} %get-tuple-element.90.refs_2_, ...), custom_call_target="tpu_custom_call" | custom-call | flops 2000000000 | bytes 1 | tf_op jit(solution)/shard_map/grad_own/pallas_call | solution.py:55
  16.5 4.4 %collective-permute-done.3.refs_1_ = bf16[512,128]{1,0:T(8,128)(2,1)S(1)} collective-permute-done((bf16[512,128]{1,0:T(8,128)(2,1)S(1)}, bf16[512,128]{1,0:T(8,128)(2,1)S(1)}, u32[]{:S(2)}, u32[]{:S(2)}) %collective-permute-start.3) | collective-permute-done | bytes 131104 | tf_op jit(solution)/shard_map/ppermute | solution.py:497
  20.9 0.0 copy-start.2
  21.0 0.0 copy-start.6
  21.0 0.0 copy-start.7
  21.0 0.0 collective-permute-done.5.refs_0_
  21.0 0.1 collective-permute-start.6
  21.1 0.5 collective-permute-start.4
  21.6 1.0 %collective-permute-start.7 = (bf16[1024,128]{1,0:T(8,128)(2,1)S(1)}, bf16[1024,128]{1,0:T(8,128)(2,1)S(1)}, u32[]{:S(2)}, u32[]{:S(2)}) collective-permute-start(bf16[1024,128]{1,0:T(8,128)(2,1)S(1)} %get-tuple-element.101.refs_0_), channel_id=1, source_target_pairs={{0,4},{2,6},{4,0},{6,2},{8,12},{10,14},{12,8},{14,10},{16,20},{18,... | collective-permute-start | bytes 786440 | tf_op jit(solution)/shard_map/ppermute | solution.py:506
  22.6 0.4 collective-permute-done.6.refs_2_.refs_4_
  23.0 0.7 grad_other.1
  23.8 0.6 collective-permute-start.9
  24.4 0.0 collective-permute-done.4.refs_5_
  24.4 3.2 %band_forward.1 = (f32[2,128,512]{2,1,0:T(8,128)S(1)}, f32[2,512]{1,0:T(2,128)S(1)}, f32[2,512]{1,0:T(2,128)S(1)}, s32[2,512]{1,0:T(2,128)S(1)}, f32[8,128]{1,0:T(8,128)S(1)}) custom-call(s32[2]{0:T(128)S(1)} %copy-done.2, bf16[512,256]{1,0:T(8,128)(2,1)S(1)} %copy-done.6, bf16[1024,128]{1,0:T(8,128)(2,1)S(1)} %copy-done.7, ...), custom_call_target="tpu_custom_call" | custom-call | flops 2700000000 | bytes 1 | tf_op jit(solution)/shard_map/band_forward/pallas_call | solution.py:55
  27.6 2.3 %collective-permute-done.7.refs_1_ = bf16[1024,128]{1,0:T(8,128)(2,1)S(1)} collective-permute-done((bf16[1024,128]{1,0:T(8,128)(2,1)S(1)}, bf16[1024,128]{1,0:T(8,128)(2,1)S(1)}, u32[]{:S(2)}, u32[]{:S(2)}) %collective-permute-start.7) | collective-permute-done | bytes 262176 | tf_op jit(solution)/shard_map/ppermute | solution.py:506
  29.9 0.1 collective-permute-start.8
  30.0 2.2 %collective-permute-done.9.refs_0_ = bf16[512,256]{1,0:T(8,128)(2,1)S(1)} collective-permute-done((bf16[512,256]{1,0:T(8,128)(2,1)S(1)}, bf16[512,256]{1,0:T(8,128)(2,1)S(1)}, u32[]{:S(2)}, u32[]{:S(2)}) %collective-permute-start.9) | collective-permute-done | bytes 262176 | tf_op jit(solution)/shard_map/ppermute | solution.py:517
  32.2 0.0 collective-permute-done.8.refs_3_.refs_7_
  32.2 2.1 %stride_forward.1 = (bf16[512,256]{1,0:T(8,128)(2,1)S(1)}, f32[2,512]{1,0:T(2,128)S(1)}, f32[8,128]{1,0:T(8,128)S(1)}) custom-call(s32[2,512]{1,0:T(2,128)S(1)} %get-tuple-element.100.refs_0_, bf16[512,256]{1,0:T(8,128)(2,1)S(1)} %copy-done.6, bf16[2048,128]{1,0:T(8,128)(2,1)S(1)} %get-tuple-element.103.refs_2_.refs_6_, ...), custom_call_target="tpu_custom_call" | custom-call | flops 35999997952 | bytes 1 | tf_op jit(solution)/shard_map/stride_forward/pallas_call | solution.py:55
  34.2 0.7 weight_grad_own.1
  35.0 0.1 collective-permute-start.11
  35.1 0.6 collective-permute-start.10
  35.7 1.3 %collective-permute-done.11.refs_1_ = bf16[4,256,256]{2,1,0:T(8,128)(2,1)S(1)} collective-permute-done((bf16[4,256,256]{2,1,0:T(8,128)(2,1)S(1)}, bf16[4,256,256]{2,1,0:T(8,128)(2,1)S(1)}, u32[]{:S(2)}, u32[]{:S(2)}) %collective-permute-start.11) | collective-permute-done | bytes 524320 | tf_op jit(solution)/shard_map/ppermute | solution.py:562
  37.0 0.1 weight_grad_own_core.1
  37.1 3.2 %collective-permute-start.14 = (bf16[2,256,256]{2,1,0:T(8,128)(2,1)S(1)}, bf16[2,256,256]{2,1,0:T(8,128)(2,1)S(1)}, u32[]{:S(2)}, u32[]{:S(2)}) collective-permute-start(bf16[2,256,256]{2,1,0:T(8,128)(2,1)S(1)} %get-tuple-element.129), channel_id=1, source_target_pairs={{0,8},{2,10},{4,12},{6,14},{8,0},{10,2},{12,4},{14,6},{16,24},{18,... | collective-permute-start | bytes 786440 | tf_op jit(solution)/shard_map/ppermute | solution.py:565
  40.3 2.7 %stride_backward.1 = (bf16[512,256]{1,0:T(8,128)(2,1)S(1)}, f32[2,512]{1,0:T(2,128)S(1)}, f32[2,128,512]{2,1,0:T(8,128)S(1)}, bf16[2048,128]{1,0:T(8,128)(2,1)S(...) custom-call(s32[2,512]{1,0:T(2,128)S(1)} %get-tuple-element.100.refs_0_, bf16[512,256]{1,0:T(8,128)(2,1)S(1)} %copy-done.6, ...), custom_call_target="tpu_custom_call" | custom-call | flops 46000001024 | bytes 1 | tf_op jit(solution)/shard_map/stride_backward/pallas_call | solution.py:55
  43.0 0.8 collective-permute-done.10.refs_0_.refs_1_
  43.8 0.7 weight_grad_other.1
  44.6 0.1 collective-permute-start.13
  44.6 0.5 collective-permute-start.12
  45.1 1.8 %collective-permute-done.14.refs_1_ = bf16[2,256,256]{2,1,0:T(8,128)(2,1)S(1)} collective-permute-done((bf16[2,256,256]{2,1,0:T(8,128)(2,1)S(1)}, bf16[2,256,256]{2,1,0:T(8,128)(2,1)S(1)}, u32[]{:S(2)}, u32[]{:S(2)}) %collective-permute-start.14) | collective-permute-done | bytes 262176 | tf_op jit(solution)/shard_map/ppermute | solution.py:565
  46.9 0.1 weight_grad_own_low.1
  47.0 0.1 weight_grad_other_core.1
  47.1 2.7 %collective-permute-start.16 = (bf16[2,256,256]{2,1,0:T(8,128)(2,1)S(1)}, bf16[2,256,256]{2,1,0:T(8,128)(2,1)S(1)}, u32[]{:S(2)}, u32[]{:S(2)}) collective-permute-start(bf16[2,256,256]{2,1,0:T(8,128)(2,1)S(1)} %get-tuple-element.137), channel_id=1, source_target_pairs={{0,8},{2,10},{4,12},{6,14},{8,0},{10,2},{12,4},{14,6},{16,24},{18,... | collective-permute-start | bytes 786440 | tf_op jit(solution)/shard_map/ppermute | solution.py:589
  49.8 0.1 stride_core.1
  50.0 1.8 %collective-permute-start.19 = (bf16[1024,128]{1,0:T(8,128)(2,1)S(1)}, bf16[1024,128]{1,0:T(8,128)(2,1)S(1)}, u32[]{:S(2)}, u32[]{:S(2)}) collective-permute-start(bf16[1024,128]{1,0:T(8,128)(2,1)S(1)} %get-tuple-element.144), channel_id=1, source_target_pairs={{0,4},{2,6},{4,0},{6,2},{8,12},{10,14},{12,8},{14,10},{16,20},{18,... | collective-permute-start | bytes 786440 | tf_op jit(solution)/shard_map/ppermute | solution.py:591
  51.8 4.1 %band_backward.1 = (bf16[512,256]{1,0:T(8,128)(2,1)}, bf16[1024,128]{1,0:T(8,128)(2,1)S(1)}, bf16[1024,128]{1,0:T(8,128)(2,1)S(1)}, bf16[1024,128]{1,0:T(8,128)(2,1)S(1)}, f32[8,128]{1,0:T(8,128)S(1)}) custom-call(bf16[512,256]{1,0:T(8,128)(2,1)S(1)} %copy-done.6, bf16[512,256]{1,0:T(8,128)(2,1)S(1)} %get-tuple-element.120.refs_1_, ...), custom_call_target="tpu_custom_call" | custom-call | flops 40000000000 | bytes 1 | tf_op jit(solution)/shard_map/band_backward/pallas_call | solution.py:55
  55.9 0.3 collective-permute-start.18
  56.2 0.3 collective-permute-done.16.refs_1_
  56.5 0.1 weight_grad_other_low.1
  56.5 1.8 %collective-permute-start.17 = (bf16[1,256,256]{2,1,0:T(8,128)(2,1)S(1)}, bf16[1,256,256]{2,1,0:T(8,128)(2,1)S(1)}, u32[]{:S(2)}, u32[]{:S(2)}) collective-permute-start(bf16[1,256,256]{2,1,0:T(8,128)(2,1)S(1)} %get-tuple-element.140), channel_id=1, source_target_pairs={{0,4},{2,6},{4,0},{6,2},{8,12},{10,14},{12,8},{14,10},{16,20},{18,... | collective-permute-start | bytes 393224 | tf_op jit(solution)/shard_map/ppermute | solution.py:607
  58.3 0.1 stride_y.1
  58.4 3.4 %collective-permute-start.21 = (bf16[512,128]{1,0:T(8,128)(2,1)S(1)}, bf16[512,128]{1,0:T(8,128)(2,1)S(1)}, u32[]{:S(2)}, u32[]{:S(2)}) collective-permute-start(bf16[512,128]{1,0:T(8,128)(2,1)S(1)} %get-tuple-element.155), channel_id=1, source_target_pairs={{0,16},{2,18},{4,20},{6,22},{8,24},{10,26},{12,28},{14,30},{16,0},... | collective-permute-start | bytes 393224 | tf_op jit(solution)/shard_map/ppermute | solution.py:609
  61.8 0.3 collective-permute-done.18.refs_1_
  62.2 2.4 %collective-permute-done.17.refs_1_ = bf16[1,256,256]{2,1,0:T(8,128)(2,1)S(1)} collective-permute-done((bf16[1,256,256]{2,1,0:T(8,128)(2,1)S(1)}, bf16[1,256,256]{2,1,0:T(8,128)(2,1)S(1)}, u32[]{:S(2)}, u32[]{:S(2)}) %collective-permute-start.17) | collective-permute-done | bytes 131104 | tf_op jit(solution)/shard_map/ppermute | solution.py:607
  64.6 0.6 collective-permute-start.22
  65.2 0.1 band_two.1
  65.3 1.3 %collective-permute-start.20 = (bf16[1024,128]{1,0:T(8,128)(2,1)S(1)}, bf16[1024,128]{1,0:T(8,128)(2,1)S(1)}, u32[]{:S(2)}, u32[]{:S(2)}) collective-permute-start(bf16[1024,128]{1,0:T(8,128)(2,1)S(1)} %get-tuple-element.153), channel_id=1, source_target_pairs={{4,0},{6,2},{8,4},{10,6},{12,8},{14,10},{16,12},{18,14},{20,16},{2... | collective-permute-start | bytes 786440 | tf_op jit(solution)/shard_map/ppermute | solution.py:617
  66.6 0.0 copy-start.3
  66.6 2.6 %layer_out.1 = (bf16[512,2048]{1,0:T(8,128)(2,1)}, f32[8,128]{1,0:T(8,128)S(1)}) custom-call(bf16[512,256]{1,0:T(8,128)(2,1)S(1)} %get-tuple-element.110.refs_0_.refs_4_, bf16[512,256]{1,0:T(8,128)(2,1)S(1)} %collective-permute-done.10.refs_0_.refs_1_, bf16[256,2048]{1,0:T(8,128)(2,1)S(1)} %get-tuple-element.111.refs_2_, ...), custom_call_target="tpu_custom_call" | custom-call | flops 25999998976 | bytes 1 | tf_op jit(solution)/shard_map/layer_out/pallas_call | solution.py:55
  69.2 0.6 collective-permute-done.22.refs_1_
  69.8 3.5 %collective-permute-start.24 = (bf16[256,256]{1,0:T(8,128)(2,1)S(1)}, bf16[256,256]{1,0:T(8,128)(2,1)S(1)}, u32[]{:S(2)}, u32[]{:S(2)}) collective-permute-start(bf16[256,256]{1,0:T(8,128)(2,1)S(1)} %get-tuple-element.166), channel_id=1, source_target_pairs={{0,16},{2,18},{4,20},{6,22},{8,24},{10,26},{12,28},{14,30},{16,0},... | collective-permute-start | bytes 393224 | tf_op jit(solution)/shard_map/ppermute | solution.py:625
  73.4 2.4 %collective-permute-start.23 = (bf16[256,128]{1,0:T(8,128)(2,1)S(1)}, bf16[256,128]{1,0:T(8,128)(2,1)S(1)}, u32[]{:S(2)}, u32[]{:S(2)}) collective-permute-start(bf16[256,128]{1,0:T(8,128)(2,1)S(1)} %get-tuple-element.161), channel_id=1, source_target_pairs={{0,8},{2,10},{4,12},{6,14},{8,0},{10,2},{12,4},{14,6},{16,24},{18,... | collective-permute-start | bytes 196616 | tf_op jit(solution)/shard_map/ppermute | solution.py:628
  75.8 2.5 %collective-permute-done.23.refs_5_ = bf16[256,128]{1,0:T(8,128)(2,1)S(1)} collective-permute-done((bf16[256,128]{1,0:T(8,128)(2,1)S(1)}, bf16[256,128]{1,0:T(8,128)(2,1)S(1)}, u32[]{:S(2)}, u32[]{:S(2)}) %collective-permute-start.23) | collective-permute-done | bytes 65568 | tf_op jit(solution)/shard_map/ppermute | solution.py:628
  78.2 1.4 %finish.1 = (bf16[512,128]{1,0:T(8,128)(2,1)}, bf16[512,128]{1,0:T(8,128)(2,1)}, f32[8,128]{1,0:T(8,128)S(1)}) custom-call(s32[2]{0:T(128)S(1)} %copy-done.3, bf16[1024,128]{1,0:T(8,128)(2,1)S(1)} %get-tuple-element.152.refs_1_, bf16[1024,128]{1,0:T(8,128)(2,1)S(1)} %collective-permute-done.15.refs_1_.refs_2_, ...), custom_call_target="tpu_custom_call" | custom-call | flops 100000000 | bytes 1 | tf_op jit(solution)/shard_map/finish/pallas_call | solution.py:55
  79.7 2.4 %collective-permute-done.24.refs_1_ = bf16[256,256]{1,0:T(8,128)(2,1)S(1)} collective-permute-done((bf16[256,256]{1,0:T(8,128)(2,1)S(1)}, bf16[256,256]{1,0:T(8,128)(2,1)S(1)}, u32[]{:S(2)}, u32[]{:S(2)}) %collective-permute-start.24) | collective-permute-done | bytes 131104 | tf_op jit(solution)/shard_map/ppermute | solution.py:625
  82.1 0.7 last_sum.1
  (33 shorter events, 0.2 us)
Async XLA Ops:
  0.6 13.8 %copy-start.4 = (bf16[256,4096]{1,0:T(8,128)(2,1)S(1)}, bf16[256,4096]{1,0:T(8,128)(2,1)}, u32[]{:S(2)}) copy-start(bf16[256,4096]{1,0:T(8,128)(2,1)} %refs_1_.6) | copy-start | bytes 6291460
  0.6 13.8 %copy-start.5 = (bf16[512,2048]{1,0:T(8,128)(2,1)S(1)}, bf16[512,2048]{1,0:T(8,128)(2,1)}, u32[]{:S(2)}) copy-start(bf16[512,2048]{1,0:T(8,128)(2,1)} %refs_0_.6) | copy-start | bytes 6291460
  2.9 18.1 %collective-permute-start.5 = (bf16[256,1024]{1,0:T(8,128)(2,1)}, bf16[256,1024]{1,0:T(8,128)(2,1)S(1)}, u32[]{:S(2)}, u32[]{:S(2)}) collective-permute-start(bf16[256,1024]{1,0:T(8,128)(2,1)} %get-tuple-element.95), channel_id=1, source_target_pairs={{0,1},{1,0},{2,3},{3,2},{4,5},{5,4},{6,7},{7,6},{8,9},{9,8},{10,11... | collective-permute-start | bytes 1572872 | tf_op jit(solution)/shard_map/ppermute | solution.py:484
  5.9 8.5 %collective-permute-start = (bf16[1024,128]{1,0:T(8,128)(2,1)}, bf16[1024,128]{1,0:T(8,128)(2,1)S(1)}, u32[]{:S(2)}, u32[]{:S(2)}) collective-permute-start(bf16[1024,128]{1,0:T(8,128)(2,1)} %get-tuple-element.87.refs_2_), channel_id=1, source_target_pairs={{0,2},{2,0},{4,6},{6,4},{8,10},{10,8},{12,14},{14,12},{16,18},{18,... | collective-permute-start | bytes 786440 | tf_op jit(solution)/shard_map/ppermute | solution.py:495
  5.9 5.0 %collective-permute-start.2 = (bf16[256,128]{1,0:T(8,128)(2,1)}, bf16[256,128]{1,0:T(8,128)(2,1)S(1)}, u32[]{:S(2)}, u32[]{:S(2)}) collective-permute-start(bf16[256,128]{1,0:T(8,128)(2,1)} %get-tuple-element.88.refs_0_), channel_id=1, source_target_pairs={{0,8},{2,10},{4,12},{6,14},{8,0},{10,2},{12,4},{14,6},{16,24},{18,... | collective-permute-start | bytes 196616 | tf_op jit(solution)/shard_map/ppermute | solution.py:493
  7.5 13.5 %collective-permute-start.1 = (bf16[1024,128]{1,0:T(8,128)(2,1)}, bf16[1024,128]{1,0:T(8,128)(2,1)S(1)}, u32[]{:S(2)}, u32[]{:S(2)}) collective-permute-start(bf16[1024,128]{1,0:T(8,128)(2,1)} %get-tuple-element.87.refs_2_), channel_id=1, source_target_pairs={{0,4},{2,6},{4,8},{6,10},{8,12},{10,14},{12,16},{14,18},{16,20},{1... | collective-permute-start | bytes 786440 | tf_op jit(solution)/shard_map/ppermute | solution.py:494
  10.9 0.8 %copy-start.8 = (bf16[256,128]{1,0:T(8,128)(2,1)S(1)}, bf16[256,128]{1,0:T(8,128)(2,1)}, u32[]{:S(2)}) copy-start(bf16[256,128]{1,0:T(8,128)(2,1)} %get-tuple-element.88.refs_0_) | copy-start | bytes 196612
  11.8 9.1 %collective-permute-start.3 = (bf16[512,128]{1,0:T(8,128)(2,1)S(1)}, bf16[512,128]{1,0:T(8,128)(2,1)S(1)}, u32[]{:S(2)}, u32[]{:S(2)}) collective-permute-start(bf16[512,128]{1,0:T(8,128)(2,1)S(1)} %get-tuple-element.89.refs_0_), channel_id=1, source_target_pairs={{0,16},{2,18},{4,20},{6,22},{8,24},{10,26},{12,28},{14,30},{16,0},... | collective-permute-start | bytes 393224 | tf_op jit(solution)/shard_map/ppermute | solution.py:497
  20.9 3.4 %copy-start.2 = (s32[2]{0:T(128)S(1)}, s32[2]{0:T(128)}, u32[]{:S(2)}) copy-start(s32[2]{0:T(128)} %refs_0_.9) | copy-start | bytes 28
  21.0 3.4 %copy-start.6 = (bf16[512,256]{1,0:T(8,128)(2,1)S(1)}, bf16[512,256]{1,0:T(8,128)(2,1)}, u32[]{:S(2)}) copy-start(bf16[512,256]{1,0:T(8,128)(2,1)} %refs_0_.8) | copy-start | bytes 786436
  21.0 3.4 %copy-start.7 = (bf16[1024,128]{1,0:T(8,128)(2,1)S(1)}, bf16[1024,128]{1,0:T(8,128)(2,1)}, u32[]{:S(2)}) copy-start(bf16[1024,128]{1,0:T(8,128)(2,1)} %get-tuple-element.87.refs_2_) | copy-start | bytes 786436
  21.0 2.0 %collective-permute-start.6 = (bf16[256,1024]{1,0:T(8,128)(2,1)S(1)}, bf16[256,1024]{1,0:T(8,128)(2,1)S(1)}, u32[]{:S(2)}, u32[]{:S(2)}) collective-permute-start(bf16[256,1024]{1,0:T(8,128)(2,1)S(1)} %get-tuple-element.97.refs_1_.refs_3_), channel_id=1, source_target_pairs={{0,2},{2,0},{4,6},{6,4},{8,10},{10,8},{12,14},{14,12},{16,18},{18,... | collective-permute-start | bytes 1572872 | tf_op jit(solution)/shard_map/ppermute | solution.py:512
  21.1 3.2 %collective-permute-start.4 = (bf16[1024,128]{1,0:T(8,128)(2,1)S(1)}, bf16[1024,128]{1,0:T(8,128)(2,1)S(1)}, u32[]{:S(2)}, u32[]{:S(2)}) collective-permute-start(bf16[1024,128]{1,0:T(8,128)(2,1)S(1)} %get-tuple-element.93.refs_4_), channel_id=1, source_target_pairs={{0,2},{2,0},{4,6},{6,4},{8,10},{10,8},{12,14},{14,12},{16,18},{18,... | collective-permute-start | bytes 786440 | tf_op jit(solution)/shard_map/ppermute | solution.py:508
  21.6 8.3 %collective-permute-start.7 = (bf16[1024,128]{1,0:T(8,128)(2,1)S(1)}, bf16[1024,128]{1,0:T(8,128)(2,1)S(1)}, u32[]{:S(2)}, u32[]{:S(2)}) collective-permute-start(bf16[1024,128]{1,0:T(8,128)(2,1)S(1)} %get-tuple-element.101.refs_0_), channel_id=1, source_target_pairs={{0,4},{2,6},{4,0},{6,2},{8,12},{10,14},{12,8},{14,10},{16,20},{18,... | collective-permute-start | bytes 786440 | tf_op jit(solution)/shard_map/ppermute | solution.py:506
  23.0 4.6 %copy-start = (bf16[256,1024]{1,0:T(8,128)(2,1)}, bf16[256,1024]{1,0:T(8,128)(2,1)S(1)}, u32[]{:S(2)}) copy-start(bf16[256,1024]{1,0:T(8,128)(2,1)S(1)} %collective-permute-done.6.refs_2_.refs_4_) | copy-start | bytes 1572868
  23.8 8.4 %collective-permute-start.9 = (bf16[512,256]{1,0:T(8,128)(2,1)S(1)}, bf16[512,256]{1,0:T(8,128)(2,1)S(1)}, u32[]{:S(2)}, u32[]{:S(2)}) collective-permute-start(bf16[512,256]{1,0:T(8,128)(2,1)S(1)} %get-tuple-element.107), channel_id=1, source_target_pairs={{0,1},{1,0},{2,3},{3,2},{4,5},{5,4},{6,7},{7,6},{8,9},{9,8},{10,11... | collective-permute-start | bytes 786440 | tf_op jit(solution)/shard_map/ppermute | solution.py:517
  29.9 2.2 %collective-permute-start.8 = (bf16[2048,128]{1,0:T(8,128)(2,1)S(1)}, bf16[2048,128]{1,0:T(8,128)(2,1)S(1)}, u32[]{:S(2)}, u32[]{:S(2)}) collective-permute-start(bf16[2048,128]{1,0:T(8,128)(2,1)S(1)} %get-tuple-element.103.refs_2_.refs_6_), channel_id=1, source_target_pairs={{0,2},{2,0},{4,6},{6,4},{8,10},{10,8},{12,14},{14,12},{16,18},{18,... | collective-permute-start | bytes 1572872 | tf_op jit(solution)/shard_map/ppermute | solution.py:530
  35.0 2.0 %collective-permute-start.11 = (bf16[4,256,256]{2,1,0:T(8,128)(2,1)S(1)}, bf16[4,256,256]{2,1,0:T(8,128)(2,1)S(1)}, u32[]{:S(2)}, u32[]{:S(2)}) collective-permute-start(bf16[4,256,256]{2,1,0:T(8,128)(2,1)S(1)} %get-tuple-element.117), channel_id=1, source_target_pairs={{0,2},{2,0},{4,6},{6,4},{8,10},{10,8},{12,14},{14,12},{16,18},{18,... | collective-permute-start | bytes 1572872 | tf_op jit(solution)/shard_map/ppermute | solution.py:562
  35.1 8.7 %collective-permute-start.10 = (bf16[512,256]{1,0:T(8,128)(2,1)S(1)}, bf16[512,256]{1,0:T(8,128)(2,1)S(1)}, u32[]{:S(2)}, u32[]{:S(2)}) collective-permute-start(bf16[512,256]{1,0:T(8,128)(2,1)S(1)} %get-tuple-element.110.refs_0_.refs_4_), channel_id=1, source_target_pairs={{0,1},{1,0},{2,3},{3,2},{4,5},{5,4},{6,7},{7,6},{8,9},{9,8},{10,11... | collective-permute-start | bytes 786440 | tf_op jit(solution)/shard_map/ppermute | solution.py:548
  37.1 9.8 %collective-permute-start.14 = (bf16[2,256,256]{2,1,0:T(8,128)(2,1)S(1)}, bf16[2,256,256]{2,1,0:T(8,128)(2,1)S(1)}, u32[]{:S(2)}, u32[]{:S(2)}) collective-permute-start(bf16[2,256,256]{2,1,0:T(8,128)(2,1)S(1)} %get-tuple-element.129), channel_id=1, source_target_pairs={{0,8},{2,10},{4,12},{6,14},{8,0},{10,2},{12,4},{14,6},{16,24},{18,... | collective-permute-start | bytes 786440 | tf_op jit(solution)/shard_map/ppermute | solution.py:565
  44.6 2.4 %collective-permute-start.13 = (bf16[4,256,256]{2,1,0:T(8,128)(2,1)S(1)}, bf16[4,256,256]{2,1,0:T(8,128)(2,1)S(1)}, u32[]{:S(2)}, u32[]{:S(2)}) collective-permute-start(bf16[4,256,256]{2,1,0:T(8,128)(2,1)S(1)} %get-tuple-element.127), channel_id=1, source_target_pairs={{0,2},{2,0},{4,6},{6,4},{8,10},{10,8},{12,14},{14,12},{16,18},{18,... | collective-permute-start | bytes 1572872 | tf_op jit(solution)/shard_map/ppermute | solution.py:582
  44.6 5.2 %collective-permute-start.12 = (bf16[2048,128]{1,0:T(8,128)(2,1)S(1)}, bf16[2048,128]{1,0:T(8,128)(2,1)S(1)}, u32[]{:S(2)}, u32[]{:S(2)}) collective-permute-start(bf16[2048,128]{1,0:T(8,128)(2,1)S(1)} %get-tuple-element.124), channel_id=1, source_target_pairs={{0,2},{2,0},{4,6},{6,4},{8,10},{10,8},{12,14},{14,12},{16,18},{18,... | collective-permute-start | bytes 1572872 | tf_op jit(solution)/shard_map/ppermute | solution.py:579
  47.1 9.3 %collective-permute-start.16 = (bf16[2,256,256]{2,1,0:T(8,128)(2,1)S(1)}, bf16[2,256,256]{2,1,0:T(8,128)(2,1)S(1)}, u32[]{:S(2)}, u32[]{:S(2)}) collective-permute-start(bf16[2,256,256]{2,1,0:T(8,128)(2,1)S(1)} %get-tuple-element.137), channel_id=1, source_target_pairs={{0,8},{2,10},{4,12},{6,14},{8,0},{10,2},{12,4},{14,6},{16,24},{18,... | collective-permute-start | bytes 786440 | tf_op jit(solution)/shard_map/ppermute | solution.py:589
  50.0 8.3 %collective-permute-start.19 = (bf16[1024,128]{1,0:T(8,128)(2,1)S(1)}, bf16[1024,128]{1,0:T(8,128)(2,1)S(1)}, u32[]{:S(2)}, u32[]{:S(2)}) collective-permute-start(bf16[1024,128]{1,0:T(8,128)(2,1)S(1)} %get-tuple-element.144), channel_id=1, source_target_pairs={{0,4},{2,6},{4,0},{6,2},{8,12},{10,14},{12,8},{14,10},{16,20},{18,... | collective-permute-start | bytes 786440 | tf_op jit(solution)/shard_map/ppermute | solution.py:591
  55.8 10.8 %copy-start.1 = (bf16[256,1024]{1,0:T(8,128)(2,1)S(1)}, bf16[256,1024]{1,0:T(8,128)(2,1)}, u32[]{:S(2)}) copy-start(bf16[256,1024]{1,0:T(8,128)(2,1)} %copy-done) | copy-start | bytes 1572868
  55.9 9.4 %collective-permute-start.15 = (bf16[1024,128]{1,0:T(8,128)(2,1)S(1)}, bf16[1024,128]{1,0:T(8,128)(2,1)S(1)}, u32[]{:S(2)}, u32[]{:S(2)}) collective-permute-start(bf16[1024,128]{1,0:T(8,128)(2,1)S(1)} %get-tuple-element.135), channel_id=1, source_target_pairs={{0,2},{2,0},{4,6},{6,4},{8,10},{10,8},{12,14},{14,12},{16,18},{18,... | collective-permute-start | bytes 786440 | tf_op jit(solution)/shard_map/ppermute | solution.py:602
  55.9 6.3 %collective-permute-start.18 = (bf16[1,256,256]{2,1,0:T(8,128)(2,1)S(1)}, bf16[1,256,256]{2,1,0:T(8,128)(2,1)S(1)}, u32[]{:S(2)}, u32[]{:S(2)}) collective-permute-start(bf16[1,256,256]{2,1,0:T(8,128)(2,1)S(1)} %get-tuple-element.142), channel_id=1, source_target_pairs={{0,4},{2,6},{4,0},{6,2},{8,12},{10,14},{12,8},{14,10},{16,20},{18,... | collective-permute-start | bytes 393224 | tf_op jit(solution)/shard_map/ppermute | solution.py:586
  56.5 8.1 %collective-permute-start.17 = (bf16[1,256,256]{2,1,0:T(8,128)(2,1)S(1)}, bf16[1,256,256]{2,1,0:T(8,128)(2,1)S(1)}, u32[]{:S(2)}, u32[]{:S(2)}) collective-permute-start(bf16[1,256,256]{2,1,0:T(8,128)(2,1)S(1)} %get-tuple-element.140), channel_id=1, source_target_pairs={{0,4},{2,6},{4,0},{6,2},{8,12},{10,14},{12,8},{14,10},{16,20},{18,... | collective-permute-start | bytes 393224 | tf_op jit(solution)/shard_map/ppermute | solution.py:607
  58.4 15.0 %collective-permute-start.21 = (bf16[512,128]{1,0:T(8,128)(2,1)S(1)}, bf16[512,128]{1,0:T(8,128)(2,1)S(1)}, u32[]{:S(2)}, u32[]{:S(2)}) collective-permute-start(bf16[512,128]{1,0:T(8,128)(2,1)S(1)} %get-tuple-element.155), channel_id=1, source_target_pairs={{0,16},{2,18},{4,20},{6,22},{8,24},{10,26},{12,28},{14,30},{16,0},... | collective-permute-start | bytes 393224 | tf_op jit(solution)/shard_map/ppermute | solution.py:609
  64.6 5.2 %collective-permute-start.22 = (bf16[256,256]{1,0:T(8,128)(2,1)S(1)}, bf16[256,256]{1,0:T(8,128)(2,1)S(1)}, u32[]{:S(2)}, u32[]{:S(2)}) collective-permute-start(bf16[256,256]{1,0:T(8,128)(2,1)S(1)} %get-tuple-element.157), channel_id=1, source_target_pairs={{0,1},{1,0},{2,3},{3,2},{4,5},{5,4},{6,7},{7,6},{8,9},{9,8},{10,11... | collective-permute-start | bytes 393224 | tf_op jit(solution)/shard_map/ppermute | solution.py:615
  65.3 12.9 %collective-permute-start.20 = (bf16[1024,128]{1,0:T(8,128)(2,1)S(1)}, bf16[1024,128]{1,0:T(8,128)(2,1)S(1)}, u32[]{:S(2)}, u32[]{:S(2)}) collective-permute-start(bf16[1024,128]{1,0:T(8,128)(2,1)S(1)} %get-tuple-element.153), channel_id=1, source_target_pairs={{4,0},{6,2},{8,4},{10,6},{12,8},{14,10},{16,12},{18,14},{20,16},{2... | collective-permute-start | bytes 786440 | tf_op jit(solution)/shard_map/ppermute | solution.py:617
  66.6 11.6 %copy-start.3 = (s32[2]{0:T(128)S(1)}, s32[2]{0:T(128)}, u32[]{:S(2)}) copy-start(s32[2]{0:T(128)} %refs_0_.9) | copy-start | bytes 28
  69.8 12.3 %collective-permute-start.24 = (bf16[256,256]{1,0:T(8,128)(2,1)S(1)}, bf16[256,256]{1,0:T(8,128)(2,1)S(1)}, u32[]{:S(2)}, u32[]{:S(2)}) collective-permute-start(bf16[256,256]{1,0:T(8,128)(2,1)S(1)} %get-tuple-element.166), channel_id=1, source_target_pairs={{0,16},{2,18},{4,20},{6,22},{8,24},{10,26},{12,28},{14,30},{16,0},... | collective-permute-start | bytes 393224 | tf_op jit(solution)/shard_map/ppermute | solution.py:625
  73.4 4.9 %collective-permute-start.23 = (bf16[256,128]{1,0:T(8,128)(2,1)S(1)}, bf16[256,128]{1,0:T(8,128)(2,1)S(1)}, u32[]{:S(2)}, u32[]{:S(2)}) collective-permute-start(bf16[256,128]{1,0:T(8,128)(2,1)S(1)} %get-tuple-element.161), channel_id=1, source_target_pairs={{0,8},{2,10},{4,12},{6,14},{8,0},{10,2},{12,4},{14,6},{16,24},{18,... | collective-permute-start | bytes 196616 | tf_op jit(solution)/shard_map/ppermute | solution.py:628

commit v4 on v3

--- a/solution.py
+++ b/solution.py
@@ -317,7 +317,7 @@
 def stride_backward_kernel(order, first_ref, q_ref, grad_own_ref, grad_got_ref, att_ref, lse_ref, mine_ref, other_ref, do_ref, dot_ref, dq_ref, keep_ref, send_ref, k_pick, v_pick, p_buf, ds_buf, s_buf, dp_buf):
     ctx = lax.axis_index("ctx")
     rows = q_ref.shape[0]
-    slots = k_pick.shape[0] // BLOCK_TOKENS
+    slots = k_pick.shape[1] // BLOCK_TOKENS
     width = 2 * TILE
     size = 4 * BLOCK_TOKENS
     do_ref[...] = (grad_own_ref[...] + grad_got_ref[...].astype(F32)).astype(BF16)
@@ -325,25 +325,40 @@
         head = slice(r * HEAD_SIZE, (r + 1) * HEAD_SIZE)
         product = do_ref[:, head].astype(F32) * att_ref[:, head].astype(F32)
         dot_ref[r : r + 1, :] = jnp.sum(product.T, axis=0, keepdims=True)
-        load_picked(mine_ref, other_ref, r, 0, k_pick)
-        load_picked(mine_ref, other_ref, r, 1, v_pick)
-        for token_start in range(0, rows, width):
-            at = slice(token_start, token_start + width)
-            q_tile = q_ref[at, head]
-            do_tile = do_ref[at, head]
-            lse = lse_ref[r : r + 1, at]
-            dot = dot_ref[r : r + 1, at]
-            s_buf[...] = mm(k_pick[...], q_tile, NT)
-            dp_buf[...] = mm(v_pick[...], do_tile, NT)
-            for slot in range(slots):
-                piece = slice(slot * BLOCK_TOKENS, (slot + 1) * BLOCK_TOKENS)
-                s = slot_scores(ctx, slot, order, first_ref[r : r + 1, at], token_start, s_buf[piece])
-                p = jnp.exp2((s - lse) * EXP2_SCALE)
-                p_buf[piece, at] = p.astype(BF16)
-                ds_buf[piece, at] = (p * (dp_buf[piece] - dot)).astype(BF16)
-        dv = mm(p_buf[...], do_ref[:, head])
-        dk = mm(ds_buf[...], q_ref[:, head]) * SCALE
-        dq_ref[r] = mm(k_pick[...], ds_buf[...], TN)
+        load_picked(mine_ref, other_ref, r, 0, k_pick.at[r])
+        load_picked(mine_ref, other_ref, r, 1, v_pick.at[r])
+    steps = [(r, token_start) for r in range(2) for token_start in range(0, rows, width)]
+
+    def products(step):
+        r, token_start = steps[step]
+        at = slice(token_start, token_start + width)
+        head = slice(r * HEAD_SIZE, (r + 1) * HEAD_SIZE)
+        s_buf[step] = mm(k_pick[r], q_ref[at, head], NT)
+        dp_buf[step] = mm(v_pick[r], do_ref[at, head], NT)
+
+    def weigh(step):
+        r, token_start = steps[step]
+        at = slice(token_start, token_start + width)
+        lse = lse_ref[r : r + 1, at]
+        dot = dot_ref[r : r + 1, at]
+        for slot in range(slots):
+            piece = slice(slot * BLOCK_TOKENS, (slot + 1) * BLOCK_TOKENS)
+            s = slot_scores(ctx, slot, order, first_ref[r : r + 1, at], token_start, s_buf[step, piece])
+            p = jnp.exp2((s - lse) * EXP2_SCALE)
+            p_buf[r, piece, at] = p.astype(BF16)
+            ds_buf[r, piece, at] = (p * (dp_buf[step, piece] - dot)).astype(BF16)
+
+    products(0)
+    for step, (r, token_start) in enumerate(steps):
+        if step + 1 < len(steps):
+            products(step + 1)
+        weigh(step)
+        if token_start + width < rows:
+            continue
+        head = slice(r * HEAD_SIZE, (r + 1) * HEAD_SIZE)
+        dv = mm(p_buf[r], do_ref[:, head])
+        dk = mm(ds_buf[r], q_ref[:, head]) * SCALE
+        dq_ref[r] = mm(k_pick[r], ds_buf[r], TN)
         for slot in range(slots):
             target = keep_ref if slot < slots // 2 else send_ref
             start = (slot % (slots // 2)) * size + 2 * r * BLOCK_TOKENS
@@ -570,10 +585,10 @@
             shape((rows, head_rows), BF16), shape((2, rows), F32), shape((2, HEAD_SIZE, rows), F32),
             shape(picks.shape, BF16), shape(picks.shape, BF16),
         ],
-        [
-            pick, pick, pltpu.VMEM((picked_rows, rows), BF16), pltpu.VMEM((picked_rows, rows), BF16),
-            pltpu.VMEM((picked_rows, 2 * TILE), F32), pltpu.VMEM((picked_rows, 2 * TILE), F32),
-        ],
+        [pltpu.VMEM((2, picked_rows, HEAD_SIZE), BF16)] * 2
+        + [pltpu.VMEM((2, picked_rows, rows), BF16)] * 2
+        + [pltpu.VMEM((rows // TILE, picked_rows, 2 * TILE), F32)] * 2,
+        mib=min(60, 2 * n_ctx),
         flops=5 * scores * picked_rows,
     )
     stride_got = lax.ppermute(stride_send, "ctx", flip(1))

time: 83 us -> 83 us (level)
  no operation moved by 1% of the time
where the time goes in v4:
time: 83 us; the launch traced here: 82.8 us
  starting transfers between devices  35.1 us (42%)
  Pallas kernels  24.1 us (29%)
  waiting for transfers between devices  21.7 us (26%)
  between operations  0.95 us (1%)
  local copies, waits for them, and re-layouts  0.88 us (1%)
    pallas_call x26, Pallas kernels, __call__(): pl.pallas_call(wrapped, name=name, out_shape=list(out_shapes) + [shape((8...  24.1 us
    ppermute x1, waiting for transfers between devices, body(): picks_got = lax.ppermute(picks, 'ctx', flip(order[1]))  4.44 us
    ppermute x1, starting transfers between devices, body(): sum_got = lax.ppermute(sum_send, 'ctx', flip(n_ctx // 2))  3.48 us
    ppermute x1, starting transfers between devices, body(): stride_got = lax.ppermute(stride_send, 'ctx', flip(stride_bits[1]))  3.44 us
    ppermute x1, starting transfers between devices, body(): kv_two = lax.ppermute(kv, 'ctx', [(i, i + 2) for i in range(n_ctx - 2)])  3.43 us
    ppermute x1, starting transfers between devices, body(): own_got = lax.ppermute(own_send, 'ctx', flip(own_bits[1]))  3.2 us
    ppermute x1, starting transfers between devices, body(): w_near = lax.ppermute(packed[2], 'head', swap)  3 us
    ppermute x1, starting transfers between devices, body(): other_got = lax.ppermute(other_send, 'ctx', flip(other_bits[1]))  2.72 us
  transfers between devices with their start and end apart: 25, of which 13 were waited for; matrix products, arithmetic and copies ran while one was open for 0% of the time, Pallas kernels for 22%

profile of v4, /device:TPU:0, one launch (start us, length us, event | category | flops | bytes accessed | tf_op | source)
XLA Modules:
  0.0 82.8 jit_solution(2779323839047983758)
XLA Ops:
  0.7 2.3 %pack.1 = (bf16[1024,128]{1,0:T(8,128)(2,1)}, bf16[256,128]{1,0:T(8,128)(2,1)}, bf16[256,1024]{1,0:T(8,128)(2,1)}, f32[8,128]{1,0:T(8,128)}) custom-call(s32[2]{0:T(128)} %refs_0_.9, bf16[512,128]{1,0:T(8,128)(2,1)} %refs_1_.5, bf16[512,128]{1,0:T(8,128)(2,1)} %refs_2_.1, bf16[256,4096]{1,0:T(8,128)(2,1)} %refs_1_.6), custom_call_target="tpu_custom_call" | custom-call | flops 2000000000 | bytes 1 | tf_op jit(solution)/shard_map/pack/pallas_call | solution.py:55
  2.9 3.0 %collective-permute-start.5 = (bf16[256,1024]{1,0:T(8,128)(2,1)}, bf16[256,1024]{1,0:T(8,128)(2,1)S(1)}, u32[]{:S(2)}, u32[]{:S(2)}) collective-permute-start(bf16[256,1024]{1,0:T(8,128)(2,1)} %get-tuple-element.95), channel_id=1, source_target_pairs={{0,1},{1,0},{2,3},{3,2},{4,5},{5,4},{6,7},{7,6},{8,9},{9,8},{10,11... | collective-permute-start | bytes 1572872 | tf_op jit(solution)/shard_map/ppermute | solution.py:499
  5.9 0.0 collective-permute-start
  5.9 1.6 %collective-permute-start.2 = (bf16[256,128]{1,0:T(8,128)(2,1)}, bf16[256,128]{1,0:T(8,128)(2,1)S(1)}, u32[]{:S(2)}, u32[]{:S(2)}) collective-permute-start(bf16[256,128]{1,0:T(8,128)(2,1)} %get-tuple-element.88.refs_0_), channel_id=1, source_target_pairs={{0,8},{2,10},{4,12},{6,14},{8,0},{10,2},{12,4},{14,6},{16,24},{18,... | collective-permute-start | bytes 196616 | tf_op jit(solution)/shard_map/ppermute | solution.py:508
  7.5 3.4 %collective-permute-start.1 = (bf16[1024,128]{1,0:T(8,128)(2,1)}, bf16[1024,128]{1,0:T(8,128)(2,1)S(1)}, u32[]{:S(2)}, u32[]{:S(2)}) collective-permute-start(bf16[1024,128]{1,0:T(8,128)(2,1)} %get-tuple-element.87.refs_2_), channel_id=1, source_target_pairs={{0,4},{2,6},{4,8},{6,10},{8,12},{10,14},{12,16},{14,18},{16,20},{1... | collective-permute-start | bytes 786440 | tf_op jit(solution)/shard_map/ppermute | solution.py:509
  10.9 0.0 collective-permute-done.2.refs_1_
  10.9 0.0 copy-start.8
  11.0 0.8 %copy-done.8 = bf16[256,128]{1,0:T(8,128)(2,1)S(1)} copy-done((bf16[256,128]{1,0:T(8,128)(2,1)S(1)}, bf16[256,128]{1,0:T(8,128)(2,1)}, u32[]{:S(2)}) %copy-start.8) | copy-done | bytes 65560
  11.8 2.6 %collective-permute-start.3 = (bf16[512,128]{1,0:T(8,128)(2,1)S(1)}, bf16[512,128]{1,0:T(8,128)(2,1)S(1)}, u32[]{:S(2)}, u32[]{:S(2)}) collective-permute-start(bf16[512,128]{1,0:T(8,128)(2,1)S(1)} %get-tuple-element.89.refs_0_), channel_id=1, source_target_pairs={{0,16},{2,18},{4,20},{6,22},{8,24},{10,26},{12,28},{14,30},{16,0},... | collective-permute-start | bytes 393224 | tf_op jit(solution)/shard_map/ppermute | solution.py:512
  14.4 0.0 collective-permute-done.refs_3_
  14.5 2.0 %grad_own.1 = (f32[512,256]{1,0:T(8,128)S(1)}, bf16[512,2048]{1,0:T(8,128)(2,1)S(1)}, bf16[256,2048]{1,0:T(8,128)(2,1)S(1)}, f32[8,128]{1,0:T(8,128)S(1)}) custom-call(bf16[512,2048]{1,0:T(8,128)(2,1)S(1)} %copy-done.5, bf16[256,4096]{1,0:T(8,128)(2,1)S(1)} %copy-done.4, f32[8,128]{1,0:T(8,128)S(1)} %get-tuple-element.90.refs_2_, ...), custom_call_target="tpu_custom_call" | custom-call | flops 2000000000 | bytes 1 | tf_op jit(solution)/shard_map/grad_own/pallas_call | solution.py:55
  16.5 4.4 %collective-permute-done.3.refs_1_ = bf16[512,128]{1,0:T(8,128)(2,1)S(1)} collective-permute-done((bf16[512,128]{1,0:T(8,128)(2,1)S(1)}, bf16[512,128]{1,0:T(8,128)(2,1)S(1)}, u32[]{:S(2)}, u32[]{:S(2)}) %collective-permute-start.3) | collective-permute-done | bytes 131104 | tf_op jit(solution)/shard_map/ppermute | solution.py:512
  20.9 0.0 copy-start.2
  21.0 0.0 copy-start.6
  21.0 0.0 copy-start.7
  21.0 0.1 collective-permute-start.6
  21.1 0.5 collective-permute-start.4
  21.6 1.0 %collective-permute-start.7 = (bf16[1024,128]{1,0:T(8,128)(2,1)S(1)}, bf16[1024,128]{1,0:T(8,128)(2,1)S(1)}, u32[]{:S(2)}, u32[]{:S(2)}) collective-permute-start(bf16[1024,128]{1,0:T(8,128)(2,1)S(1)} %get-tuple-element.101.refs_0_), channel_id=1, source_target_pairs={{0,4},{2,6},{4,0},{6,2},{8,12},{10,14},{12,8},{14,10},{16,20},{18,... | collective-permute-start | bytes 786440 | tf_op jit(solution)/shard_map/ppermute | solution.py:521
  22.6 0.4 collective-permute-done.6.refs_2_.refs_4_
  23.0 0.7 grad_other.1
  23.8 0.6 collective-permute-start.9
  24.4 3.2 %band_forward.1 = (f32[2,128,512]{2,1,0:T(8,128)S(1)}, f32[2,512]{1,0:T(2,128)S(1)}, f32[2,512]{1,0:T(2,128)S(1)}, s32[2,512]{1,0:T(2,128)S(1)}, f32[8,128]{1,0:T(8,128)S(1)}) custom-call(s32[2]{0:T(128)S(1)} %copy-done.2, bf16[512,256]{1,0:T(8,128)(2,1)S(1)} %copy-done.6, bf16[1024,128]{1,0:T(8,128)(2,1)S(1)} %copy-done.7, ...), custom_call_target="tpu_custom_call" | custom-call | flops 2700000000 | bytes 1 | tf_op jit(solution)/shard_map/band_forward/pallas_call | solution.py:55
  27.6 2.3 %collective-permute-done.7.refs_1_ = bf16[1024,128]{1,0:T(8,128)(2,1)S(1)} collective-permute-done((bf16[1024,128]{1,0:T(8,128)(2,1)S(1)}, bf16[1024,128]{1,0:T(8,128)(2,1)S(1)}, u32[]{:S(2)}, u32[]{:S(2)}) %collective-permute-start.7) | collective-permute-done | bytes 262176 | tf_op jit(solution)/shard_map/ppermute | solution.py:521
  29.9 0.1 collective-permute-start.8
  30.0 2.2 %collective-permute-done.9.refs_0_ = bf16[512,256]{1,0:T(8,128)(2,1)S(1)} collective-permute-done((bf16[512,256]{1,0:T(8,128)(2,1)S(1)}, bf16[512,256]{1,0:T(8,128)(2,1)S(1)}, u32[]{:S(2)}, u32[]{:S(2)}) %collective-permute-start.9) | collective-permute-done | bytes 262176 | tf_op jit(solution)/shard_map/ppermute | solution.py:532
  32.2 2.1 %stride_forward.1 = (bf16[512,256]{1,0:T(8,128)(2,1)S(1)}, f32[2,512]{1,0:T(2,128)S(1)}, f32[8,128]{1,0:T(8,128)S(1)}) custom-call(s32[2,512]{1,0:T(2,128)S(1)} %get-tuple-element.100.refs_0_, bf16[512,256]{1,0:T(8,128)(2,1)S(1)} %copy-done.6, bf16[2048,128]{1,0:T(8,128)(2,1)S(1)} %get-tuple-element.103.refs_2_.refs_6_, ...), custom_call_target="tpu_custom_call" | custom-call | flops 35999997952 | bytes 1 | tf_op jit(solution)/shard_map/stride_forward/pallas_call | solution.py:55
  34.2 0.7 weight_grad_own.1
  35.0 0.1 collective-permute-start.11
  35.1 0.6 collective-permute-start.10
  35.7 1.3 %collective-permute-done.11.refs_1_ = bf16[4,256,256]{2,1,0:T(8,128)(2,1)S(1)} collective-permute-done((bf16[4,256,256]{2,1,0:T(8,128)(2,1)S(1)}, bf16[4,256,256]{2,1,0:T(8,128)(2,1)S(1)}, u32[]{:S(2)}, u32[]{:S(2)}) %collective-permute-start.11) | collective-permute-done | bytes 524320 | tf_op jit(solution)/shard_map/ppermute | solution.py:577
  37.0 0.1 weight_grad_own_core.1
  37.1 3.2 %collective-permute-start.14 = (bf16[2,256,256]{2,1,0:T(8,128)(2,1)S(1)}, bf16[2,256,256]{2,1,0:T(8,128)(2,1)S(1)}, u32[]{:S(2)}, u32[]{:S(2)}) collective-permute-start(bf16[2,256,256]{2,1,0:T(8,128)(2,1)S(1)} %get-tuple-element.129), channel_id=1, source_target_pairs={{0,8},{2,10},{4,12},{6,14},{8,0},{10,2},{12,4},{14,6},{16,24},{18,... | collective-permute-start | bytes 786440 | tf_op jit(solution)/shard_map/ppermute | solution.py:580
  40.3 2.7 %stride_backward.1 = (bf16[512,256]{1,0:T(8,128)(2,1)S(1)}, f32[2,512]{1,0:T(2,128)S(1)}, f32[2,128,512]{2,1,0:T(8,128)S(1)}, bf16[2048,128]{1,0:T(8,128)(2,1)S(...) custom-call(s32[2,512]{1,0:T(2,128)S(1)} %get-tuple-element.100.refs_0_, bf16[512,256]{1,0:T(8,128)(2,1)S(1)} %copy-done.6, ...), custom_call_target="tpu_custom_call" | custom-call | flops 46000001024 | bytes 1 | tf_op jit(solution)/shard_map/stride_backward/pallas_call | solution.py:55
  43.0 0.8 collective-permute-done.10.refs_0_.refs_1_
  43.8 0.7 weight_grad_other.1
  44.6 0.1 collective-permute-start.13
  44.6 0.5 collective-permute-start.12
  45.1 1.8 %collective-permute-done.14.refs_1_ = bf16[2,256,256]{2,1,0:T(8,128)(2,1)S(1)} collective-permute-done((bf16[2,256,256]{2,1,0:T(8,128)(2,1)S(1)}, bf16[2,256,256]{2,1,0:T(8,128)(2,1)S(1)}, u32[]{:S(2)}, u32[]{:S(2)}) %collective-permute-start.14) | collective-permute-done | bytes 262176 | tf_op jit(solution)/shard_map/ppermute | solution.py:580
  46.9 0.1 weight_grad_own_low.1
  47.0 0.1 weight_grad_other_core.1
  47.1 2.7 %collective-permute-start.16 = (bf16[2,256,256]{2,1,0:T(8,128)(2,1)S(1)}, bf16[2,256,256]{2,1,0:T(8,128)(2,1)S(1)}, u32[]{:S(2)}, u32[]{:S(2)}) collective-permute-start(bf16[2,256,256]{2,1,0:T(8,128)(2,1)S(1)} %get-tuple-element.137), channel_id=1, source_target_pairs={{0,8},{2,10},{4,12},{6,14},{8,0},{10,2},{12,4},{14,6},{16,24},{18,... | collective-permute-start | bytes 786440 | tf_op jit(solution)/shard_map/ppermute | solution.py:604
  49.8 0.1 stride_core.1
  50.0 1.8 %collective-permute-start.19 = (bf16[1024,128]{1,0:T(8,128)(2,1)S(1)}, bf16[1024,128]{1,0:T(8,128)(2,1)S(1)}, u32[]{:S(2)}, u32[]{:S(2)}) collective-permute-start(bf16[1024,128]{1,0:T(8,128)(2,1)S(1)} %get-tuple-element.144), channel_id=1, source_target_pairs={{0,4},{2,6},{4,0},{6,2},{8,12},{10,14},{12,8},{14,10},{16,20},{18,... | collective-permute-start | bytes 786440 | tf_op jit(solution)/shard_map/ppermute | solution.py:606
  51.8 4.1 %band_backward.1 = (bf16[512,256]{1,0:T(8,128)(2,1)}, bf16[1024,128]{1,0:T(8,128)(2,1)S(1)}, bf16[1024,128]{1,0:T(8,128)(2,1)S(1)}, bf16[1024,128]{1,0:T(8,128)(2,1)S(1)}, f32[8,128]{1,0:T(8,128)S(1)}) custom-call(bf16[512,256]{1,0:T(8,128)(2,1)S(1)} %copy-done.6, bf16[512,256]{1,0:T(8,128)(2,1)S(1)} %get-tuple-element.120.refs_1_, ...), custom_call_target="tpu_custom_call" | custom-call | flops 40000000000 | bytes 1 | tf_op jit(solution)/shard_map/band_backward/pallas_call | solution.py:55
  55.9 0.3 collective-permute-start.18
  56.2 0.3 collective-permute-done.16.refs_1_
  56.5 0.1 weight_grad_other_low.1
  56.5 1.8 %collective-permute-start.17 = (bf16[1,256,256]{2,1,0:T(8,128)(2,1)S(1)}, bf16[1,256,256]{2,1,0:T(8,128)(2,1)S(1)}, u32[]{:S(2)}, u32[]{:S(2)}) collective-permute-start(bf16[1,256,256]{2,1,0:T(8,128)(2,1)S(1)} %get-tuple-element.140), channel_id=1, source_target_pairs={{0,4},{2,6},{4,0},{6,2},{8,12},{10,14},{12,8},{14,10},{16,20},{18,... | collective-permute-start | bytes 393224 | tf_op jit(solution)/shard_map/ppermute | solution.py:622
  58.3 0.1 stride_y.1
  58.4 3.4 %collective-permute-start.21 = (bf16[512,128]{1,0:T(8,128)(2,1)S(1)}, bf16[512,128]{1,0:T(8,128)(2,1)S(1)}, u32[]{:S(2)}, u32[]{:S(2)}) collective-permute-start(bf16[512,128]{1,0:T(8,128)(2,1)S(1)} %get-tuple-element.155), channel_id=1, source_target_pairs={{0,16},{2,18},{4,20},{6,22},{8,24},{10,26},{12,28},{14,30},{16,0},... | collective-permute-start | bytes 393224 | tf_op jit(solution)/shard_map/ppermute | solution.py:624
  61.8 0.3 collective-permute-done.18.refs_1_
  62.2 2.4 %collective-permute-done.17.refs_1_ = bf16[1,256,256]{2,1,0:T(8,128)(2,1)S(1)} collective-permute-done((bf16[1,256,256]{2,1,0:T(8,128)(2,1)S(1)}, bf16[1,256,256]{2,1,0:T(8,128)(2,1)S(1)}, u32[]{:S(2)}, u32[]{:S(2)}) %collective-permute-start.17) | collective-permute-done | bytes 131104 | tf_op jit(solution)/shard_map/ppermute | solution.py:622
  64.6 0.6 collective-permute-start.22
  65.2 0.1 band_two.1
  65.3 1.3 %collective-permute-start.20 = (bf16[1024,128]{1,0:T(8,128)(2,1)S(1)}, bf16[1024,128]{1,0:T(8,128)(2,1)S(1)}, u32[]{:S(2)}, u32[]{:S(2)}) collective-permute-start(bf16[1024,128]{1,0:T(8,128)(2,1)S(1)} %get-tuple-element.153), channel_id=1, source_target_pairs={{4,0},{6,2},{8,4},{10,6},{12,8},{14,10},{16,12},{18,14},{20,16},{2... | collective-permute-start | bytes 786440 | tf_op jit(solution)/shard_map/ppermute | solution.py:632
  66.6 0.0 copy-start.3
  66.6 2.6 %layer_out.1 = (bf16[512,2048]{1,0:T(8,128)(2,1)}, f32[8,128]{1,0:T(8,128)S(1)}) custom-call(bf16[512,256]{1,0:T(8,128)(2,1)S(1)} %get-tuple-element.110.refs_0_.refs_4_, bf16[512,256]{1,0:T(8,128)(2,1)S(1)} %collective-permute-done.10.refs_0_.refs_1_, bf16[256,2048]{1,0:T(8,128)(2,1)S(1)} %get-tuple-element.111.refs_2_, ...), custom_call_target="tpu_custom_call" | custom-call | flops 25999998976 | bytes 1 | tf_op jit(solution)/shard_map/layer_out/pallas_call | solution.py:55
  69.2 0.6 collective-permute-done.22.refs_1_
  69.8 3.5 %collective-permute-start.24 = (bf16[256,256]{1,0:T(8,128)(2,1)S(1)}, bf16[256,256]{1,0:T(8,128)(2,1)S(1)}, u32[]{:S(2)}, u32[]{:S(2)}) collective-permute-start(bf16[256,256]{1,0:T(8,128)(2,1)S(1)} %get-tuple-element.166), channel_id=1, source_target_pairs={{0,16},{2,18},{4,20},{6,22},{8,24},{10,26},{12,28},{14,30},{16,0},... | collective-permute-start | bytes 393224 | tf_op jit(solution)/shard_map/ppermute | solution.py:640
  73.4 2.4 %collective-permute-start.23 = (bf16[256,128]{1,0:T(8,128)(2,1)S(1)}, bf16[256,128]{1,0:T(8,128)(2,1)S(1)}, u32[]{:S(2)}, u32[]{:S(2)}) collective-permute-start(bf16[256,128]{1,0:T(8,128)(2,1)S(1)} %get-tuple-element.161), channel_id=1, source_target_pairs={{0,8},{2,10},{4,12},{6,14},{8,0},{10,2},{12,4},{14,6},{16,24},{18,... | collective-permute-start | bytes 196616 | tf_op jit(solution)/shard_map/ppermute | solution.py:643
  75.8 2.5 %collective-permute-done.23.refs_5_ = bf16[256,128]{1,0:T(8,128)(2,1)S(1)} collective-permute-done((bf16[256,128]{1,0:T(8,128)(2,1)S(1)}, bf16[256,128]{1,0:T(8,128)(2,1)S(1)}, u32[]{:S(2)}, u32[]{:S(2)}) %collective-permute-start.23) | collective-permute-done | bytes 65568 | tf_op jit(solution)/shard_map/ppermute | solution.py:643
  78.3 1.4 %finish.1 = (bf16[512,128]{1,0:T(8,128)(2,1)}, bf16[512,128]{1,0:T(8,128)(2,1)}, f32[8,128]{1,0:T(8,128)S(1)}) custom-call(s32[2]{0:T(128)S(1)} %copy-done.3, bf16[1024,128]{1,0:T(8,128)(2,1)S(1)} %get-tuple-element.152.refs_1_, bf16[1024,128]{1,0:T(8,128)(2,1)S(1)} %collective-permute-done.15.refs_1_.refs_2_, ...), custom_call_target="tpu_custom_call" | custom-call | flops 100000000 | bytes 1 | tf_op jit(solution)/shard_map/finish/pallas_call | solution.py:55
  79.7 2.4 %collective-permute-done.24.refs_1_ = bf16[256,256]{1,0:T(8,128)(2,1)S(1)} collective-permute-done((bf16[256,256]{1,0:T(8,128)(2,1)S(1)}, bf16[256,256]{1,0:T(8,128)(2,1)S(1)}, u32[]{:S(2)}, u32[]{:S(2)}) %collective-permute-start.24) | collective-permute-done | bytes 131104 | tf_op jit(solution)/shard_map/ppermute | solution.py:640
  82.1 0.7 last_sum.1
  (33 shorter events, 0.2 us)
Async XLA Ops:
  0.6 13.8 %copy-start.4 = (bf16[256,4096]{1,0:T(8,128)(2,1)S(1)}, bf16[256,4096]{1,0:T(8,128)(2,1)}, u32[]{:S(2)}) copy-start(bf16[256,4096]{1,0:T(8,128)(2,1)} %refs_1_.6) | copy-start | bytes 6291460
  0.6 13.8 %copy-start.5 = (bf16[512,2048]{1,0:T(8,128)(2,1)S(1)}, bf16[512,2048]{1,0:T(8,128)(2,1)}, u32[]{:S(2)}) copy-start(bf16[512,2048]{1,0:T(8,128)(2,1)} %refs_0_.6) | copy-start | bytes 6291460
  2.9 18.1 %collective-permute-start.5 = (bf16[256,1024]{1,0:T(8,128)(2,1)}, bf16[256,1024]{1,0:T(8,128)(2,1)S(1)}, u32[]{:S(2)}, u32[]{:S(2)}) collective-permute-start(bf16[256,1024]{1,0:T(8,128)(2,1)} %get-tuple-element.95), channel_id=1, source_target_pairs={{0,1},{1,0},{2,3},{3,2},{4,5},{5,4},{6,7},{7,6},{8,9},{9,8},{10,11... | collective-permute-start | bytes 1572872 | tf_op jit(solution)/shard_map/ppermute | solution.py:499
  5.9 8.5 %collective-permute-start = (bf16[1024,128]{1,0:T(8,128)(2,1)}, bf16[1024,128]{1,0:T(8,128)(2,1)S(1)}, u32[]{:S(2)}, u32[]{:S(2)}) collective-permute-start(bf16[1024,128]{1,0:T(8,128)(2,1)} %get-tuple-element.87.refs_2_), channel_id=1, source_target_pairs={{0,2},{2,0},{4,6},{6,4},{8,10},{10,8},{12,14},{14,12},{16,18},{18,... | collective-permute-start | bytes 786440 | tf_op jit(solution)/shard_map/ppermute | solution.py:510
  5.9 5.0 %collective-permute-start.2 = (bf16[256,128]{1,0:T(8,128)(2,1)}, bf16[256,128]{1,0:T(8,128)(2,1)S(1)}, u32[]{:S(2)}, u32[]{:S(2)}) collective-permute-start(bf16[256,128]{1,0:T(8,128)(2,1)} %get-tuple-element.88.refs_0_), channel_id=1, source_target_pairs={{0,8},{2,10},{4,12},{6,14},{8,0},{10,2},{12,4},{14,6},{16,24},{18,... | collective-permute-start | bytes 196616 | tf_op jit(solution)/shard_map/ppermute | solution.py:508
  7.5 13.5 %collective-permute-start.1 = (bf16[1024,128]{1,0:T(8,128)(2,1)}, bf16[1024,128]{1,0:T(8,128)(2,1)S(1)}, u32[]{:S(2)}, u32[]{:S(2)}) collective-permute-start(bf16[1024,128]{1,0:T(8,128)(2,1)} %get-tuple-element.87.refs_2_), channel_id=1, source_target_pairs={{0,4},{2,6},{4,8},{6,10},{8,12},{10,14},{12,16},{14,18},{16,20},{1... | collective-permute-start | bytes 786440 | tf_op jit(solution)/shard_map/ppermute | solution.py:509
  10.9 0.8 %copy-start.8 = (bf16[256,128]{1,0:T(8,128)(2,1)S(1)}, bf16[256,128]{1,0:T(8,128)(2,1)}, u32[]{:S(2)}) copy-start(bf16[256,128]{1,0:T(8,128)(2,1)} %get-tuple-element.88.refs_0_) | copy-start | bytes 196612
  11.8 9.1 %collective-permute-start.3 = (bf16[512,128]{1,0:T(8,128)(2,1)S(1)}, bf16[512,128]{1,0:T(8,128)(2,1)S(1)}, u32[]{:S(2)}, u32[]{:S(2)}) collective-permute-start(bf16[512,128]{1,0:T(8,128)(2,1)S(1)} %get-tuple-element.89.refs_0_), channel_id=1, source_target_pairs={{0,16},{2,18},{4,20},{6,22},{8,24},{10,26},{12,28},{14,30},{16,0},... | collective-permute-start | bytes 393224 | tf_op jit(solution)/shard_map/ppermute | solution.py:512
  20.9 3.4 %copy-start.2 = (s32[2]{0:T(128)S(1)}, s32[2]{0:T(128)}, u32[]{:S(2)}) copy-start(s32[2]{0:T(128)} %refs_0_.9) | copy-start | bytes 28
  21.0 3.4 %copy-start.6 = (bf16[512,256]{1,0:T(8,128)(2,1)S(1)}, bf16[512,256]{1,0:T(8,128)(2,1)}, u32[]{:S(2)}) copy-start(bf16[512,256]{1,0:T(8,128)(2,1)} %refs_0_.8) | copy-start | bytes 786436
  21.0 3.4 %copy-start.7 = (bf16[1024,128]{1,0:T(8,128)(2,1)S(1)}, bf16[1024,128]{1,0:T(8,128)(2,1)}, u32[]{:S(2)}) copy-start(bf16[1024,128]{1,0:T(8,128)(2,1)} %get-tuple-element.87.refs_2_) | copy-start | bytes 786436
  21.0 2.0 %collective-permute-start.6 = (bf16[256,1024]{1,0:T(8,128)(2,1)S(1)}, bf16[256,1024]{1,0:T(8,128)(2,1)S(1)}, u32[]{:S(2)}, u32[]{:S(2)}) collective-permute-start(bf16[256,1024]{1,0:T(8,128)(2,1)S(1)} %get-tuple-element.97.refs_1_.refs_3_), channel_id=1, source_target_pairs={{0,2},{2,0},{4,6},{6,4},{8,10},{10,8},{12,14},{14,12},{16,18},{18,... | collective-permute-start | bytes 1572872 | tf_op jit(solution)/shard_map/ppermute | solution.py:527
  21.1 3.2 %collective-permute-start.4 = (bf16[1024,128]{1,0:T(8,128)(2,1)S(1)}, bf16[1024,128]{1,0:T(8,128)(2,1)S(1)}, u32[]{:S(2)}, u32[]{:S(2)}) collective-permute-start(bf16[1024,128]{1,0:T(8,128)(2,1)S(1)} %get-tuple-element.93.refs_4_), channel_id=1, source_target_pairs={{0,2},{2,0},{4,6},{6,4},{8,10},{10,8},{12,14},{14,12},{16,18},{18,... | collective-permute-start | bytes 786440 | tf_op jit(solution)/shard_map/ppermute | solution.py:523
  21.6 8.3 %collective-permute-start.7 = (bf16[1024,128]{1,0:T(8,128)(2,1)S(1)}, bf16[1024,128]{1,0:T(8,128)(2,1)S(1)}, u32[]{:S(2)}, u32[]{:S(2)}) collective-permute-start(bf16[1024,128]{1,0:T(8,128)(2,1)S(1)} %get-tuple-element.101.refs_0_), channel_id=1, source_target_pairs={{0,4},{2,6},{4,0},{6,2},{8,12},{10,14},{12,8},{14,10},{16,20},{18,... | collective-permute-start | bytes 786440 | tf_op jit(solution)/shard_map/ppermute | solution.py:521
  23.0 4.6 %copy-start = (bf16[256,1024]{1,0:T(8,128)(2,1)}, bf16[256,1024]{1,0:T(8,128)(2,1)S(1)}, u32[]{:S(2)}) copy-start(bf16[256,1024]{1,0:T(8,128)(2,1)S(1)} %collective-permute-done.6.refs_2_.refs_4_) | copy-start | bytes 1572868
  23.8 8.4 %collective-permute-start.9 = (bf16[512,256]{1,0:T(8,128)(2,1)S(1)}, bf16[512,256]{1,0:T(8,128)(2,1)S(1)}, u32[]{:S(2)}, u32[]{:S(2)}) collective-permute-start(bf16[512,256]{1,0:T(8,128)(2,1)S(1)} %get-tuple-element.107), channel_id=1, source_target_pairs={{0,1},{1,0},{2,3},{3,2},{4,5},{5,4},{6,7},{7,6},{8,9},{9,8},{10,11... | collective-permute-start | bytes 786440 | tf_op jit(solution)/shard_map/ppermute | solution.py:532
  29.9 2.2 %collective-permute-start.8 = (bf16[2048,128]{1,0:T(8,128)(2,1)S(1)}, bf16[2048,128]{1,0:T(8,128)(2,1)S(1)}, u32[]{:S(2)}, u32[]{:S(2)}) collective-permute-start(bf16[2048,128]{1,0:T(8,128)(2,1)S(1)} %get-tuple-element.103.refs_2_.refs_6_), channel_id=1, source_target_pairs={{0,2},{2,0},{4,6},{6,4},{8,10},{10,8},{12,14},{14,12},{16,18},{18,... | collective-permute-start | bytes 1572872 | tf_op jit(solution)/shard_map/ppermute | solution.py:545
  35.0 2.0 %collective-permute-start.11 = (bf16[4,256,256]{2,1,0:T(8,128)(2,1)S(1)}, bf16[4,256,256]{2,1,0:T(8,128)(2,1)S(1)}, u32[]{:S(2)}, u32[]{:S(2)}) collective-permute-start(bf16[4,256,256]{2,1,0:T(8,128)(2,1)S(1)} %get-tuple-element.117), channel_id=1, source_target_pairs={{0,2},{2,0},{4,6},{6,4},{8,10},{10,8},{12,14},{14,12},{16,18},{18,... | collective-permute-start | bytes 1572872 | tf_op jit(solution)/shard_map/ppermute | solution.py:577
  35.1 8.7 %collective-permute-start.10 = (bf16[512,256]{1,0:T(8,128)(2,1)S(1)}, bf16[512,256]{1,0:T(8,128)(2,1)S(1)}, u32[]{:S(2)}, u32[]{:S(2)}) collective-permute-start(bf16[512,256]{1,0:T(8,128)(2,1)S(1)} %get-tuple-element.110.refs_0_.refs_4_), channel_id=1, source_target_pairs={{0,1},{1,0},{2,3},{3,2},{4,5},{5,4},{6,7},{7,6},{8,9},{9,8},{10,11... | collective-permute-start | bytes 786440 | tf_op jit(solution)/shard_map/ppermute | solution.py:563
  37.1 9.8 %collective-permute-start.14 = (bf16[2,256,256]{2,1,0:T(8,128)(2,1)S(1)}, bf16[2,256,256]{2,1,0:T(8,128)(2,1)S(1)}, u32[]{:S(2)}, u32[]{:S(2)}) collective-permute-start(bf16[2,256,256]{2,1,0:T(8,128)(2,1)S(1)} %get-tuple-element.129), channel_id=1, source_target_pairs={{0,8},{2,10},{4,12},{6,14},{8,0},{10,2},{12,4},{14,6},{16,24},{18,... | collective-permute-start | bytes 786440 | tf_op jit(solution)/shard_map/ppermute | solution.py:580
  44.6 2.4 %collective-permute-start.13 = (bf16[4,256,256]{2,1,0:T(8,128)(2,1)S(1)}, bf16[4,256,256]{2,1,0:T(8,128)(2,1)S(1)}, u32[]{:S(2)}, u32[]{:S(2)}) collective-permute-start(bf16[4,256,256]{2,1,0:T(8,128)(2,1)S(1)} %get-tuple-element.127), channel_id=1, source_target_pairs={{0,2},{2,0},{4,6},{6,4},{8,10},{10,8},{12,14},{14,12},{16,18},{18,... | collective-permute-start | bytes 1572872 | tf_op jit(solution)/shard_map/ppermute | solution.py:597
  44.6 5.2 %collective-permute-start.12 = (bf16[2048,128]{1,0:T(8,128)(2,1)S(1)}, bf16[2048,128]{1,0:T(8,128)(2,1)S(1)}, u32[]{:S(2)}, u32[]{:S(2)}) collective-permute-start(bf16[2048,128]{1,0:T(8,128)(2,1)S(1)} %get-tuple-element.124), channel_id=1, source_target_pairs={{0,2},{2,0},{4,6},{6,4},{8,10},{10,8},{12,14},{14,12},{16,18},{18,... | collective-permute-start | bytes 1572872 | tf_op jit(solution)/shard_map/ppermute | solution.py:594
  47.1 9.3 %collective-permute-start.16 = (bf16[2,256,256]{2,1,0:T(8,128)(2,1)S(1)}, bf16[2,256,256]{2,1,0:T(8,128)(2,1)S(1)}, u32[]{:S(2)}, u32[]{:S(2)}) collective-permute-start(bf16[2,256,256]{2,1,0:T(8,128)(2,1)S(1)} %get-tuple-element.137), channel_id=1, source_target_pairs={{0,8},{2,10},{4,12},{6,14},{8,0},{10,2},{12,4},{14,6},{16,24},{18,... | collective-permute-start | bytes 786440 | tf_op jit(solution)/shard_map/ppermute | solution.py:604
  50.0 8.3 %collective-permute-start.19 = (bf16[1024,128]{1,0:T(8,128)(2,1)S(1)}, bf16[1024,128]{1,0:T(8,128)(2,1)S(1)}, u32[]{:S(2)}, u32[]{:S(2)}) collective-permute-start(bf16[1024,128]{1,0:T(8,128)(2,1)S(1)} %get-tuple-element.144), channel_id=1, source_target_pairs={{0,4},{2,6},{4,0},{6,2},{8,12},{10,14},{12,8},{14,10},{16,20},{18,... | collective-permute-start | bytes 786440 | tf_op jit(solution)/shard_map/ppermute | solution.py:606
  55.9 10.8 %copy-start.1 = (bf16[256,1024]{1,0:T(8,128)(2,1)S(1)}, bf16[256,1024]{1,0:T(8,128)(2,1)}, u32[]{:S(2)}) copy-start(bf16[256,1024]{1,0:T(8,128)(2,1)} %copy-done) | copy-start | bytes 1572868
  55.9 9.4 %collective-permute-start.15 = (bf16[1024,128]{1,0:T(8,128)(2,1)S(1)}, bf16[1024,128]{1,0:T(8,128)(2,1)S(1)}, u32[]{:S(2)}, u32[]{:S(2)}) collective-permute-start(bf16[1024,128]{1,0:T(8,128)(2,1)S(1)} %get-tuple-element.135), channel_id=1, source_target_pairs={{0,2},{2,0},{4,6},{6,4},{8,10},{10,8},{12,14},{14,12},{16,18},{18,... | collective-permute-start | bytes 786440 | tf_op jit(solution)/shard_map/ppermute | solution.py:617
  55.9 6.3 %collective-permute-start.18 = (bf16[1,256,256]{2,1,0:T(8,128)(2,1)S(1)}, bf16[1,256,256]{2,1,0:T(8,128)(2,1)S(1)}, u32[]{:S(2)}, u32[]{:S(2)}) collective-permute-start(bf16[1,256,256]{2,1,0:T(8,128)(2,1)S(1)} %get-tuple-element.142), channel_id=1, source_target_pairs={{0,4},{2,6},{4,0},{6,2},{8,12},{10,14},{12,8},{14,10},{16,20},{18,... | collective-permute-start | bytes 393224 | tf_op jit(solution)/shard_map/ppermute | solution.py:601
  56.5 8.1 %collective-permute-start.17 = (bf16[1,256,256]{2,1,0:T(8,128)(2,1)S(1)}, bf16[1,256,256]{2,1,0:T(8,128)(2,1)S(1)}, u32[]{:S(2)}, u32[]{:S(2)}) collective-permute-start(bf16[1,256,256]{2,1,0:T(8,128)(2,1)S(1)} %get-tuple-element.140), channel_id=1, source_target_pairs={{0,4},{2,6},{4,0},{6,2},{8,12},{10,14},{12,8},{14,10},{16,20},{18,... | collective-permute-start | bytes 393224 | tf_op jit(solution)/shard_map/ppermute | solution.py:622
  58.4 15.0 %collective-permute-start.21 = (bf16[512,128]{1,0:T(8,128)(2,1)S(1)}, bf16[512,128]{1,0:T(8,128)(2,1)S(1)}, u32[]{:S(2)}, u32[]{:S(2)}) collective-permute-start(bf16[512,128]{1,0:T(8,128)(2,1)S(1)} %get-tuple-element.155), channel_id=1, source_target_pairs={{0,16},{2,18},{4,20},{6,22},{8,24},{10,26},{12,28},{14,30},{16,0},... | collective-permute-start | bytes 393224 | tf_op jit(solution)/shard_map/ppermute | solution.py:624
  64.6 5.2 %collective-permute-start.22 = (bf16[256,256]{1,0:T(8,128)(2,1)S(1)}, bf16[256,256]{1,0:T(8,128)(2,1)S(1)}, u32[]{:S(2)}, u32[]{:S(2)}) collective-permute-start(bf16[256,256]{1,0:T(8,128)(2,1)S(1)} %get-tuple-element.157), channel_id=1, source_target_pairs={{0,1},{1,0},{2,3},{3,2},{4,5},{5,4},{6,7},{7,6},{8,9},{9,8},{10,11... | collective-permute-start | bytes 393224 | tf_op jit(solution)/shard_map/ppermute | solution.py:630
  65.3 12.9 %collective-permute-start.20 = (bf16[1024,128]{1,0:T(8,128)(2,1)S(1)}, bf16[1024,128]{1,0:T(8,128)(2,1)S(1)}, u32[]{:S(2)}, u32[]{:S(2)}) collective-permute-start(bf16[1024,128]{1,0:T(8,128)(2,1)S(1)} %get-tuple-element.153), channel_id=1, source_target_pairs={{4,0},{6,2},{8,4},{10,6},{12,8},{14,10},{16,12},{18,14},{20,16},{2... | collective-permute-start | bytes 786440 | tf_op jit(solution)/shard_map/ppermute | solution.py:632
  66.6 11.6 %copy-start.3 = (s32[2]{0:T(128)S(1)}, s32[2]{0:T(128)}, u32[]{:S(2)}) copy-start(s32[2]{0:T(128)} %refs_0_.9) | copy-start | bytes 28
  69.8 12.3 %collective-permute-start.24 = (bf16[256,256]{1,0:T(8,128)(2,1)S(1)}, bf16[256,256]{1,0:T(8,128)(2,1)S(1)}, u32[]{:S(2)}, u32[]{:S(2)}) collective-permute-start(bf16[256,256]{1,0:T(8,128)(2,1)S(1)} %get-tuple-element.166), channel_id=1, source_target_pairs={{0,16},{2,18},{4,20},{6,22},{8,24},{10,26},{12,28},{14,30},{16,0},... | collective-permute-start | bytes 393224 | tf_op jit(solution)/shard_map/ppermute | solution.py:640
  73.4 4.9 %collective-permute-start.23 = (bf16[256,128]{1,0:T(8,128)(2,1)S(1)}, bf16[256,128]{1,0:T(8,128)(2,1)S(1)}, u32[]{:S(2)}, u32[]{:S(2)}) collective-permute-start(bf16[256,128]{1,0:T(8,128)(2,1)S(1)} %get-tuple-element.161), channel_id=1, source_target_pairs={{0,8},{2,10},{4,12},{6,14},{8,0},{10,2},{12,4},{14,6},{16,24},{18,... | collective-permute-start | bytes 196616 | tf_op jit(solution)/shard_map/ppermute | solution.py:643
